TPU v7x, 128 devices: a whole 4x4x4 slice. The times are simulated.
128 devices in a mesh: row: 8 (over y_hi, z), col: 16 (over x, y_lo, core).
Axes of the slice: x: 4, y: 4 (y_hi: 2, y_lo: 2; y = y_hi * 2 + y_lo), z: 4, core: 2. Of those that a mesh axis runs over, the one named last changes fastest.
Arguments:
- object_slab: float32 [2, 4096, 8192], P(None, 'row', 'col'), may hold values from -5 to 5
- probe: float32 [2, 256, 256], replicated, may hold values from -6 to 6
- offsets: int32 [8, 16, 2, 8], P('row', 'col'), may hold values from 0 to 511
- counts: int32 [8, 16], P('row', 'col'), may hold values from 1 to 8, as said below
- patterns: float32 [8, 16, 8, 256, 256], P('row', 'col'), may hold values from 0 to 2
Outputs:
- object_out: float32 [2, 4096, 8192], P(None, 'row', 'col')
- probe_out: float32 [2, 256, 256], replicated
Inputs may be any that keep to these rules, and one draw needn't show every extreme that they name: `counts`: some tile has all 8 slots live in every draw.
All inputs are finite; a program needn't handle non-finite values.
Results may differ from a plain program's by a relative error of at most 0.0003.
Values sent between devices are 32-bit elements; how exact they have to be, the bound alone decides.
No kernel may reach another device: no remote copies, remote signals or barrier semaphores. Data moves between devices by JAX's collectives and lax.ppermute only.
A program may use at most 128 MiB of HBM per device.

v0:
```python
import functools
import itertools
import math

import jax
import jax.numpy as jnp
import numpy as np
from jax import lax
from jax.experimental import pallas as pl
from jax.experimental.pallas import tpu as pltpu
from jax.sharding import Mesh, PartitionSpec as P

OBJECT_RATE = 0.1
PROBE_RATE = 0.5
M = 256
HALF = M // 2
LANES = 128
COL = ("x", "y_lo", "core")
STRIP = 32
F32 = jnp.float32
BF16 = jnp.bfloat16


def packed_tables():
    j = np.arange(HALF)[:, None]
    k = np.arange(M)[None, :]
    angle = 2.0 * np.pi * ((j * k) % M) / M
    cosine = np.cos(angle)
    sine = np.sin(angle)
    sine[0] = np.where(np.arange(M) % 2 == 0, 1.0, -1.0)
    table = np.concatenate([cosine, sine]) / math.sqrt(M)

    def split(t):
        high = t.astype(jnp.bfloat16)
        low = (t - high.astype(np.float64)).astype(jnp.bfloat16)
        return high, low

    return split(table) + split(table.T)


def split_parts(x):
    high = x.astype(BF16)
    low = (x - high.astype(F32)).astype(BF16)
    return high, low

def butterfly(uc, us, vc, vs, first):
    if first is None:
        return uc + vs, uc - vs, vc - us, vc + us
    rp = uc + jnp.where(first, 0.0, vs)
    rm = jnp.where(first, us, uc - vs)
    ip = vc - jnp.where(first, 0.0, us)
    im = jnp.where(first, vs, vc + us)
    return rp, rm, ip, im

def butterfly_adjoint(rp, rm, ip, im, first):
    if first is None:
        return rp + rm, im - ip, ip + im, rp - rm
    uc = rp + jnp.where(first, 0.0, rm)
    vs = jnp.where(first, im, rp - rm)
    vc = ip + jnp.where(first, 0.0, im)
    us = jnp.where(first, rm, im - ip)
    return uc, us, vc, vs

def halves(x):
    return x[:, :LANES], x[:, LANES:]

def window(s, live, offs, probe, pats, tables, ext, gacc, pacc, scratch):
    rh, rl, th, tl = tables
    ah, al, bh, bl, f, pr = scratch
    r = offs[0, s]
    c = offs[1, s]
    a = c // LANES
    b = c - a * LANES
    lane = lax.broadcasted_iota(jnp.int32, (STRIP, LANES), 1)
    keep = lane >= b
    lane_first = lane == 0
    row_first = lax.broadcasted_iota(jnp.int32, (STRIP, M), 0) == 0

    def cut(part, i):
        rows = pl.ds(r + i * STRIP, STRIP)
        t0 = ext[a, part, rows, :]
        t1 = ext[a + 1, part, rows, :]
        t2 = ext[a + 2, part, rows, :]
        return jnp.concatenate([jnp.where(keep, t0, t2), t1], axis=1)

    def turn(part, i):
        rows = pl.ds(i * STRIP, STRIP)
        p0 = pltpu.roll(probe[0, part, rows, :], b, 1)
        p1 = pltpu.roll(probe[1, part, rows, :], b, 1)
        return jnp.concatenate([jnp.where(keep, p0, p1), jnp.where(keep, p1, p0)], axis=1)

    def put(high, low, part, rows, value):
        h, l = split_parts(value)
        high[part, rows, :] = h
        low[part, rows, :] = l

    def right(high, low, wh, wl, emit):
        w = jnp.concatenate([wh[...], wh[...], wl[...]], axis=0)
        for part in range(2):
            h, l = high[part], low[part]
            emit(part, slice(0, M), jnp.dot(jnp.concatenate([h, l, h], axis=1), w, preferred_element_type=F32))

    def left(wh, wl, high, low, emit):
        w = jnp.concatenate([wh[...], wl[...], wh[...]], axis=1)
        for part in range(2):
            h, l = high[part], low[part]
            x = jnp.concatenate([h, h, l], axis=0)
            emit(part, slice(0, M), jnp.dot(w, x, preferred_element_type=F32))

    def keep_f32(part, rows, value):
        f[part, rows, :] = value

    for i in range(M // STRIP):
        rows = slice(i * STRIP, (i + 1) * STRIP)
        o_re, o_im = cut(0, i), cut(1, i)
        p_re, p_im = turn(0, i), turn(1, i)
        pr[0, rows, :] = p_re
        pr[1, rows, :] = p_im
        put(ah, al, 0, rows, p_re * o_re - p_im * o_im)
        put(ah, al, 1, rows, p_re * o_im + p_im * o_re)
    yield
    right(ah, al, th, tl, functools.partial(put, bh, bl))
    yield
    left(rh, rl, bh, bl, keep_f32)
    yield
    for i in range(HALF // STRIP):
        top = slice(i * STRIP, (i + 1) * STRIP)
        bot = slice(HALF + i * STRIP, HALF + (i + 1) * STRIP)
        first = row_first if i == 0 else None
        u_c, u_s, v_c, v_s = f[0, top, :], f[0, bot, :], f[1, top, :], f[1, bot, :]
        wide = []
        for u, v in ((u_c, v_c), (u_s, v_s)):
            rp, rm, ip, im = butterfly(*halves(u), *halves(v), lane_first)
            wide += [jnp.concatenate([rp, rm], axis=1), jnp.concatenate([ip, im], axis=1)]
        rp, rm, ip, im = butterfly(wide[0], wide[2], wide[1], wide[3], first)
        res_p = rp * rp + ip * ip - pats[s, top, :]
        res_m = rm * rm + im * im - pats[s, bot, :]
        if live is not None:
            res_p, res_m = res_p * live, res_m * live
        uc, us, vc, vs = butterfly_adjoint(res_p * rp, res_m * rm, res_p * ip, res_m * im, first)
        for u, v, rows in ((uc, vc, top), (us, vs, bot)):
            x_c, x_s, y_c, y_s = butterfly_adjoint(*halves(u), *halves(v), lane_first)
            put(ah, al, 0, rows, jnp.concatenate([x_c, x_s], axis=1))
            put(ah, al, 1, rows, jnp.concatenate([y_c, y_s], axis=1))
    yield
    left(th, tl, ah, al, functools.partial(put, bh, bl))
    yield
    right(bh, bl, rh, rl, keep_f32)
    yield
    back = lane < LANES - b
    for i in range(M // STRIP):
        rows = slice(i * STRIP, (i + 1) * STRIP)
        spot = pl.ds(r + i * STRIP, STRIP)
        b_re, b_im = f[0, rows, :], f[1, rows, :]
        o_re, o_im = cut(0, i), cut(1, i)
        p_re, p_im = pr[0, rows, :], pr[1, rows, :]
        go = (p_re * b_re + p_im * b_im, p_re * b_im - p_im * b_re)
        gp = (o_re * b_re + o_im * b_im, o_re * b_im - o_im * b_re)
        for part in range(2):
            g0, g1 = halves(go[part])
            gacc[a, part, spot, :] += jnp.where(keep, g0, 0.0)
            gacc[a + 1, part, spot, :] += g1
            gacc[a + 2, part, spot, :] += jnp.where(keep, 0.0, g0)
            q0, q1 = halves(gp[part])
            q0 = pltpu.roll(q0, LANES - b, 1)
            q1 = pltpu.roll(q1, LANES - b, 1)
            pacc[0, part, rows, :] += jnp.where(back, q0, q1)
            pacc[1, part, rows, :] += jnp.where(back, q1, q0)


def windows_kernel(*refs):
    offs, count = refs[:2]
    blocks, (probe, pats) = refs[2:11], refs[11:13]
    tables, grads, gprobe = refs[13:17], refs[17:26], refs[26]
    ext, gacc, pats_here, *scratch, sem_in, sem_out, sem_pats = refs[27:]

    def place(buffer, k):
        i, j = divmod(k, 3)
        return buffer.at[2 * j:2 * j + 2, :, i * M:(i + 1) * M, :]

    arrivals = [pltpu.make_async_copy(blocks[k], place(ext, k), sem_in.at[k]) for k in range(9)]
    arrivals.append(pltpu.make_async_copy(pats, pats_here, sem_pats))
    for copy in arrivals:
        copy.start()

    def clear(i, carry):
        gacc[:, :, pl.ds(i * STRIP, STRIP), :] = jnp.zeros((6, 2, STRIP, LANES), F32)
        return carry

    lax.fori_loop(0, 3 * M // STRIP, clear, 0)
    gprobe[...] = jnp.zeros(gprobe.shape, F32)
    for copy in arrivals:
        copy.wait()

    def pair(k, carry):
        turns = []
        for n in range(2):
            live = None if n == 0 else jnp.where(2 * k + 1 < count[0], 1.0, 0.0)
            own = [buffer.at[n] for buffer in scratch]
            turns.append(window(2 * k + n, live, offs, probe, pats_here, tables, ext, gacc, gprobe, own))
        for _ in itertools.zip_longest(*turns):
            pass
        return carry

    lax.fori_loop(0, (count[0] + 1) // 2, pair, 0)
    departures = [pltpu.make_async_copy(place(gacc, k), grads[k], sem_out.at[k]) for k in range(9)]
    for copy in departures:
        copy.start()
    for copy in departures:
        copy.wait()


def in_hbm(arrays):
    return [pltpu.with_memory_space_constraint(x, pltpu.HBM) for x in arrays]


def windows(offs, count, blocks, probe, pats, tables):
    smem = pl.BlockSpec(memory_space=pltpu.SMEM)
    vmem = pl.BlockSpec(memory_space=pltpu.VMEM)
    where = pl.BlockSpec(memory_space=pl.ANY)
    block = jax.ShapeDtypeStruct((2, 2, M, LANES), F32)
    halves16 = pltpu.VMEM((2, 2, M, M), BF16)
    whole32 = pltpu.VMEM((2, 2, M, M), F32)
    extended = pltpu.VMEM((6, 2, 3 * M, LANES), F32)
    return pl.pallas_call(
        windows_kernel,
        out_shape=[pltpu.HBM(block.shape, F32)] * 9 + [block],
        in_specs=[smem, smem] + [where] * 9 + [vmem, where] + [vmem] * 4,
        out_specs=[where] * 9 + [vmem],
        scratch_shapes=[extended, extended, pltpu.VMEM(pats.shape, F32)] + [halves16] * 4 + [whole32] * 2
        + [pltpu.SemaphoreType.DMA((9,)), pltpu.SemaphoreType.DMA((9,)), pltpu.SemaphoreType.DMA],
        compiler_params=pltpu.CompilerParams(vmem_limit_bytes=24 * 1024 * 1024),
        name="windows",
    )(offs, count, *in_hbm(blocks), probe, *in_hbm([pats]), *tables)


def shift(block, axis, distance):
    n = lax.axis_size(axis)
    return lax.ppermute(block, axis, [(i, (i + distance) % n) for i in range(n)])


RING = 4


def shift_z(block, distance):
    pairs = [(i, i // RING * RING + (i + distance) % RING) for i in range(lax.axis_size("row"))]
    return lax.ppermute(block, "row", pairs)


def cross_y(block, distance):
    n, edge = lax.axis_size("row"), 0 if distance > 0 else RING - 1
    far = lax.ppermute(block, "row", [(i, (i + RING) % n) for i in range(edge, n, RING)])
    return jnp.where(lax.axis_index("row") % RING == edge, far, block)


def most_kernel(*refs):
    whole, here, sem = refs[11:]
    arrivals = [pltpu.make_async_copy(refs[k], here.at[k], sem.at[k]) for k in range(11)]
    for copy in arrivals:
        copy.start()
    for copy in arrivals:
        copy.wait()
    for k, grads in enumerate(((4, 8), (5, 9), (6, 10), (7,))):
        i, j = divmod(k, 2)
        for tile in range(2):
            lanes = pl.ds((2 * j + tile) * LANES, LANES)
            for part in range(2):
                total = sum((here[g, tile, part] for g in grads[1:]), here[grads[0], tile, part])
                whole[part, pl.ds(i * M, M), lanes] = here[k, tile, part] - OBJECT_RATE * total


def rest_kernel(pstep, grad, probe, summed, whole_in, whole, probe_out, corner, sem):
    del whole_in
    view = whole.at[:, pl.ds(0, M), pl.ds(0, M)]
    arrive = pltpu.make_async_copy(view, corner, sem.at[0])
    arrive.start()
    for tile in range(2):
        for part in range(2):
            lanes = pl.ds(tile * LANES, LANES)
            probe_out[part, :, lanes] = probe[tile, part] - pstep * summed[tile, part]
    arrive.wait()
    for tile in range(2):
        for part in range(2):
            lanes = pl.ds(tile * LANES, LANES)
            corner[part, :, lanes] = corner[part, :, lanes] - OBJECT_RATE * grad[tile, part]
    leave = pltpu.make_async_copy(corner, view, sem.at[1])
    leave.start()
    leave.wait()


def most(own, grads):
    vmem, where = pl.BlockSpec(memory_space=pltpu.VMEM), pl.BlockSpec(memory_space=pl.ANY)
    return pl.pallas_call(
        most_kernel,
        out_shape=jax.ShapeDtypeStruct((2, 2 * M, 2 * M), F32),
        in_specs=[where] * 11,
        out_specs=vmem,
        scratch_shapes=[pltpu.VMEM((11, *own[0].shape), F32), pltpu.SemaphoreType.DMA((11,))],
        compiler_params=pltpu.CompilerParams(vmem_limit_bytes=24 * 1024 * 1024),
        name="most",
    )(*in_hbm([*own, *grads]))


def rest(pstep, grad, probe, summed, whole):
    vmem, where = pl.BlockSpec(memory_space=pltpu.VMEM), pl.BlockSpec(memory_space=pl.ANY)
    return pl.pallas_call(
        functools.partial(rest_kernel, pstep),
        out_shape=(pltpu.HBM(whole.shape, F32), jax.ShapeDtypeStruct((2, M, M), F32)),
        in_specs=[vmem] * 3 + [where],
        out_specs=(where, vmem),
        scratch_shapes=[pltpu.VMEM((2, M, M), F32), pltpu.SemaphoreType.DMA((2,))],
        input_output_aliases={3: 0},
        compiler_params=pltpu.CompilerParams(vmem_limit_bytes=24 * 1024 * 1024),
        name="rest",
    )(grad, probe, summed, *in_hbm([whole]))


def deal(x):
    return jnp.sum(lax.all_to_all(x.reshape(-1, 8, LANES), ("row", *COL), 0, 0, tiled=True), axis=0)


def collect(share, shape):
    n = lax.axis_size(("row", *COL))
    spread = jnp.broadcast_to(share[None], (n, *share.shape))
    return lax.all_to_all(spread, ("row", *COL), 0, 0, tiled=True).reshape(shape)


def together(*values):
    return lax.optimization_barrier(values)


def tile_block(x, i, j):
    part = x[:, i * M:(i + 1) * M, j * M:(j + 1) * M]
    return jnp.stack([part[:, :, :LANES], part[:, :, LANES:]])


def body(object_slab, probe, offsets, counts, patterns):
    tile_h, tile_w = object_slab.shape[1:]
    slots = patterns.shape[2]
    offs = offsets[0, 0]
    count = counts[0]
    tables = tuple(jnp.asarray(t) for t in packed_tables())
    axes = ("row", *COL)
    pstep = PROBE_RATE / math.sqrt(lax.axis_size(axes) * slots)

    pats = patterns[0, 0]
    order = np.concatenate([np.arange(HALF + 1), np.arange(M - 1, HALF, -1)])
    turned = np.zeros((M, M), np.float32)
    turned[np.arange(M), order] = 1.0
    high = lax.Precision.HIGHEST
    pats = jnp.einsum("jk,skl->sjl", turned, pats, precision=high)
    pats = jnp.einsum("sjk,lk->sjl", pats, turned, precision=high)

    def step(x, *grads):
        return x - OBJECT_RATE * sum(grads[1:], grads[0])

    probe = tile_block(probe, 0, 0)
    own00, own01 = tile_block(object_slab, 0, 0), tile_block(object_slab, 0, 1)
    own10, own11 = tile_block(object_slab, 1, 0), tile_block(object_slab, 1, 1)
    own20, own21 = shift(own00, "row", -1), shift(own01, "row", -1)
    own02, own12 = shift(own00, COL, -1), shift(own10, COL, -1)
    own22 = shift(own20, COL, -1)

    blocks = (own00, own01, own02, own10, own11, own12, own20, own21, own22)
    g00, g01, g02, g10, g11, g12, g20, g21, g22, gprobe = windows(offs, count, blocks, probe, pats, tables)
    left0, left2, above1, under1, share = together(
        shift(g02, COL, 1), shift(g22, COL, 1), shift(g21, "row", 1), shift(g01, "row", -1), deal(gprobe)
    )
    g00, g20, share = together(g00 + left0, g20 + left2, share)
    above0, under0, left1, own01, own11, own21 = together(
        shift(g20, "row", 1), shift(g00, "row", -1), shift(g12, COL, 1),
        step(own01, g01, above1), step(own11, g11), step(own21, g21, under1),
    )
    own00, own20, own10, share = together(
        step(own00, g00, above0), step(own20, g20, under0), step(own10, g10, left1), share
    )
    own02, own22, own12, summed = together(
        shift(own00, COL, -1), shift(own20, COL, -1), shift(own10, COL, -1), collect(share, probe.shape)
    )
    probe = probe - pstep * summed

    blocks = (own00, own01, own02, own10, own11, own12, own20, own21, own22)
    g00, g01, g02, g10, g11, g12, g20, g21, g22, gprobe = windows(offs, count, blocks, probe, pats, tables)
    left2, left0, left1, above1, share = together(
        shift(g22, COL, 1), shift(g02, COL, 1), shift(g12, COL, 1), shift_z(g21, 1), deal(gprobe)
    )
    g20, share = together(g20 + left2, share)
    whole = most((own00, own01, own10, own11), (g00, g01, g10, g11, left0, cross_y(above1, 1), left1))
    above0, summed, whole = together(shift(g20, "row", 1), collect(share, probe.shape), whole)
    return rest(pstep, above0, probe, summed, whole)


def solution(mesh):
    mesh = Mesh(mesh.devices.reshape(-1, 4, 2, 2), ("row", *COL))
    placed = (
        P(None, "row", COL),
        P(),
        P("row", COL, None, None),
        P("row", COL),
        P("row", COL, None, None, None),
    )
    return jax.shard_map(
        body, mesh=mesh, in_specs=placed, out_specs=(P(None, "row", COL), P()), check_vma=False
    )
```

profile of v0, /device:TPU:1, one launch (start us, length us, event | category | flops | bytes accessed | tf_op | source)
XLA Modules:
  0.0 238.8 jit_solution(4564544737146792228)
XLA Ops:
  0.6 1.8 slice_bitcast_fusion.3
  2.6 7.3 %collective-permute-start.2 = (f32[2,2,256,128]{3,2,1,0:T(8,128)S(1)}, f32[2,2,256,128]{3,2,1,0:T(8,128)S(1)}, u32[]{:S(2)}, u32[]{:S(2)}) collective-permute-start(f32[2,2,256,128]{3,2,1,0:T(8,128)S(1)} %pad_maximum_fusion.refs_2_), channel_id=1, source_target_pairs={{0,112},{16,0},{32,16},{48,32},{64,48},{80,64},{96,80},{112,96},{1... | collective-permute-start | bytes 1572872 | tf_op jit(solution)/shard_map/ppermute | solution.py:239
  11.2 3.0 %collective-permute-start.1 = (f32[2,2,256,128]{3,2,1,0:T(8,128)S(1)}, f32[2,2,256,128]{3,2,1,0:T(8,128)S(1)}, u32[]{:S(2)}, u32[]{:S(2)}) collective-permute-start(f32[2,2,256,128]{3,2,1,0:T(8,128)S(1)} %pad_maximum_fusion.2.refs_5_), channel_id=1, source_target_pairs={{0,15},{1,0},{2,1},{3,2},{4,3},{5,4},{6,5},{7,6},{8,7},{9,8},{10,9... | collective-permute-start | bytes 1572872 | tf_op jit(solution)/shard_map/ppermute | solution.py:239
  14.2 1.9 fusion.2
  16.2 15.5 %collective-permute-done.2.refs_8_ = f32[2,2,256,128]{3,2,1,0:T(8,128)S(1)} collective-permute-done((f32[2,2,256,128]{3,2,1,0:T(8,128)S(1)}, f32[2,2,256,128]{3,2,1,0:T(8,128)S(1)}, u32[]{:S(2)}, u32[]{:S(2)}) %collective-permute-start.2) | collective-permute-done | bytes 524320 | tf_op jit(solution)/shard_map/ppermute | solution.py:239
  31.8 2.7 %collective-permute-start.4 = (f32[2,2,256,128]{3,2,1,0:T(8,128)S(1)}, f32[2,2,256,128]{3,2,1,0:T(8,128)S(1)}, u32[]{:S(2)}, u32[]{:S(2)}) collective-permute-start(f32[2,2,256,128]{3,2,1,0:T(8,128)S(1)} %collective-permute-done.2.refs_8_), channel_id=1, source_target_pairs={{0,15},{1,0},{2,1},{3,2},{4,3},{5,4},{6,5},{7,6},{8,7},{9,8},{10,9... | collective-permute-start | bytes 1572872 | tf_op jit(solution)/shard_map/ppermute | solution.py:239
  36.1 3.2 %fusion.refs_12_ = f32[8,256,256]{2,1,0:T(8,128)} fusion(f32[256,256,1]{1,0,2:T(8,128)S(1)} %copy-done.28, f32[256,8,256]{2,0,1:T(8,128)S(1)} %fusion.2), kind=kOutput, calls=%fused_computation | convolution fusion | flops 1610612736 | bytes 4456448 | tf_op jit(solution)/shard_map/sjk,lk->sjl/dot_general | solution.py:352
  39.3 9.3 %collective-permute-done.3.refs_9_ = f32[2,2,256,128]{3,2,1,0:T(8,128)S(1)} collective-permute-done((f32[2,2,256,128]{3,2,1,0:T(8,128)S(1)}, f32[2,2,256,128]{3,2,1,0:T(8,128)S(1)}, u32[]{:S(2)}, u32[]{:S(2)}) %collective-permute-start.3) | collective-permute-done | bytes 524320 | tf_op jit(solution)/shard_map/ppermute | solution.py:239
  48.6 2.0 collective-permute-done.4.refs_10_
  51.4 9.3 %windows.2 = (f32[2,2,256,128]{3,2,1,0:T(8,128)}, f32[2,2,256,128]{3,2,1,0:T(8,128)}, f32[2,2,256,128]{3,2,1,0:T(8,128)}, f32[2,2,256,128]{3,2,1,0:T(8,128)}, f3...) custom-call(s32[2,8]{1,0:T(2,128)S(1)} %bitcast.39, ...), custom_call_target="tpu_custom_call" | custom-call | tf_op jit(solution)/shard_map/windows/pallas_call | solution.py:225
  60.8 5.1 %collective-permute-start.8 = (f32[2,2,256,128]{3,2,1,0:T(8,128)}, f32[2,2,256,128]{3,2,1,0:T(8,128)}, u32[]{:S(2)}, u32[]{:S(2)}) collective-permute-start(f32[2,2,256,128]{3,2,1,0:T(8,128)} %get-tuple-element.58), channel_id=1, source_target_pairs={{0,112},{16,0},{32,16},{48,32},{64,48},{80,64},{96,80},{112,96},{1... | collective-permute-start | bytes 1572872 | tf_op jit(solution)/shard_map/ppermute | solution.py:239
  65.8 8.3 %collective-permute-start.5 = (f32[2,2,256,128]{3,2,1,0:T(8,128)}, f32[2,2,256,128]{3,2,1,0:T(8,128)}, u32[]{:S(2)}, u32[]{:S(2)}) collective-permute-start(f32[2,2,256,128]{3,2,1,0:T(8,128)} %get-tuple-element.55), channel_id=1, source_target_pairs={{0,1},{1,2},{2,3},{3,4},{4,5},{5,6},{6,7},{7,8},{8,9},{9,10},{10,1... | collective-permute-start | bytes 1572872 | tf_op jit(solution)/shard_map/ppermute | solution.py:239
  74.1 6.8 %all-to-all-start = ((f32[128,8,128]{2,1,0:T(8,128)}), f32[128,8,128]{2,1,0:T(8,128)}, u32[]{:S(2)}, u32[]{:S(2)}) async-start(f32[128,8,128]{2,1,0:T(8,128)} %bitcast.15), calls=%async_computation | async-start | bytes 1048576 | tf_op jit(solution)/shard_map/all_to_all | solution.py:319
  80.9 1.7 collective-permute-start.11
  82.6 2.1 multiply_subtract_fusion.5.refs_6_.refs_3_
  84.7 17.0 %all-to-all-done = f32[128,8,128]{2,1,0:T(8,128)} async-done(((f32[128,8,128]{2,1,0:T(8,128)}), f32[128,8,128]{2,1,0:T(8,128)}, u32[]{:S(2)}, u32[]{:S(2)}) %all-to-all-start) | async-done | bytes 524320 | tf_op jit(solution)/shard_map/all_to_all | solution.py:319
  107.4 1.9 multiply_subtract_fusion.6.refs_3_.refs_1_
  109.4 1.9 multiply_subtract_fusion.4.refs_9_
  111.3 7.8 %collective-permute-done.10 = f32[2,2,256,128]{3,2,1,0:T(8,128)S(1)} collective-permute-done((f32[2,2,256,128]{3,2,1,0:T(8,128)S(1)}, f32[2,2,256,128]{3,2,1,0:T(8,128)S(1)}, u32[]{:S(2)}, u32[]{:S(2)}) %collective-permute-start.10) | collective-permute-done | bytes 524320 | tf_op jit(solution)/shard_map/ppermute | solution.py:239
  119.1 3.8 %collective-permute-done.9 = f32[2,2,256,128]{3,2,1,0:T(8,128)S(1)} collective-permute-done((f32[2,2,256,128]{3,2,1,0:T(8,128)S(1)}, f32[2,2,256,128]{3,2,1,0:T(8,128)S(1)}, u32[]{:S(2)}, u32[]{:S(2)}) %collective-permute-start.9) | collective-permute-done | bytes 524320 | tf_op jit(solution)/shard_map/ppermute | solution.py:239
  124.4 1.6 collective-permute-start.12
  128.0 28.4 %all_to_all.20 = f32[128,8,128]{2,1,0:T(8,128)S(1)} all-to-all(f32[128,8,128]{2,1,0:T(8,128)S(1)} %broadcast_in_dim.4), channel_id=1, replica_groups=mesh['row'=8,'x'=4,'y_lo'=2,'core'=2] {'row','x','y_lo','core'}, dimensions={0} | all-to-all | bytes 1048576 | tf_op jit(solution)/shard_map/all_to_all | solution.py:325
  157.6 8.5 %windows.3 = (f32[2,2,256,128]{3,2,1,0:T(8,128)}, f32[2,2,256,128]{3,2,1,0:T(8,128)}, f32[2,2,256,128]{3,2,1,0:T(8,128)}, f32[2,2,256,128]{3,2,1,0:T(8,128)}, f3...) custom-call(s32[2,8]{1,0:T(2,128)S(1)} %bitcast.40, ...), custom_call_target="tpu_custom_call" | custom-call | tf_op jit(solution)/shard_map/windows/pallas_call | solution.py:225
  166.2 9.0 %collective-permute-start.15 = (f32[2,2,256,128]{3,2,1,0:T(8,128)}, f32[2,2,256,128]{3,2,1,0:T(8,128)}, u32[]{:S(2)}, u32[]{:S(2)}) collective-permute-start(f32[2,2,256,128]{3,2,1,0:T(8,128)} %get-tuple-element.87), channel_id=1, source_target_pairs={{0,1},{1,2},{2,3},{3,4},{4,5},{5,6},{6,7},{7,8},{8,9},{9,10},{10,1... | collective-permute-start | bytes 1572872 | tf_op jit(solution)/shard_map/ppermute | solution.py:239
  175.3 30.4 %all_to_all.21 = f32[128,8,128]{2,1,0:T(8,128)S(1)} all-to-all(f32[128,8,128]{2,1,0:T(8,128)S(1)} %bitcast.38), channel_id=1, replica_groups=mesh['row'=8,'x'=4,'y_lo'=2,'core'=2] {'row','x','y_lo','core'}, dimensions={0} | all-to-all | bytes 1048576 | tf_op jit(solution)/shard_map/all_to_all | solution.py:319
  205.9 3.2 %collective-permute-start.20 = (f32[2,2,256,128]{3,2,1,0:T(8,128)}, f32[2,2,256,128]{3,2,1,0:T(8,128)}, u32[]{:S(2)}, u32[]{:S(2)}) collective-permute-start(f32[2,2,256,128]{3,2,1,0:T(8,128)} %collective-permute-done.18), channel_id=1, source_target_pairs={{0,64},{64,0},{1,65},{65,1},{2,66},{66,2},{3,67},{67,3},{4,68},{68... | collective-permute-start | bytes 1572872 | tf_op jit(solution)/shard_map/ppermute | solution.py:252
  209.1 2.1 add.35
  212.1 9.2 %all-to-all-start.3 = ((f32[128,8,128]{2,1,0:T(8,128)}), f32[128,8,128]{2,1,0:T(8,128)S(1)}, u32[]{:S(2)}, u32[]{:S(2)}) async-start(f32[128,8,128]{2,1,0:T(8,128)} %broadcast_in_dim.5), calls=%async_computation.3 | async-start | bytes 1048576 | tf_op jit(solution)/shard_map/all_to_all | solution.py:325
  222.7 1.9 broadcast_select_fusion.refs_9_
  224.6 4.4 %most.1.whole_in = f32[2,512,512]{2,1,0:T(8,128)} custom-call(f32[2,2,256,128]{3,2,1,0:T(8,128)} %copy-done.7, f32[2,2,256,128]{3,2,1,0:T(8,128)} %multiply_subtract_fusion.6.refs_3_.refs_1_, f32[2,2,256,128]{3,2,1,0:T(8,128)} %copy-done.6, f32[2,2,256,128]{3,2,1,0:T(8,128)} %multiply_subtract_fusion.5.refs_6_.refs_3_, ...), custom_call_target="tpu_custom_call" | custom-call | tf_op jit(solution)/shard_map/most/pallas_call | solution.py:293
  229.0 5.8 %all-to-all-done.3 = f32[128,8,128]{2,1,0:T(8,128)S(1)} async-done(((f32[128,8,128]{2,1,0:T(8,128)}), f32[128,8,128]{2,1,0:T(8,128)S(1)}, u32[]{:S(2)}, u32[]{:S(2)}) %all-to-all-start.3) | async-done | bytes 524320 | tf_op jit(solution)/shard_map/all_to_all | solution.py:325
  234.8 3.8 %rest.1 = (f32[2,512,512]{2,1,0:T(8,128)}, f32[2,256,256]{2,1,0:T(8,128)}) custom-call(f32[2,2,256,128]{3,2,1,0:T(8,128)} %collective-permute-done.19.grad, f32[2,2,256,128]{3,2,1,0:T(8,128)S(1)} %multiply_subtract_fusion.refs_11_.probe, f32[2,2,256,128]{3,2,1,0:T(8,128)S(1)} %bitcast.37, f32[2,512,512]{2,1,0:T(8,128)} %most.1.whole_in), custom_call_target="tpu_custom_call", output_to_operand_aliasing={{0}: (3, {})} | custom-call | tf_op jit(solution)/shard_map/rest/pallas_call | solution.py:306
  (121 shorter events, 16.0 us)
Async XLA Ops:
  2.5 31.9 %copy-start.10 = (f32[1,2,256,128]{3,2,1,0:T(8,128)}, f32[1,2,256,128]{3,2,1,0:T(8,128)S(1)}, u32[]{:S(2)}) copy-start(f32[1,2,256,128]{3,2,1,0:T(8,128)S(1)} %get-tuple-element.106) | copy-start | bytes 786436
  2.5 31.9 %copy-start.11 = (f32[1,2,256,128]{3,2,1,0:T(8,128)}, f32[1,2,256,128]{3,2,1,0:T(8,128)S(1)}, u32[]{:S(2)}) copy-start(f32[1,2,256,128]{3,2,1,0:T(8,128)S(1)} %get-tuple-element.113) | copy-start | bytes 786436
  2.6 29.1 %collective-permute-start.2 = (f32[2,2,256,128]{3,2,1,0:T(8,128)S(1)}, f32[2,2,256,128]{3,2,1,0:T(8,128)S(1)}, u32[]{:S(2)}, u32[]{:S(2)}) collective-permute-start(f32[2,2,256,128]{3,2,1,0:T(8,128)S(1)} %pad_maximum_fusion.refs_2_), channel_id=1, source_target_pairs={{0,112},{16,0},{32,16},{48,32},{64,48},{80,64},{96,80},{112,96},{1... | collective-permute-start | bytes 1572872 | tf_op jit(solution)/shard_map/ppermute | solution.py:239
  9.9 38.7 %collective-permute-start = (f32[2,2,256,128]{3,2,1,0:T(8,128)S(1)}, f32[2,2,256,128]{3,2,1,0:T(8,128)S(1)}, u32[]{:S(2)}, u32[]{:S(2)}) collective-permute-start(f32[2,2,256,128]{3,2,1,0:T(8,128)S(1)} %pad_maximum_fusion.refs_2_), channel_id=1, source_target_pairs={{0,15},{1,0},{2,1},{3,2},{4,3},{5,4},{6,5},{7,6},{8,7},{9,8},{10,9... | collective-permute-start | bytes 1572872 | tf_op jit(solution)/shard_map/ppermute | solution.py:239
  10.9 37.7 %collective-permute-start.3 = (f32[2,2,256,128]{3,2,1,0:T(8,128)S(1)}, f32[2,2,256,128]{3,2,1,0:T(8,128)S(1)}, u32[]{:S(2)}, u32[]{:S(2)}) collective-permute-start(f32[2,2,256,128]{3,2,1,0:T(8,128)S(1)} %pad_maximum_fusion.1.refs_3_), channel_id=1, source_target_pairs={{0,112},{16,0},{32,16},{48,32},{64,48},{80,64},{96,80},{112,96},{1... | collective-permute-start | bytes 1572872 | tf_op jit(solution)/shard_map/ppermute | solution.py:239
  11.2 37.4 %collective-permute-start.1 = (f32[2,2,256,128]{3,2,1,0:T(8,128)S(1)}, f32[2,2,256,128]{3,2,1,0:T(8,128)S(1)}, u32[]{:S(2)}, u32[]{:S(2)}) collective-permute-start(f32[2,2,256,128]{3,2,1,0:T(8,128)S(1)} %pad_maximum_fusion.2.refs_5_), channel_id=1, source_target_pairs={{0,15},{1,0},{2,1},{3,2},{4,3},{5,4},{6,5},{7,6},{8,7},{9,8},{10,9... | collective-permute-start | bytes 1572872 | tf_op jit(solution)/shard_map/ppermute | solution.py:239
  14.2 21.8 %copy-start.12 = (f32[1,2,256,128]{3,2,1,0:T(8,128)}, f32[1,2,256,128]{3,2,1,0:T(8,128)S(1)}, u32[]{:S(2)}) copy-start(f32[1,2,256,128]{3,2,1,0:T(8,128)S(1)} %get-tuple-element.114) | copy-start | bytes 786436
  14.2 21.8 %copy-start.14 = (f32[1,2,256,128]{3,2,1,0:T(8,128)}, f32[1,2,256,128]{3,2,1,0:T(8,128)S(1)}, u32[]{:S(2)}) copy-start(f32[1,2,256,128]{3,2,1,0:T(8,128)S(1)} %get-tuple-element.115) | copy-start | bytes 786436
  31.8 18.8 %collective-permute-start.4 = (f32[2,2,256,128]{3,2,1,0:T(8,128)S(1)}, f32[2,2,256,128]{3,2,1,0:T(8,128)S(1)}, u32[]{:S(2)}, u32[]{:S(2)}) collective-permute-start(f32[2,2,256,128]{3,2,1,0:T(8,128)S(1)} %collective-permute-done.2.refs_8_), channel_id=1, source_target_pairs={{0,15},{1,0},{2,1},{3,2},{4,3},{5,4},{6,5},{7,6},{8,7},{9,8},{10,9... | collective-permute-start | bytes 1572872 | tf_op jit(solution)/shard_map/ppermute | solution.py:239
  60.7 42.3 %collective-permute-start.7 = (f32[2,2,256,128]{3,2,1,0:T(8,128)}, f32[2,2,256,128]{3,2,1,0:T(8,128)}, u32[]{:S(2)}, u32[]{:S(2)}) collective-permute-start(f32[2,2,256,128]{3,2,1,0:T(8,128)} %get-tuple-element.57), channel_id=1, source_target_pairs={{0,16},{16,32},{32,48},{48,64},{64,80},{80,96},{96,112},{112,0},{1... | collective-permute-start | bytes 1572872 | tf_op jit(solution)/shard_map/ppermute | solution.py:239
  60.8 42.2 %collective-permute-start.8 = (f32[2,2,256,128]{3,2,1,0:T(8,128)}, f32[2,2,256,128]{3,2,1,0:T(8,128)}, u32[]{:S(2)}, u32[]{:S(2)}) collective-permute-start(f32[2,2,256,128]{3,2,1,0:T(8,128)} %get-tuple-element.58), channel_id=1, source_target_pairs={{0,112},{16,0},{32,16},{48,32},{64,48},{80,64},{96,80},{112,96},{1... | collective-permute-start | bytes 1572872 | tf_op jit(solution)/shard_map/ppermute | solution.py:239
  65.8 37.1 %collective-permute-start.5 = (f32[2,2,256,128]{3,2,1,0:T(8,128)}, f32[2,2,256,128]{3,2,1,0:T(8,128)}, u32[]{:S(2)}, u32[]{:S(2)}) collective-permute-start(f32[2,2,256,128]{3,2,1,0:T(8,128)} %get-tuple-element.55), channel_id=1, source_target_pairs={{0,1},{1,2},{2,3},{3,4},{4,5},{5,6},{6,7},{7,8},{8,9},{9,10},{10,1... | collective-permute-start | bytes 1572872 | tf_op jit(solution)/shard_map/ppermute | solution.py:239
  74.1 28.9 %collective-permute-start.6 = (f32[2,2,256,128]{3,2,1,0:T(8,128)}, f32[2,2,256,128]{3,2,1,0:T(8,128)}, u32[]{:S(2)}, u32[]{:S(2)}) collective-permute-start(f32[2,2,256,128]{3,2,1,0:T(8,128)} %get-tuple-element.56), channel_id=1, source_target_pairs={{0,1},{1,2},{2,3},{3,4},{4,5},{5,6},{6,7},{7,8},{8,9},{9,10},{10,1... | collective-permute-start | bytes 1572872 | tf_op jit(solution)/shard_map/ppermute | solution.py:239
  74.1 27.6 %all-to-all-start = ((f32[128,8,128]{2,1,0:T(8,128)}), f32[128,8,128]{2,1,0:T(8,128)}, u32[]{:S(2)}, u32[]{:S(2)}) async-start(f32[128,8,128]{2,1,0:T(8,128)} %bitcast.15), calls=%async_computation | async-start | bytes 1048576 | tf_op jit(solution)/shard_map/all_to_all | solution.py:319
  80.9 30.4 %collective-permute-start.11 = (f32[2,2,256,128]{3,2,1,0:T(8,128)}, f32[2,2,256,128]{3,2,1,0:T(8,128)}, u32[]{:S(2)}, u32[]{:S(2)}) collective-permute-start(f32[2,2,256,128]{3,2,1,0:T(8,128)} %get-tuple-element.66), channel_id=1, source_target_pairs={{0,1},{1,2},{2,3},{3,4},{4,5},{5,6},{6,7},{7,8},{8,9},{9,10},{10,1... | collective-permute-start | bytes 1572872 | tf_op jit(solution)/shard_map/ppermute | solution.py:239
  105.7 13.4 %collective-permute-start.10 = (f32[2,2,256,128]{3,2,1,0:T(8,128)S(1)}, f32[2,2,256,128]{3,2,1,0:T(8,128)S(1)}, u32[]{:S(2)}, u32[]{:S(2)}) collective-permute-start(f32[2,2,256,128]{3,2,1,0:T(8,128)S(1)} %add.28), channel_id=1, source_target_pairs={{0,112},{16,0},{32,16},{48,32},{64,48},{80,64},{96,80},{112,96},{1... | collective-permute-start | bytes 1572872 | tf_op jit(solution)/shard_map/ppermute | solution.py:239
  106.5 16.4 %collective-permute-start.9 = (f32[2,2,256,128]{3,2,1,0:T(8,128)S(1)}, f32[2,2,256,128]{3,2,1,0:T(8,128)S(1)}, u32[]{:S(2)}, u32[]{:S(2)}) collective-permute-start(f32[2,2,256,128]{3,2,1,0:T(8,128)S(1)} %add.29), channel_id=1, source_target_pairs={{0,16},{16,32},{32,48},{48,64},{64,80},{80,96},{96,112},{112,0},{1... | collective-permute-start | bytes 1572872 | tf_op jit(solution)/shard_map/ppermute | solution.py:239
  124.2 32.3 %copy-start.6 = (f32[2,2,256,128]{3,2,1,0:T(8,128)}, f32[2,2,256,128]{3,2,1,0:T(8,128)S(1)}, u32[]{:S(2)}) copy-start(f32[2,2,256,128]{3,2,1,0:T(8,128)S(1)} %get-tuple-element.78.refs_5_.refs_2_) | copy-start | bytes 1572868
  124.2 32.3 %copy-start.7 = (f32[2,2,256,128]{3,2,1,0:T(8,128)}, f32[2,2,256,128]{3,2,1,0:T(8,128)S(1)}, u32[]{:S(2)}) copy-start(f32[2,2,256,128]{3,2,1,0:T(8,128)S(1)} %get-tuple-element.75.refs_2_.refs_0_) | copy-start | bytes 1572868
  124.2 32.2 %copy-start.13 = (f32[1,2,256,128]{3,2,1,0:T(8,128)S(1)}, f32[1,2,256,128]{3,2,1,0:T(8,128)}, u32[]{:S(2)}) copy-start(f32[1,2,256,128]{3,2,1,0:T(8,128)} %copy-done.12) | copy-start | bytes 786436
  124.3 32.2 %copy-start.15 = (f32[1,2,256,128]{3,2,1,0:T(8,128)S(1)}, f32[1,2,256,128]{3,2,1,0:T(8,128)}, u32[]{:S(2)}) copy-start(f32[1,2,256,128]{3,2,1,0:T(8,128)} %copy-done.14) | copy-start | bytes 786436
  124.4 32.2 %copy-start.27 = (f32[2,2,256,128]{3,2,1,0:T(8,128)}, f32[2,2,256,128]{3,2,1,0:T(8,128)S(1)}, u32[]{:S(2)}) copy-start(f32[2,2,256,128]{3,2,1,0:T(8,128)S(1)} %multiply_subtract_fusion.2.refs_8_) | copy-start | bytes 1572868
  124.4 32.1 %collective-permute-start.12 = (f32[2,2,256,128]{3,2,1,0:T(8,128)S(1)}, f32[2,2,256,128]{3,2,1,0:T(8,128)S(1)}, u32[]{:S(2)}, u32[]{:S(2)}) collective-permute-start(f32[2,2,256,128]{3,2,1,0:T(8,128)S(1)} %get-tuple-element.75.refs_2_.refs_0_), channel_id=1, source_target_pairs={{0,15},{1,0},{2,1},{3,2},{4,3},{5,4},{6,5},{7,6},{8,7},{9,8},{10,9... | collective-permute-start | bytes 1572872 | tf_op jit(solution)/shard_map/ppermute | solution.py:239
  126.0 30.4 %collective-permute-start.13 = (f32[2,2,256,128]{3,2,1,0:T(8,128)S(1)}, f32[2,2,256,128]{3,2,1,0:T(8,128)S(1)}, u32[]{:S(2)}, u32[]{:S(2)}) collective-permute-start(f32[2,2,256,128]{3,2,1,0:T(8,128)S(1)} %multiply_subtract_fusion.2.refs_8_), channel_id=1, source_target_pairs={{0,15},{1,0},{2,1},{3,2},{4,3},{5,4},{6,5},{7,6},{8,7},{9,8},{10,9... | collective-permute-start | bytes 1572872 | tf_op jit(solution)/shard_map/ppermute | solution.py:239
  126.4 30.0 %collective-permute-start.14 = (f32[2,2,256,128]{3,2,1,0:T(8,128)S(1)}, f32[2,2,256,128]{3,2,1,0:T(8,128)S(1)}, u32[]{:S(2)}, u32[]{:S(2)}) collective-permute-start(f32[2,2,256,128]{3,2,1,0:T(8,128)S(1)} %get-tuple-element.78.refs_5_.refs_2_), channel_id=1, source_target_pairs={{0,15},{1,0},{2,1},{3,2},{4,3},{5,4},{6,5},{7,6},{8,7},{9,8},{10,9... | collective-permute-start | bytes 1572872 | tf_op jit(solution)/shard_map/ppermute | solution.py:239
  166.2 39.7 %collective-permute-start.15 = (f32[2,2,256,128]{3,2,1,0:T(8,128)}, f32[2,2,256,128]{3,2,1,0:T(8,128)}, u32[]{:S(2)}, u32[]{:S(2)}) collective-permute-start(f32[2,2,256,128]{3,2,1,0:T(8,128)} %get-tuple-element.87), channel_id=1, source_target_pairs={{0,1},{1,2},{2,3},{3,4},{4,5},{5,6},{6,7},{7,8},{8,9},{9,10},{10,1... | collective-permute-start | bytes 1572872 | tf_op jit(solution)/shard_map/ppermute | solution.py:239
  175.1 30.8 %collective-permute-start.16 = (f32[2,2,256,128]{3,2,1,0:T(8,128)}, f32[2,2,256,128]{3,2,1,0:T(8,128)}, u32[]{:S(2)}, u32[]{:S(2)}) collective-permute-start(f32[2,2,256,128]{3,2,1,0:T(8,128)} %get-tuple-element.88), channel_id=1, source_target_pairs={{0,1},{1,2},{2,3},{3,4},{4,5},{5,6},{6,7},{7,8},{8,9},{9,10},{10,1... | collective-permute-start | bytes 1572872 | tf_op jit(solution)/shard_map/ppermute | solution.py:239
  175.2 30.7 %collective-permute-start.17 = (f32[2,2,256,128]{3,2,1,0:T(8,128)}, f32[2,2,256,128]{3,2,1,0:T(8,128)}, u32[]{:S(2)}, u32[]{:S(2)}) collective-permute-start(f32[2,2,256,128]{3,2,1,0:T(8,128)} %get-tuple-element.89), channel_id=1, source_target_pairs={{0,1},{1,2},{2,3},{3,4},{4,5},{5,6},{6,7},{7,8},{8,9},{9,10},{10,1... | collective-permute-start | bytes 1572872 | tf_op jit(solution)/shard_map/ppermute | solution.py:239
  175.3 30.6 %collective-permute-start.18 = (f32[2,2,256,128]{3,2,1,0:T(8,128)}, f32[2,2,256,128]{3,2,1,0:T(8,128)}, u32[]{:S(2)}, u32[]{:S(2)}) collective-permute-start(f32[2,2,256,128]{3,2,1,0:T(8,128)} %get-tuple-element.90), channel_id=1, source_target_pairs={{0,16},{16,32},{32,48},{48,0},{64,80},{80,96},{96,112},{112,64},{1... | collective-permute-start | bytes 1572872 | tf_op jit(solution)/shard_map/ppermute | solution.py:247
  205.9 16.8 %collective-permute-start.20 = (f32[2,2,256,128]{3,2,1,0:T(8,128)}, f32[2,2,256,128]{3,2,1,0:T(8,128)}, u32[]{:S(2)}, u32[]{:S(2)}) collective-permute-start(f32[2,2,256,128]{3,2,1,0:T(8,128)} %collective-permute-done.18), channel_id=1, source_target_pairs={{0,64},{64,0},{1,65},{65,1},{2,66},{66,2},{3,67},{67,3},{4,68},{68... | collective-permute-start | bytes 1572872 | tf_op jit(solution)/shard_map/ppermute | solution.py:252
  211.2 23.6 %collective-permute-start.19 = (f32[2,2,256,128]{3,2,1,0:T(8,128)}, f32[2,2,256,128]{3,2,1,0:T(8,128)}, u32[]{:S(2)}, u32[]{:S(2)}) collective-permute-start(f32[2,2,256,128]{3,2,1,0:T(8,128)} %add.35), channel_id=1, source_target_pairs={{0,16},{16,32},{32,48},{48,64},{64,80},{80,96},{96,112},{112,0},{1... | collective-permute-start | bytes 1572872 | tf_op jit(solution)/shard_map/ppermute | solution.py:239
  212.1 22.8 %all-to-all-start.3 = ((f32[128,8,128]{2,1,0:T(8,128)}), f32[128,8,128]{2,1,0:T(8,128)S(1)}, u32[]{:S(2)}, u32[]{:S(2)}) async-start(f32[128,8,128]{2,1,0:T(8,128)} %broadcast_in_dim.5), calls=%async_computation.3 | async-start | bytes 1048576 | tf_op jit(solution)/shard_map/all_to_all | solution.py:325
  (30 other events, 248.9 us)
where the time goes:
time: 239 us
  starting transfers between devices  63 us (26%)
  waiting for transfers between devices  62.7 us (26%)
  blocking collectives  58.8 us (25%)
  Pallas kernels  25.9 us (11%)
  other arithmetic  16.4 us (7%)
  matrix products  5.08 us (2%)
  local copies, waits for them, and re-layouts  4.76 us (2%)
    ppermute x19, starting transfers between devices, shift(): lax.ppermute(block, axis, [(i, (i + distance) % n) for i in range(n)])  43.7 us
    ppermute x19, waiting for transfers between devices, shift(): lax.ppermute(block, axis, [(i, (i + distance) % n) for i in range(n)])  38.5 us
    all_to_all x1, blocking collectives, deal(): lax.all_to_all(x.reshape(-1, 8, LANES), ('row', *COL), 0, 0, tiled=True)  30.4 us
    all_to_all x1, blocking collectives, collect(): lax.all_to_all(spread, ('row', *COL), 0, 0, tiled=True).reshape(shape)  28.4 us
    pallas_call x2, Pallas kernels, windows(): pl.pallas_call(windows_kernel, out_shape=[pltpu.HBM(block.shape, F32)] *...  17.8 us
    all_to_all x1, waiting for transfers between devices, deal(): lax.all_to_all(x.reshape(-1, 8, LANES), ('row', *COL), 0, 0, tiled=True)  17 us
    all_to_all x1, starting transfers between devices, collect(): lax.all_to_all(spread, ('row', *COL), 0, 0, tiled=True).reshape(shape)  9.23 us
    sub x5, other arithmetic, step(): return x - OBJECT_RATE * sum(grads[1:], grads[0])  7.32 us
  transfers between devices with their start and end apart: 23, of which 8 were waited for; matrix products, arithmetic and copies ran while one was open for 9% of the time, Pallas kernels for 2%

commit v1 on v0

--- a/solution.py
+++ b/solution.py
@@ -194,15 +194,15 @@
 
     def pair(k, carry):
         turns = []
-        for n in range(2):
-            live = None if n == 0 else jnp.where(2 * k + 1 < count[0], 1.0, 0.0)
+        for n in range(4):
+            live = None if n == 0 else jnp.where(4 * k + n < count[0], 1.0, 0.0)
             own = [buffer.at[n] for buffer in scratch]
-            turns.append(window(2 * k + n, live, offs, probe, pats_here, tables, ext, gacc, gprobe, own))
+            turns.append(window(4 * k + n, live, offs, probe, pats_here, tables, ext, gacc, gprobe, own))
         for _ in itertools.zip_longest(*turns):
             pass
         return carry
 
-    lax.fori_loop(0, (count[0] + 1) // 2, pair, 0)
+    lax.fori_loop(0, (count[0] + 3) // 4, pair, 0)
     departures = [pltpu.make_async_copy(place(gacc, k), grads[k], sem_out.at[k]) for k in range(9)]
     for copy in departures:
         copy.start()
@@ -219,8 +219,8 @@
     vmem = pl.BlockSpec(memory_space=pltpu.VMEM)
     where = pl.BlockSpec(memory_space=pl.ANY)
     block = jax.ShapeDtypeStruct((2, 2, M, LANES), F32)
-    halves16 = pltpu.VMEM((2, 2, M, M), BF16)
-    whole32 = pltpu.VMEM((2, 2, M, M), F32)
+    halves16 = pltpu.VMEM((4, 2, M, M), BF16)
+    whole32 = pltpu.VMEM((4, 2, M, M), F32)
     extended = pltpu.VMEM((6, 2, 3 * M, LANES), F32)
     return pl.pallas_call(
         windows_kernel,
@@ -229,7 +229,7 @@
         out_specs=[where] * 9 + [vmem],
         scratch_shapes=[extended, extended, pltpu.VMEM(pats.shape, F32)] + [halves16] * 4 + [whole32] * 2
         + [pltpu.SemaphoreType.DMA((9,)), pltpu.SemaphoreType.DMA((9,)), pltpu.SemaphoreType.DMA],
-        compiler_params=pltpu.CompilerParams(vmem_limit_bytes=24 * 1024 * 1024),
+        compiler_params=pltpu.CompilerParams(vmem_limit_bytes=34 * 1024 * 1024),
         name="windows",
     )(offs, count, *in_hbm(blocks), probe, *in_hbm([pats]), *tables)
 
@@ -249,18 +249,22 @@
 
 def cross_y(block, distance):
     n, edge = lax.axis_size("row"), 0 if distance > 0 else RING - 1
-    far = lax.ppermute(block, "row", [(i, (i + RING) % n) for i in range(edge, n, RING)])
-    return jnp.where(lax.axis_index("row") % RING == edge, far, block)
+    wrapped = (lax.axis_index("row") % RING == edge).astype(jnp.int32).reshape(1)
+    return lax.ppermute(block, "row", [(i, (i + RING) % n) for i in range(edge, n, RING)]), wrapped
+
+
+def fetch(refs, here, sem):
+    copies = [pltpu.make_async_copy(ref, here.at[k], sem.at[k]) for k, ref in enumerate(refs)]
+    for copy in copies:
+        copy.start()
+    for copy in copies:
+        copy.wait()
 
 
 def most_kernel(*refs):
-    whole, here, sem = refs[11:]
-    arrivals = [pltpu.make_async_copy(refs[k], here.at[k], sem.at[k]) for k in range(11)]
-    for copy in arrivals:
-        copy.start()
-    for copy in arrivals:
-        copy.wait()
-    for k, grads in enumerate(((4, 8), (5, 9), (6, 10), (7,))):
+    whole, here, sem = refs[10:]
+    fetch(refs[:10], here, sem)
+    for k, grads in enumerate(((4, 8), (5,), (6, 9), (7,))):
         i, j = divmod(k, 2)
         for tile in range(2):
             lanes = pl.ds((2 * j + tile) * LANES, LANES)
@@ -269,22 +273,26 @@
                 whole[part, pl.ds(i * M, M), lanes] = here[k, tile, part] - OBJECT_RATE * total
 
 
-def rest_kernel(pstep, grad, probe, summed, whole_in, whole, probe_out, corner, sem):
+def rest_kernel(pstep, wrapped, above0, near, far, probe, summed, whole_in, whole, probe_out, top, here, sem, sem_top):
     del whole_in
-    view = whole.at[:, pl.ds(0, M), pl.ds(0, M)]
-    arrive = pltpu.make_async_copy(view, corner, sem.at[0])
+    view = whole.at[:, pl.ds(0, M), :]
+    arrive = pltpu.make_async_copy(view, top, sem_top.at[0])
     arrive.start()
+    fetch((above0, near, far, probe, summed), here, sem)
+    arrive.wait()
+    from_far = wrapped[0] == 1
+    for tile in range(2):
+        for part in range(2):
+            lanes, beside = pl.ds(tile * LANES, LANES), pl.ds((2 + tile) * LANES, LANES)
+            top[part, :, lanes] = top[part, :, lanes] - OBJECT_RATE * here[0, tile, part]
+            above1 = jnp.where(from_far, here[2, tile, part], here[1, tile, part])
+            top[part, :, beside] = top[part, :, beside] - OBJECT_RATE * above1
+    leave = pltpu.make_async_copy(top, view, sem_top.at[1])
+    leave.start()
     for tile in range(2):
         for part in range(2):
             lanes = pl.ds(tile * LANES, LANES)
-            probe_out[part, :, lanes] = probe[tile, part] - pstep * summed[tile, part]
-    arrive.wait()
-    for tile in range(2):
-        for part in range(2):
-            lanes = pl.ds(tile * LANES, LANES)
-            corner[part, :, lanes] = corner[part, :, lanes] - OBJECT_RATE * grad[tile, part]
-    leave = pltpu.make_async_copy(corner, view, sem.at[1])
-    leave.start()
+            probe_out[part, :, lanes] = here[3, tile, part] - pstep * here[4, tile, part]
     leave.wait()
 
 
@@ -293,35 +301,40 @@
     return pl.pallas_call(
         most_kernel,
         out_shape=jax.ShapeDtypeStruct((2, 2 * M, 2 * M), F32),
-        in_specs=[where] * 11,
+        in_specs=[where] * 10,
         out_specs=vmem,
-        scratch_shapes=[pltpu.VMEM((11, *own[0].shape), F32), pltpu.SemaphoreType.DMA((11,))],
+        scratch_shapes=[pltpu.VMEM((10, *own[0].shape), F32), pltpu.SemaphoreType.DMA((10,))],
         compiler_params=pltpu.CompilerParams(vmem_limit_bytes=24 * 1024 * 1024),
         name="most",
     )(*in_hbm([*own, *grads]))
 
 
-def rest(pstep, grad, probe, summed, whole):
-    vmem, where = pl.BlockSpec(memory_space=pltpu.VMEM), pl.BlockSpec(memory_space=pl.ANY)
+def rest(pstep, wrapped, moved, probe, summed, whole):
+    smem, vmem = pl.BlockSpec(memory_space=pltpu.SMEM), pl.BlockSpec(memory_space=pltpu.VMEM)
+    where = pl.BlockSpec(memory_space=pl.ANY)
     return pl.pallas_call(
         functools.partial(rest_kernel, pstep),
         out_shape=(pltpu.HBM(whole.shape, F32), jax.ShapeDtypeStruct((2, M, M), F32)),
-        in_specs=[vmem] * 3 + [where],
+        in_specs=[smem] + [where] * 6,
         out_specs=(where, vmem),
-        scratch_shapes=[pltpu.VMEM((2, M, M), F32), pltpu.SemaphoreType.DMA((2,))],
-        input_output_aliases={3: 0},
+        scratch_shapes=[
+            pltpu.VMEM((2, M, 2 * M), F32),
+            pltpu.VMEM((5, *probe.shape), F32),
+            pltpu.SemaphoreType.DMA((5,)),
+            pltpu.SemaphoreType.DMA((2,)),
+        ],
+        input_output_aliases={6: 0},
         compiler_params=pltpu.CompilerParams(vmem_limit_bytes=24 * 1024 * 1024),
         name="rest",
-    )(grad, probe, summed, *in_hbm([whole]))
+    )(wrapped, *in_hbm([*moved, probe, summed, whole]))
 
 
 def deal(x):
-    return jnp.sum(lax.all_to_all(x.reshape(-1, 8, LANES), ("row", *COL), 0, 0, tiled=True), axis=0)
-
-
-def collect(share, shape):
-    n = lax.axis_size(("row", *COL))
-    spread = jnp.broadcast_to(share[None], (n, *share.shape))
+    return lax.all_to_all(x.reshape(-1, 8, LANES), ("row", *COL), 0, 0, tiled=True)
+
+
+def collect(terms, shape):
+    spread = jnp.broadcast_to(jnp.sum(terms, axis=0)[None], terms.shape)
     return lax.all_to_all(spread, ("row", *COL), 0, 0, tiled=True).reshape(shape)
 
 
@@ -363,31 +376,32 @@
 
     blocks = (own00, own01, own02, own10, own11, own12, own20, own21, own22)
     g00, g01, g02, g10, g11, g12, g20, g21, g22, gprobe = windows(offs, count, blocks, probe, pats, tables)
-    left0, left2, above1, under1, share = together(
-        shift(g02, COL, 1), shift(g22, COL, 1), shift(g21, "row", 1), shift(g01, "row", -1), deal(gprobe)
-    )
-    g00, g20, share = together(g00 + left0, g20 + left2, share)
-    above0, under0, left1, own01, own11, own21 = together(
-        shift(g20, "row", 1), shift(g00, "row", -1), shift(g12, COL, 1),
+    terms = deal(gprobe)
+    left0, left2 = shift(g02, COL, 1), shift(g22, COL, 1)
+    above1, under1 = shift(g21, "row", 1), shift(g01, "row", -1)
+    left1 = shift(g12, COL, 1)
+    g00, g20 = together(g00 + left0, g20 + left2)
+    summed = collect(together(terms, g00, g20)[0], probe.shape)
+    own10 = step(own10, g10, left1)
+    above0, under0, own12, own01, own11, own21 = together(
+        shift(g20, "row", 1), shift(g00, "row", -1), shift(own10, COL, -1),
         step(own01, g01, above1), step(own11, g11), step(own21, g21, under1),
     )
-    own00, own20, own10, share = together(
-        step(own00, g00, above0), step(own20, g20, under0), step(own10, g10, left1), share
-    )
-    own02, own22, own12, summed = together(
-        shift(own00, COL, -1), shift(own20, COL, -1), shift(own10, COL, -1), collect(share, probe.shape)
-    )
+    own00, own20 = together(step(own00, g00, above0), step(own20, g20, under0))
+    own02, own22 = shift(own00, COL, -1), shift(own20, COL, -1)
     probe = probe - pstep * summed
 
     blocks = (own00, own01, own02, own10, own11, own12, own20, own21, own22)
     g00, g01, g02, g10, g11, g12, g20, g21, g22, gprobe = windows(offs, count, blocks, probe, pats, tables)
-    left2, left0, left1, above1, share = together(
-        shift(g22, COL, 1), shift(g02, COL, 1), shift(g12, COL, 1), shift_z(g21, 1), deal(gprobe)
-    )
-    g20, share = together(g20 + left2, share)
-    whole = most((own00, own01, own10, own11), (g00, g01, g10, g11, left0, cross_y(above1, 1), left1))
-    above0, summed, whole = together(shift(g20, "row", 1), collect(share, probe.shape), whole)
-    return rest(pstep, above0, probe, summed, whole)
+    terms = deal(gprobe)
+    left2, left0, left1 = shift(g22, COL, 1), shift(g02, COL, 1), shift(g12, COL, 1)
+    above1 = shift_z(g21, 1)
+    g20 = g20 + left2
+    above0, (far1, wrapped) = shift(g20, "row", 1), cross_y(above1, 1)
+    summed = collect(together(terms, g20)[0], probe.shape)
+    whole = most((own00, own01, own10, own11), (g00, g01, g10, g11, left0, left1))
+    above0, far1, summed, whole = together(above0, far1, summed, whole)
+    return rest(pstep, wrapped, (above0, above1, far1), probe, summed, whole)
 
 
 def solution(mesh):

time: 239 us -> 219 us (0.916)
  blocking collectives: 58.8 us -> 0 us
  waiting for transfers between devices: 62.7 us -> 78.3 us
  Pallas kernels: 25.9 us -> 40.7 us
  other arithmetic: 16.4 us -> 21.6 us
  starting transfers between devices: 63 us -> 65.9 us
    all_to_all x2 -> x0, blocking collectives: 58.8 us -> none  [the longest x1 30.4 us: deal(): lax.all_to_all(x.reshape(-1, 8, LANES), ('row', *COL), 0, 0, tiled=True)]
    ppermute x19, waiting for transfers between devices: 38.5 us -> 55.1 us  [shift(): lax.ppermute(block, axis, [(i, (i + distance) % n) for i in range(n)])]
    all_to_all x1 -> x2, starting transfers between devices: 6.79 us -> 21.7 us  [deal(): lax.all_to_all(x.reshape(-1, 8, LANES), ('row', *COL), 0, 0, tiled=True)]
    pallas_call x2, Pallas kernels: 17.8 us -> 32.6 us  [windows(): pl.pallas_call(windows_kernel, out_shape=[pltpu.HBM(block.shape, F32)] *...]
    ppermute x19, starting transfers between devices: 43.7 us -> 30.4 us  [shift(): lax.ppermute(block, axis, [(i, (i + distance) % n) for i in range(n)])]
    all_to_all x1 -> x2, waiting for transfers between devices: 17 us -> 6.47 us  [deal(): lax.all_to_all(x.reshape(-1, 8, LANES), ('row', *COL), 0, 0, tiled=True)]
    all_to_all x1 -> x2, waiting for transfers between devices: 5.83 us -> 13.8 us  [collect(): lax.all_to_all(spread, ('row', *COL), 0, 0, tiled=True).reshape(shape)]
    sub x5 -> x6, other arithmetic: 7.32 us -> 11.1 us  [step(): return x - OBJECT_RATE * sum(grads[1:], grads[0])]
  transfers between devices with their start and end apart: 23 -> 25, of which waited for: 8 -> 13; matrix products, arithmetic and copies ran while one was open for 9% -> 13% of each run, Pallas kernels for 2% -> 2%
where the time goes in v1:
time: 219 us
  waiting for transfers between devices  78.3 us (36%)
  starting transfers between devices  65.9 us (30%)
  Pallas kernels  40.7 us (19%)
  other arithmetic  21.6 us (10%)
  local copies, waits for them, and re-layouts  5.33 us (2%)
  matrix products  5.08 us (2%)
    ppermute x19, waiting for transfers between devices, shift(): lax.ppermute(block, axis, [(i, (i + distance) % n) for i in range(n)])  55.1 us
    pallas_call x2, Pallas kernels, windows(): pl.pallas_call(windows_kernel, out_shape=[pltpu.HBM(block.shape, F32)] *...  32.6 us
    ppermute x19, starting transfers between devices, shift(): lax.ppermute(block, axis, [(i, (i + distance) % n) for i in range(n)])  30.4 us
    all_to_all x2, starting transfers between devices, deal(): lax.all_to_all(x.reshape(-1, 8, LANES), ('row', *COL), 0, 0, tiled=True)  21.7 us
    all_to_all x2, waiting for transfers between devices, collect(): lax.all_to_all(spread, ('row', *COL), 0, 0, tiled=True).reshape(shape)  13.8 us
    all_to_all x2, starting transfers between devices, collect(): lax.all_to_all(spread, ('row', *COL), 0, 0, tiled=True).reshape(shape)  11.9 us
    sub x6, other arithmetic, step(): return x - OBJECT_RATE * sum(grads[1:], grads[0])  11.1 us
    all_to_all x2, waiting for transfers between devices, deal(): lax.all_to_all(x.reshape(-1, 8, LANES), ('row', *COL), 0, 0, tiled=True)  6.47 us
  transfers between devices with their start and end apart: 25, of which 13 were waited for; matrix products, arithmetic and copies ran while one was open for 13% of the time, Pallas kernels for 2%

profile of v1, /device:TPU:1, one launch (start us, length us, event | category | flops | bytes accessed | tf_op | source)
XLA Modules:
  0.0 218.9 jit_solution(3074227738889877006)
XLA Ops:
  2.6 7.3 %collective-permute-start.2 = (f32[2,2,256,128]{3,2,1,0:T(8,128)S(1)}, f32[2,2,256,128]{3,2,1,0:T(8,128)S(1)}, u32[]{:S(2)}, u32[]{:S(2)}) collective-permute-start(f32[2,2,256,128]{3,2,1,0:T(8,128)S(1)} %pad_maximum_fusion.refs_2_), channel_id=1, source_target_pairs={{0,112},{16,0},{32,16},{48,32},{64,48},{80,64},{96,80},{112,96},{1... | collective-permute-start | bytes 1572872 | tf_op jit(solution)/shard_map/ppermute | solution.py:239
  11.2 3.0 %collective-permute-start.1 = (f32[2,2,256,128]{3,2,1,0:T(8,128)S(1)}, f32[2,2,256,128]{3,2,1,0:T(8,128)S(1)}, u32[]{:S(2)}, u32[]{:S(2)}) collective-permute-start(f32[2,2,256,128]{3,2,1,0:T(8,128)S(1)} %pad_maximum_fusion.2.refs_5_), channel_id=1, source_target_pairs={{0,15},{1,0},{2,1},{3,2},{4,3},{5,4},{6,5},{7,6},{8,7},{9,8},{10,9... | collective-permute-start | bytes 1572872 | tf_op jit(solution)/shard_map/ppermute | solution.py:239
  14.2 1.9 fusion.2
  16.2 15.6 %collective-permute-done.2.refs_8_ = f32[2,2,256,128]{3,2,1,0:T(8,128)S(1)} collective-permute-done((f32[2,2,256,128]{3,2,1,0:T(8,128)S(1)}, f32[2,2,256,128]{3,2,1,0:T(8,128)S(1)}, u32[]{:S(2)}, u32[]{:S(2)}) %collective-permute-start.2) | collective-permute-done | bytes 524320 | tf_op jit(solution)/shard_map/ppermute | solution.py:239
  31.7 2.7 %collective-permute-start.4 = (f32[2,2,256,128]{3,2,1,0:T(8,128)S(1)}, f32[2,2,256,128]{3,2,1,0:T(8,128)S(1)}, u32[]{:S(2)}, u32[]{:S(2)}) collective-permute-start(f32[2,2,256,128]{3,2,1,0:T(8,128)S(1)} %collective-permute-done.2.refs_8_), channel_id=1, source_target_pairs={{0,15},{1,0},{2,1},{3,2},{4,3},{5,4},{6,5},{7,6},{8,7},{9,8},{10,9... | collective-permute-start | bytes 1572872 | tf_op jit(solution)/shard_map/ppermute | solution.py:239
  36.1 3.2 %fusion.refs_12_ = f32[8,256,256]{2,1,0:T(8,128)} fusion(f32[256,256,1]{1,0,2:T(8,128)S(1)} %copy-done.26, f32[256,8,256]{2,0,1:T(8,128)S(1)} %fusion.2), kind=kOutput, calls=%fused_computation | convolution fusion | flops 1610612736 | bytes 4456448 | tf_op jit(solution)/shard_map/sjk,lk->sjl/dot_general | solution.py:365
  39.3 9.3 %collective-permute-done.3.refs_9_ = f32[2,2,256,128]{3,2,1,0:T(8,128)S(1)} collective-permute-done((f32[2,2,256,128]{3,2,1,0:T(8,128)S(1)}, f32[2,2,256,128]{3,2,1,0:T(8,128)S(1)}, u32[]{:S(2)}, u32[]{:S(2)}) %collective-permute-start.3) | collective-permute-done | bytes 524320 | tf_op jit(solution)/shard_map/ppermute | solution.py:239
  48.6 2.0 collective-permute-done.4.refs_10_
  51.4 16.3 %windows.2 = (f32[2,2,256,128]{3,2,1,0:T(8,128)}, f32[2,2,256,128]{3,2,1,0:T(8,128)}, f32[2,2,256,128]{3,2,1,0:T(8,128)}, f32[2,2,256,128]{3,2,1,0:T(8,128)}, f3...) custom-call(s32[2,8]{1,0:T(2,128)S(1)} %bitcast.38, ...), custom_call_target="tpu_custom_call" | custom-call | tf_op jit(solution)/shard_map/windows/pallas_call | solution.py:225
  68.1 12.2 %all-to-all-start = ((f32[128,8,128]{2,1,0:T(8,128)}), f32[128,8,128]{2,1,0:T(8,128)}, u32[]{:S(2)}, u32[]{:S(2)}) async-start(f32[128,8,128]{2,1,0:T(8,128)} %bitcast.16), calls=%async_computation | async-start | bytes 1048576 | tf_op jit(solution)/shard_map/all_to_all | solution.py:333
  81.9 4.4 %collective-permute-start.12 = (f32[2,2,256,128]{3,2,1,0:T(8,128)}, f32[2,2,256,128]{3,2,1,0:T(8,128)}, u32[]{:S(2)}, u32[]{:S(2)}) collective-permute-start(f32[2,2,256,128]{3,2,1,0:T(8,128)} %get-tuple-element.46), channel_id=1, source_target_pairs={{0,112},{16,0},{32,16},{48,32},{64,48},{80,64},{96,80},{112,96},{1... | collective-permute-start | bytes 1572872 | tf_op jit(solution)/shard_map/ppermute | solution.py:239
  86.2 2.1 multiply_subtract_fusion.3.refs_6_.refs_3_
  88.3 2.1 add.30
  92.3 5.1 %collective-permute-start.8 = (f32[2,2,256,128]{3,2,1,0:T(8,128)}, f32[2,2,256,128]{3,2,1,0:T(8,128)}, u32[]{:S(2)}, u32[]{:S(2)}) collective-permute-start(f32[2,2,256,128]{3,2,1,0:T(8,128)} %add.29), channel_id=1, source_target_pairs={{0,112},{16,0},{32,16},{48,32},{64,48},{80,64},{96,80},{112,96},{1... | collective-permute-start | bytes 1572872 | tf_op jit(solution)/shard_map/ppermute | solution.py:239
  97.4 2.6 %all-to-all-done = f32[128,8,128]{2,1,0:T(8,128)} async-done(((f32[128,8,128]{2,1,0:T(8,128)}), f32[128,8,128]{2,1,0:T(8,128)}, u32[]{:S(2)}, u32[]{:S(2)}) %all-to-all-start) | async-done | bytes 524320 | tf_op jit(solution)/shard_map/all_to_all | solution.py:333
  102.0 5.9 %all-to-all-start.1 = ((f32[128,8,128]{2,1,0:T(8,128)}), f32[128,8,128]{2,1,0:T(8,128)}, u32[]{:S(2)}, u32[]{:S(2)}) async-start(f32[128,8,128]{2,1,0:T(8,128)} %broadcast_in_dim.4), calls=%async_computation.1 | async-start | bytes 1048576 | tf_op jit(solution)/shard_map/all_to_all | solution.py:338
  111.4 1.9 multiply_subtract_fusion.4.refs_3_.refs_1_
  113.4 2.0 multiply_subtract_fusion.2.refs_9_
  115.3 9.0 %collective-permute-done.10.refs_7_ = f32[2,2,256,128]{3,2,1,0:T(8,128)S(1)} collective-permute-done((f32[2,2,256,128]{3,2,1,0:T(8,128)S(1)}, f32[2,2,256,128]{3,2,1,0:T(8,128)S(1)}, u32[]{:S(2)}, u32[]{:S(2)}) %collective-permute-start.10) | collective-permute-done | bytes 524320 | tf_op jit(solution)/shard_map/ppermute | solution.py:239
  124.3 5.0 %collective-permute-done.7 = f32[2,2,256,128]{3,2,1,0:T(8,128)} collective-permute-done((f32[2,2,256,128]{3,2,1,0:T(8,128)}, f32[2,2,256,128]{3,2,1,0:T(8,128)}, u32[]{:S(2)}, u32[]{:S(2)}) %collective-permute-start.7) | collective-permute-done | bytes 524320 | tf_op jit(solution)/shard_map/ppermute | solution.py:239
  130.7 2.3 %multiply_subtract_fusion.refs_8_ = f32[2,2,256,128]{3,2,1,0:T(8,128)} fusion(f32[2,2,256,128]{3,2,1,0:T(8,128)S(1)} %copy-done.23, f32[2,2,256,128]{3,2,1,0:T(8,128)} %add.30, f32[2,2,256,128]{3,2,1,0:T(8,128)} %collective-permute-done.8), kind=kLoop, calls=%fused_computation.9 | loop fusion | flops 393216 | bytes 2097152 | tf_op jit(solution)/shard_map/sub | solution.py:368
  135.4 6.2 %collective-permute-done.13.refs_4_ = f32[2,2,256,128]{3,2,1,0:T(8,128)} collective-permute-done((f32[2,2,256,128]{3,2,1,0:T(8,128)S(1)}, f32[2,2,256,128]{3,2,1,0:T(8,128)}, u32[]{:S(2)}, u32[]{:S(2)}) %collective-permute-start.13) | collective-permute-done | bytes 524320 | tf_op jit(solution)/shard_map/ppermute | solution.py:239
  141.7 5.6 %collective-permute-done.14.refs_10_ = f32[2,2,256,128]{3,2,1,0:T(8,128)} collective-permute-done((f32[2,2,256,128]{3,2,1,0:T(8,128)}, f32[2,2,256,128]{3,2,1,0:T(8,128)}, u32[]{:S(2)}, u32[]{:S(2)}) %collective-permute-start.14) | collective-permute-done | bytes 524320 | tf_op jit(solution)/shard_map/ppermute | solution.py:239
  147.3 16.3 %windows.3 = (f32[2,2,256,128]{3,2,1,0:T(8,128)}, f32[2,2,256,128]{3,2,1,0:T(8,128)}, f32[2,2,256,128]{3,2,1,0:T(8,128)}, f32[2,2,256,128]{3,2,1,0:T(8,128)}, f3...) custom-call(s32[2,8]{1,0:T(2,128)S(1)} %bitcast.39, ...), custom_call_target="tpu_custom_call" | custom-call | tf_op jit(solution)/shard_map/windows/pallas_call | solution.py:225
  163.8 9.5 %all-to-all-start.2 = ((f32[128,8,128]{2,1,0:T(8,128)}), f32[128,8,128]{2,1,0:T(8,128)S(1)}, u32[]{:S(2)}, u32[]{:S(2)}) async-start(f32[128,8,128]{2,1,0:T(8,128)} %bitcast.18), calls=%async_computation.2 | async-start | bytes 1048576 | tf_op jit(solution)/shard_map/all_to_all | solution.py:333
  175.1 2.1 add.36
  178.5 2.8 %collective-permute-done.17.near = f32[2,2,256,128]{3,2,1,0:T(8,128)} collective-permute-done((f32[2,2,256,128]{3,2,1,0:T(8,128)}, f32[2,2,256,128]{3,2,1,0:T(8,128)}, u32[]{:S(2)}, u32[]{:S(2)}) %collective-permute-start.17) | collective-permute-done | bytes 524320 | tf_op jit(solution)/shard_map/ppermute | solution.py:247
  183.3 3.9 %all-to-all-done.2 = f32[128,8,128]{2,1,0:T(8,128)S(1)} async-done(((f32[128,8,128]{2,1,0:T(8,128)}), f32[128,8,128]{2,1,0:T(8,128)S(1)}, u32[]{:S(2)}, u32[]{:S(2)}) %all-to-all-start.2) | async-done | bytes 524320 | tf_op jit(solution)/shard_map/all_to_all | solution.py:333
  188.1 6.1 %all-to-all-start.3 = ((f32[128,8,128]{2,1,0:T(8,128)}), f32[128,8,128]{2,1,0:T(8,128)S(1)}, u32[]{:S(2)}, u32[]{:S(2)}) async-start(f32[128,8,128]{2,1,0:T(8,128)} %broadcast_in_dim.5), calls=%async_computation.3 | async-start | bytes 1048576 | tf_op jit(solution)/shard_map/all_to_all | solution.py:338
  195.9 4.2 %most.1.whole_in = f32[2,512,512]{2,1,0:T(8,128)} custom-call(f32[2,2,256,128]{3,2,1,0:T(8,128)} %copy-done.8, f32[2,2,256,128]{3,2,1,0:T(8,128)} %multiply_subtract_fusion.4.refs_3_.refs_1_, f32[2,2,256,128]{3,2,1,0:T(8,128)} %copy-done.7, f32[2,2,256,128]{3,2,1,0:T(8,128)} %multiply_subtract_fusion.3.refs_6_.refs_3_, ...), custom_call_target="tpu_custom_call" | custom-call | tf_op jit(solution)/shard_map/most/pallas_call | solution.py:301
  200.2 13.8 %all-to-all-done.3 = f32[128,8,128]{2,1,0:T(8,128)S(1)} async-done(((f32[128,8,128]{2,1,0:T(8,128)}), f32[128,8,128]{2,1,0:T(8,128)S(1)}, u32[]{:S(2)}, u32[]{:S(2)}) %all-to-all-start.3) | async-done | bytes 524320 | tf_op jit(solution)/shard_map/all_to_all | solution.py:338
  214.8 4.0 %rest.1 = (f32[2,512,512]{2,1,0:T(8,128)}, f32[2,256,256]{2,1,0:T(8,128)}) custom-call(s32[1]{0:T(128)} %bitcast.wrapped, f32[2,2,256,128]{3,2,1,0:T(8,128)} %collective-permute-done.16.above0, f32[2,2,256,128]{3,2,1,0:T(8,128)} %collective-permute-done.17.near, f32[2,2,256,128]{3,2,1,0:T(8,128)} %collective-permute-done.18.far, ...), custom_call_target="tpu_custom_call", output_to_operand_aliasing={{0}: (6, {})} | custom-call | tf_op jit(solution)/shard_map/rest/pallas_call | solution.py:315
  (117 shorter events, 26.9 us)
Async XLA Ops:
  2.5 32.6 %copy-start.13 = (f32[1,2,256,128]{3,2,1,0:T(8,128)}, f32[1,2,256,128]{3,2,1,0:T(8,128)S(1)}, u32[]{:S(2)}) copy-start(f32[1,2,256,128]{3,2,1,0:T(8,128)S(1)} %get-tuple-element.74) | copy-start | bytes 786436
  2.5 32.6 %copy-start.14 = (f32[1,2,256,128]{3,2,1,0:T(8,128)}, f32[1,2,256,128]{3,2,1,0:T(8,128)S(1)}, u32[]{:S(2)}) copy-start(f32[1,2,256,128]{3,2,1,0:T(8,128)S(1)} %get-tuple-element.81) | copy-start | bytes 786436
  2.6 29.1 %collective-permute-start.2 = (f32[2,2,256,128]{3,2,1,0:T(8,128)S(1)}, f32[2,2,256,128]{3,2,1,0:T(8,128)S(1)}, u32[]{:S(2)}, u32[]{:S(2)}) collective-permute-start(f32[2,2,256,128]{3,2,1,0:T(8,128)S(1)} %pad_maximum_fusion.refs_2_), channel_id=1, source_target_pairs={{0,112},{16,0},{32,16},{48,32},{64,48},{80,64},{96,80},{112,96},{1... | collective-permute-start | bytes 1572872 | tf_op jit(solution)/shard_map/ppermute | solution.py:239
  9.9 38.7 %collective-permute-start = (f32[2,2,256,128]{3,2,1,0:T(8,128)S(1)}, f32[2,2,256,128]{3,2,1,0:T(8,128)S(1)}, u32[]{:S(2)}, u32[]{:S(2)}) collective-permute-start(f32[2,2,256,128]{3,2,1,0:T(8,128)S(1)} %pad_maximum_fusion.refs_2_), channel_id=1, source_target_pairs={{0,15},{1,0},{2,1},{3,2},{4,3},{5,4},{6,5},{7,6},{8,7},{9,8},{10,9... | collective-permute-start | bytes 1572872 | tf_op jit(solution)/shard_map/ppermute | solution.py:239
  10.9 37.7 %collective-permute-start.3 = (f32[2,2,256,128]{3,2,1,0:T(8,128)S(1)}, f32[2,2,256,128]{3,2,1,0:T(8,128)S(1)}, u32[]{:S(2)}, u32[]{:S(2)}) collective-permute-start(f32[2,2,256,128]{3,2,1,0:T(8,128)S(1)} %pad_maximum_fusion.1.refs_3_), channel_id=1, source_target_pairs={{0,112},{16,0},{32,16},{48,32},{64,48},{80,64},{96,80},{112,96},{1... | collective-permute-start | bytes 1572872 | tf_op jit(solution)/shard_map/ppermute | solution.py:239
  11.2 23.3 %copy-start.33 = (f32[2,256,256]{2,1,0:T(8,128)S(1)}, f32[2,256,256]{2,1,0:T(8,128)}, u32[]{:S(2)}) copy-start(f32[2,256,256]{2,1,0:T(8,128)} %param.12) | copy-start | bytes 1572868
  11.2 37.4 %collective-permute-start.1 = (f32[2,2,256,128]{3,2,1,0:T(8,128)S(1)}, f32[2,2,256,128]{3,2,1,0:T(8,128)S(1)}, u32[]{:S(2)}, u32[]{:S(2)}) collective-permute-start(f32[2,2,256,128]{3,2,1,0:T(8,128)S(1)} %pad_maximum_fusion.2.refs_5_), channel_id=1, source_target_pairs={{0,15},{1,0},{2,1},{3,2},{4,3},{5,4},{6,5},{7,6},{8,7},{9,8},{10,9... | collective-permute-start | bytes 1572872 | tf_op jit(solution)/shard_map/ppermute | solution.py:239
  31.7 18.8 %collective-permute-start.4 = (f32[2,2,256,128]{3,2,1,0:T(8,128)S(1)}, f32[2,2,256,128]{3,2,1,0:T(8,128)S(1)}, u32[]{:S(2)}, u32[]{:S(2)}) collective-permute-start(f32[2,2,256,128]{3,2,1,0:T(8,128)S(1)} %collective-permute-done.2.refs_8_), channel_id=1, source_target_pairs={{0,15},{1,0},{2,1},{3,2},{4,3},{5,4},{6,5},{7,6},{8,7},{9,8},{10,9... | collective-permute-start | bytes 1572872 | tf_op jit(solution)/shard_map/ppermute | solution.py:239
  36.1 15.3 %copy-start.6 = (s32[1,1,2,8]{3,2,1,0:T(2,128)S(1)}, s32[1,1,2,8]{3,2,1,0:T(2,128)}, u32[]{:S(2)}) copy-start(s32[1,1,2,8]{3,2,1,0:T(2,128)} %param.13) | copy-start | bytes 196
  67.7 20.6 %collective-permute-start.6 = (f32[2,2,256,128]{3,2,1,0:T(8,128)}, f32[2,2,256,128]{3,2,1,0:T(8,128)}, u32[]{:S(2)}, u32[]{:S(2)}) collective-permute-start(f32[2,2,256,128]{3,2,1,0:T(8,128)} %get-tuple-element.41), channel_id=1, source_target_pairs={{0,1},{1,2},{2,3},{3,4},{4,5},{5,6},{6,7},{7,8},{8,9},{9,10},{10,1... | collective-permute-start | bytes 1572872 | tf_op jit(solution)/shard_map/ppermute | solution.py:239
  67.7 22.6 %collective-permute-start.5 = (f32[2,2,256,128]{3,2,1,0:T(8,128)}, f32[2,2,256,128]{3,2,1,0:T(8,128)}, u32[]{:S(2)}, u32[]{:S(2)}) collective-permute-start(f32[2,2,256,128]{3,2,1,0:T(8,128)} %get-tuple-element.39), channel_id=1, source_target_pairs={{0,1},{1,2},{2,3},{3,4},{4,5},{5,6},{6,7},{7,8},{8,9},{9,10},{10,1... | collective-permute-start | bytes 1572872 | tf_op jit(solution)/shard_map/ppermute | solution.py:239
  67.8 40.1 %collective-permute-start.9 = (f32[2,2,256,128]{3,2,1,0:T(8,128)}, f32[2,2,256,128]{3,2,1,0:T(8,128)}, u32[]{:S(2)}, u32[]{:S(2)}) collective-permute-start(f32[2,2,256,128]{3,2,1,0:T(8,128)} %get-tuple-element.45), channel_id=1, source_target_pairs={{0,1},{1,2},{2,3},{3,4},{4,5},{5,6},{6,7},{7,8},{8,9},{9,10},{10,1... | collective-permute-start | bytes 1572872 | tf_op jit(solution)/shard_map/ppermute | solution.py:239
  68.1 31.9 %all-to-all-start = ((f32[128,8,128]{2,1,0:T(8,128)}), f32[128,8,128]{2,1,0:T(8,128)}, u32[]{:S(2)}, u32[]{:S(2)}) async-start(f32[128,8,128]{2,1,0:T(8,128)} %bitcast.16), calls=%async_computation | async-start | bytes 1048576 | tf_op jit(solution)/shard_map/all_to_all | solution.py:333
  80.3 31.1 %collective-permute-start.11 = (f32[2,2,256,128]{3,2,1,0:T(8,128)}, f32[2,2,256,128]{3,2,1,0:T(8,128)}, u32[]{:S(2)}, u32[]{:S(2)}) collective-permute-start(f32[2,2,256,128]{3,2,1,0:T(8,128)} %get-tuple-element.47), channel_id=1, source_target_pairs={{0,16},{16,32},{32,48},{48,64},{64,80},{80,96},{96,112},{112,0},{1... | collective-permute-start | bytes 1572872 | tf_op jit(solution)/shard_map/ppermute | solution.py:239
  81.9 31.5 %collective-permute-start.12 = (f32[2,2,256,128]{3,2,1,0:T(8,128)}, f32[2,2,256,128]{3,2,1,0:T(8,128)}, u32[]{:S(2)}, u32[]{:S(2)}) collective-permute-start(f32[2,2,256,128]{3,2,1,0:T(8,128)} %get-tuple-element.46), channel_id=1, source_target_pairs={{0,112},{16,0},{32,16},{48,32},{64,48},{80,64},{96,80},{112,96},{1... | collective-permute-start | bytes 1572872 | tf_op jit(solution)/shard_map/ppermute | solution.py:239
  92.3 37.1 %collective-permute-start.7 = (f32[2,2,256,128]{3,2,1,0:T(8,128)}, f32[2,2,256,128]{3,2,1,0:T(8,128)}, u32[]{:S(2)}, u32[]{:S(2)}) collective-permute-start(f32[2,2,256,128]{3,2,1,0:T(8,128)} %add.30), channel_id=1, source_target_pairs={{0,16},{16,32},{32,48},{48,64},{64,80},{80,96},{96,112},{112,0},{1... | collective-permute-start | bytes 1572872 | tf_op jit(solution)/shard_map/ppermute | solution.py:239
  92.3 37.1 %collective-permute-start.8 = (f32[2,2,256,128]{3,2,1,0:T(8,128)}, f32[2,2,256,128]{3,2,1,0:T(8,128)}, u32[]{:S(2)}, u32[]{:S(2)}) collective-permute-start(f32[2,2,256,128]{3,2,1,0:T(8,128)} %add.29), channel_id=1, source_target_pairs={{0,112},{16,0},{32,16},{48,32},{64,48},{80,64},{96,80},{112,96},{1... | collective-permute-start | bytes 1572872 | tf_op jit(solution)/shard_map/ppermute | solution.py:239
  102.0 31.3 %all-to-all-start.1 = ((f32[128,8,128]{2,1,0:T(8,128)}), f32[128,8,128]{2,1,0:T(8,128)}, u32[]{:S(2)}, u32[]{:S(2)}) async-start(f32[128,8,128]{2,1,0:T(8,128)} %broadcast_in_dim.4), calls=%async_computation.1 | async-start | bytes 1048576 | tf_op jit(solution)/shard_map/all_to_all | solution.py:338
  109.5 19.9 %copy-start.10 = (f32[1,2,256,128]{3,2,1,0:T(8,128)S(1)}, f32[1,2,256,128]{3,2,1,0:T(8,128)}, u32[]{:S(2)}) copy-start(f32[1,2,256,128]{3,2,1,0:T(8,128)} %copy-done.9) | copy-start | bytes 786436
  109.5 14.9 %collective-permute-start.10 = (f32[2,2,256,128]{3,2,1,0:T(8,128)S(1)}, f32[2,2,256,128]{3,2,1,0:T(8,128)S(1)}, u32[]{:S(2)}, u32[]{:S(2)}) collective-permute-start(f32[2,2,256,128]{3,2,1,0:T(8,128)S(1)} %multiply_subtract_fusion.5.refs_5_.refs_2_), channel_id=1, source_target_pairs={{0,15},{1,0},{2,1},{3,2},{4,3},{5,4},{6,5},{7,6},{8,7},{9,8},{10,9... | collective-permute-start | bytes 1572872 | tf_op jit(solution)/shard_map/ppermute | solution.py:239
  113.3 17.3 %copy-start.23 = (f32[2,2,256,128]{3,2,1,0:T(8,128)S(1)}, f32[2,2,256,128]{3,2,1,0:T(8,128)}, u32[]{:S(2)}) copy-start(f32[2,2,256,128]{3,2,1,0:T(8,128)} %copy-done.22) | copy-start | bytes 1572868
  132.9 8.7 %collective-permute-start.13 = (f32[2,2,256,128]{3,2,1,0:T(8,128)S(1)}, f32[2,2,256,128]{3,2,1,0:T(8,128)}, u32[]{:S(2)}, u32[]{:S(2)}) collective-permute-start(f32[2,2,256,128]{3,2,1,0:T(8,128)S(1)} %multiply_subtract_fusion.1.refs_2_.refs_0_), channel_id=1, source_target_pairs={{0,15},{1,0},{2,1},{3,2},{4,3},{5,4},{6,5},{7,6},{8,7},{9,8},{10,9... | collective-permute-start | bytes 1572872 | tf_op jit(solution)/shard_map/ppermute | solution.py:239
  133.0 14.3 %collective-permute-start.14 = (f32[2,2,256,128]{3,2,1,0:T(8,128)}, f32[2,2,256,128]{3,2,1,0:T(8,128)}, u32[]{:S(2)}, u32[]{:S(2)}) collective-permute-start(f32[2,2,256,128]{3,2,1,0:T(8,128)} %multiply_subtract_fusion.refs_8_), channel_id=1, source_target_pairs={{0,15},{1,0},{2,1},{3,2},{4,3},{5,4},{6,5},{7,6},{8,7},{9,8},{10,9... | collective-permute-start | bytes 1572872 | tf_op jit(solution)/shard_map/ppermute | solution.py:239
  135.4 28.2 %copy-start.1 = (f32[2,2,256,128]{3,2,1,0:T(8,128)}, f32[2,2,256,128]{3,2,1,0:T(8,128)S(1)}, u32[]{:S(2)}) copy-start(f32[2,2,256,128]{3,2,1,0:T(8,128)S(1)} %fusion.4.refs_11_.probe) | copy-start | bytes 1572868
  163.6 11.5 %collective-permute-start.15 = (f32[2,2,256,128]{3,2,1,0:T(8,128)}, f32[2,2,256,128]{3,2,1,0:T(8,128)}, u32[]{:S(2)}, u32[]{:S(2)}) collective-permute-start(f32[2,2,256,128]{3,2,1,0:T(8,128)} %get-tuple-element.60), channel_id=1, source_target_pairs={{0,1},{1,2},{2,3},{3,4},{4,5},{5,6},{6,7},{7,8},{8,9},{9,10},{10,1... | collective-permute-start | bytes 1572872 | tf_op jit(solution)/shard_map/ppermute | solution.py:239
  163.7 17.7 %collective-permute-start.17 = (f32[2,2,256,128]{3,2,1,0:T(8,128)}, f32[2,2,256,128]{3,2,1,0:T(8,128)}, u32[]{:S(2)}, u32[]{:S(2)}) collective-permute-start(f32[2,2,256,128]{3,2,1,0:T(8,128)} %get-tuple-element.61), channel_id=1, source_target_pairs={{0,16},{16,32},{32,48},{48,0},{64,80},{80,96},{96,112},{112,64},{1... | collective-permute-start | bytes 1572872 | tf_op jit(solution)/shard_map/ppermute | solution.py:247
  163.8 23.4 %all-to-all-start.2 = ((f32[128,8,128]{2,1,0:T(8,128)}), f32[128,8,128]{2,1,0:T(8,128)S(1)}, u32[]{:S(2)}, u32[]{:S(2)}) async-start(f32[128,8,128]{2,1,0:T(8,128)} %bitcast.18), calls=%async_computation.2 | async-start | bytes 1048576 | tf_op jit(solution)/shard_map/all_to_all | solution.py:333
  173.3 21.0 %collective-permute-start.19 = (f32[2,2,256,128]{3,2,1,0:T(8,128)}, f32[2,2,256,128]{3,2,1,0:T(8,128)S(1)}, u32[]{:S(2)}, u32[]{:S(2)}) collective-permute-start(f32[2,2,256,128]{3,2,1,0:T(8,128)} %get-tuple-element.68), channel_id=1, source_target_pairs={{0,1},{1,2},{2,3},{3,4},{4,5},{5,6},{6,7},{7,8},{8,9},{9,10},{10,1... | collective-permute-start | bytes 1572872 | tf_op jit(solution)/shard_map/ppermute | solution.py:239
  175.0 21.0 %collective-permute-start.20 = (f32[2,2,256,128]{3,2,1,0:T(8,128)}, f32[2,2,256,128]{3,2,1,0:T(8,128)}, u32[]{:S(2)}, u32[]{:S(2)}) collective-permute-start(f32[2,2,256,128]{3,2,1,0:T(8,128)} %get-tuple-element.69), channel_id=1, source_target_pairs={{0,1},{1,2},{2,3},{3,4},{4,5},{5,6},{6,7},{7,8},{8,9},{9,10},{10,1... | collective-permute-start | bytes 1572872 | tf_op jit(solution)/shard_map/ppermute | solution.py:239
  177.2 36.8 %collective-permute-start.16 = (f32[2,2,256,128]{3,2,1,0:T(8,128)}, f32[2,2,256,128]{3,2,1,0:T(8,128)}, u32[]{:S(2)}, u32[]{:S(2)}) collective-permute-start(f32[2,2,256,128]{3,2,1,0:T(8,128)} %add.36), channel_id=1, source_target_pairs={{0,16},{16,32},{32,48},{48,64},{64,80},{80,96},{96,112},{112,0},{1... | collective-permute-start | bytes 1572872 | tf_op jit(solution)/shard_map/ppermute | solution.py:239
  181.4 32.6 %collective-permute-start.18 = (f32[2,2,256,128]{3,2,1,0:T(8,128)}, f32[2,2,256,128]{3,2,1,0:T(8,128)}, u32[]{:S(2)}, u32[]{:S(2)}) collective-permute-start(f32[2,2,256,128]{3,2,1,0:T(8,128)} %collective-permute-done.17.near), channel_id=1, source_target_pairs={{0,64},{64,0},{1,65},{65,1},{2,66},{66,2},{3,67},{67,3},{4,68},{68... | collective-permute-start | bytes 1572872 | tf_op jit(solution)/shard_map/ppermute | solution.py:253
  188.1 25.8 %all-to-all-start.3 = ((f32[128,8,128]{2,1,0:T(8,128)}), f32[128,8,128]{2,1,0:T(8,128)S(1)}, u32[]{:S(2)}, u32[]{:S(2)}) async-start(f32[128,8,128]{2,1,0:T(8,128)} %broadcast_in_dim.5), calls=%async_computation.3 | async-start | bytes 1048576 | tf_op jit(solution)/shard_map/all_to_all | solution.py:338
  (29 other events, 210.6 us)

commit v2 on v1

--- a/solution.py
+++ b/solution.py
@@ -171,15 +171,18 @@
 def windows_kernel(*refs):
     offs, count = refs[:2]
     blocks, (probe, pats) = refs[2:11], refs[11:13]
-    tables, grads, gprobe = refs[13:17], refs[17:26], refs[26]
-    ext, gacc, pats_here, *scratch, sem_in, sem_out, sem_pats = refs[27:]
+    tables, grads, gprobe_out = refs[13:17], refs[17:26], refs[26]
+    ext, gacc, pats_here, probe_here, gprobe, *scratch = refs[27:]
+    *scratch, table0, table1, table2, table3, sem_in, sem_out = scratch
+    tables_here = (table0, table1, table2, table3)
 
     def place(buffer, k):
         i, j = divmod(k, 3)
         return buffer.at[2 * j:2 * j + 2, :, i * M:(i + 1) * M, :]
 
     arrivals = [pltpu.make_async_copy(blocks[k], place(ext, k), sem_in.at[k]) for k in range(9)]
-    arrivals.append(pltpu.make_async_copy(pats, pats_here, sem_pats))
+    others = ((pats, pats_here), (probe, probe_here), *zip(tables, tables_here))
+    arrivals += [pltpu.make_async_copy(there, here, sem_in.at[9 + k]) for k, (there, here) in enumerate(others)]
     for copy in arrivals:
         copy.start()
 
@@ -197,13 +200,14 @@
         for n in range(4):
             live = None if n == 0 else jnp.where(4 * k + n < count[0], 1.0, 0.0)
             own = [buffer.at[n] for buffer in scratch]
-            turns.append(window(4 * k + n, live, offs, probe, pats_here, tables, ext, gacc, gprobe, own))
+            turns.append(window(4 * k + n, live, offs, probe_here, pats_here, tables_here, ext, gacc, gprobe, own))
         for _ in itertools.zip_longest(*turns):
             pass
         return carry
 
     lax.fori_loop(0, (count[0] + 3) // 4, pair, 0)
     departures = [pltpu.make_async_copy(place(gacc, k), grads[k], sem_out.at[k]) for k in range(9)]
+    departures.append(pltpu.make_async_copy(gprobe, gprobe_out, sem_out.at[9]))
     for copy in departures:
         copy.start()
     for copy in departures:
@@ -216,7 +220,6 @@
 
 def windows(offs, count, blocks, probe, pats, tables):
     smem = pl.BlockSpec(memory_space=pltpu.SMEM)
-    vmem = pl.BlockSpec(memory_space=pltpu.VMEM)
     where = pl.BlockSpec(memory_space=pl.ANY)
     block = jax.ShapeDtypeStruct((2, 2, M, LANES), F32)
     halves16 = pltpu.VMEM((4, 2, M, M), BF16)
@@ -224,14 +227,15 @@
     extended = pltpu.VMEM((6, 2, 3 * M, LANES), F32)
     return pl.pallas_call(
         windows_kernel,
-        out_shape=[pltpu.HBM(block.shape, F32)] * 9 + [block],
-        in_specs=[smem, smem] + [where] * 9 + [vmem, where] + [vmem] * 4,
-        out_specs=[where] * 9 + [vmem],
-        scratch_shapes=[extended, extended, pltpu.VMEM(pats.shape, F32)] + [halves16] * 4 + [whole32] * 2
-        + [pltpu.SemaphoreType.DMA((9,)), pltpu.SemaphoreType.DMA((9,)), pltpu.SemaphoreType.DMA],
+        out_shape=[pltpu.HBM(block.shape, F32)] * 10,
+        in_specs=[smem, smem] + [where] * 15,
+        out_specs=[where] * 10,
+        scratch_shapes=[extended, extended] + [pltpu.VMEM(x.shape, F32) for x in (pats, probe, block)]
+        + [halves16] * 4 + [whole32] * 2 + [pltpu.VMEM(tables[0].shape, BF16)] * 4
+        + [pltpu.SemaphoreType.DMA((15,)), pltpu.SemaphoreType.DMA((10,))],
         compiler_params=pltpu.CompilerParams(vmem_limit_bytes=34 * 1024 * 1024),
         name="windows",
-    )(offs, count, *in_hbm(blocks), probe, *in_hbm([pats]), *tables)
+    )(offs, count, *in_hbm([*blocks, probe, pats]), *tables)
 
 
 def shift(block, axis, distance):
@@ -273,12 +277,12 @@
                 whole[part, pl.ds(i * M, M), lanes] = here[k, tile, part] - OBJECT_RATE * total
 
 
-def rest_kernel(pstep, wrapped, above0, near, far, probe, summed, whole_in, whole, probe_out, top, here, sem, sem_top):
+def rest_kernel(wrapped, above0, near, far, whole_in, whole, top, here, sem, sem_top):
     del whole_in
     view = whole.at[:, pl.ds(0, M), :]
     arrive = pltpu.make_async_copy(view, top, sem_top.at[0])
     arrive.start()
-    fetch((above0, near, far, probe, summed), here, sem)
+    fetch((above0, near, far), here, sem)
     arrive.wait()
     from_far = wrapped[0] == 1
     for tile in range(2):
@@ -289,11 +293,13 @@
             top[part, :, beside] = top[part, :, beside] - OBJECT_RATE * above1
     leave = pltpu.make_async_copy(top, view, sem_top.at[1])
     leave.start()
+    leave.wait()
+
+
+def probe_kernel(pstep, probe, summed, out):
     for tile in range(2):
         for part in range(2):
-            lanes = pl.ds(tile * LANES, LANES)
-            probe_out[part, :, lanes] = here[3, tile, part] - pstep * here[4, tile, part]
-    leave.wait()
+            out[part, :, tile * LANES:(tile + 1) * LANES] = probe[tile, part] - pstep * summed[tile, part]
 
 
 def most(own, grads):
@@ -309,24 +315,35 @@
     )(*in_hbm([*own, *grads]))
 
 
-def rest(pstep, wrapped, moved, probe, summed, whole):
-    smem, vmem = pl.BlockSpec(memory_space=pltpu.SMEM), pl.BlockSpec(memory_space=pltpu.VMEM)
+def rest(wrapped, moved, whole):
     where = pl.BlockSpec(memory_space=pl.ANY)
     return pl.pallas_call(
-        functools.partial(rest_kernel, pstep),
-        out_shape=(pltpu.HBM(whole.shape, F32), jax.ShapeDtypeStruct((2, M, M), F32)),
-        in_specs=[smem] + [where] * 6,
-        out_specs=(where, vmem),
+        rest_kernel,
+        out_shape=pltpu.HBM(whole.shape, F32),
+        in_specs=[pl.BlockSpec(memory_space=pltpu.SMEM)] + [where] * 4,
+        out_specs=where,
         scratch_shapes=[
             pltpu.VMEM((2, M, 2 * M), F32),
-            pltpu.VMEM((5, *probe.shape), F32),
-            pltpu.SemaphoreType.DMA((5,)),
+            pltpu.VMEM((3, *moved[0].shape), F32),
+            pltpu.SemaphoreType.DMA((3,)),
             pltpu.SemaphoreType.DMA((2,)),
         ],
-        input_output_aliases={6: 0},
+        input_output_aliases={4: 0},
         compiler_params=pltpu.CompilerParams(vmem_limit_bytes=24 * 1024 * 1024),
         name="rest",
-    )(wrapped, *in_hbm([*moved, probe, summed, whole]))
+    )(wrapped, *in_hbm([*moved, whole]))
+
+
+def last_probe(pstep, probe, summed):
+    vmem = pl.BlockSpec(memory_space=pltpu.VMEM)
+    return pl.pallas_call(
+        functools.partial(probe_kernel, pstep),
+        out_shape=jax.ShapeDtypeStruct((2, M, M), F32),
+        in_specs=[vmem] * 2,
+        out_specs=vmem,
+        compiler_params=pltpu.CompilerParams(vmem_limit_bytes=24 * 1024 * 1024),
+        name="last_probe",
+    )(probe, summed)
 
 
 def deal(x):
@@ -400,8 +417,9 @@
     above0, (far1, wrapped) = shift(g20, "row", 1), cross_y(above1, 1)
     summed = collect(together(terms, g20)[0], probe.shape)
     whole = most((own00, own01, own10, own11), (g00, g01, g10, g11, left0, left1))
-    above0, far1, summed, whole = together(above0, far1, summed, whole)
-    return rest(pstep, wrapped, (above0, above1, far1), probe, summed, whole)
+    whole = rest(wrapped, (above0, above1, far1), whole)
+    summed, whole = together(summed, whole)
+    return whole, last_probe(pstep, probe, summed)
 
 
 def solution(mesh):

time: 219 us -> 217 us (level)
  waiting for transfers between devices: 78.3 us -> 68.5 us
  starting transfers between devices: 65.9 us -> 72.5 us
    all_to_all x2, waiting for transfers between devices: 13.8 us -> 0.01 us  [collect(): lax.all_to_all(spread, ('row', *COL), 0, 0, tiled=True).reshape(shape)]
    ppermute x19, waiting for transfers between devices: 55.1 us -> 65.1 us  [shift(): lax.ppermute(block, axis, [(i, (i + distance) % n) for i in range(n)])]
    ppermute x1, starting transfers between devices: 1.91 us -> 10.3 us  [cross_y(): lax.ppermute(block, 'row', [(i, (i + RING) % n) for i in range(edge, n, R...]
    all_to_all x2, waiting for transfers between devices: 6.47 us -> 2.43 us  [deal(): lax.all_to_all(x.reshape(-1, 8, LANES), ('row', *COL), 0, 0, tiled=True)]
  transfers between devices with their start and end apart: 25 -> 25, of which waited for: 13 -> 10; matrix products, arithmetic and copies ran while one was open for 13% -> 14% of each run, Pallas kernels for 2% -> 3%
where the time goes in v2:
time: 217 us; the launch traced here: 216 us
  starting transfers between devices  72.5 us (33%)
  waiting for transfers between devices  68.5 us (32%)
  Pallas kernels  39.7 us (18%)
  other arithmetic  22.8 us (11%)
  local copies, waits for them, and re-layouts  5.36 us (2%)
  matrix products  5.08 us (2%)
    ppermute x19, waiting for transfers between devices, shift(): lax.ppermute(block, axis, [(i, (i + distance) % n) for i in range(n)])  65.1 us
    pallas_call x2, Pallas kernels, windows(): pl.pallas_call(windows_kernel, out_shape=[pltpu.HBM(block.shape, F32)] *...  31.7 us
    ppermute x19, starting transfers between devices, shift(): lax.ppermute(block, axis, [(i, (i + distance) % n) for i in range(n)])  30.1 us
    all_to_all x2, starting transfers between devices, deal(): lax.all_to_all(x.reshape(-1, 8, LANES), ('row', *COL), 0, 0, tiled=True)  20.8 us
    sub x6, other arithmetic, step(): return x - OBJECT_RATE * sum(grads[1:], grads[0])  11.3 us
    all_to_all x2, starting transfers between devices, collect(): lax.all_to_all(spread, ('row', *COL), 0, 0, tiled=True).reshape(shape)  11.3 us
    ppermute x1, starting transfers between devices, cross_y(): lax.ppermute(block, 'row', [(i, (i + RING) % n) for i in range(edge, n, R...  10.3 us
  transfers between devices with their start and end apart: 25, of which 10 were waited for; matrix products, arithmetic and copies ran while one was open for 14% of the time, Pallas kernels for 3%

profile of v2, /device:TPU:1, one launch (start us, length us, event | category | flops | bytes accessed | tf_op | source)
XLA Modules:
  0.0 215.9 jit_solution(5086986304900269092)
XLA Ops:
  2.6 7.3 %collective-permute-start.2 = (f32[2,2,256,128]{3,2,1,0:T(8,128)S(1)}, f32[2,2,256,128]{3,2,1,0:T(8,128)S(1)}, u32[]{:S(2)}, u32[]{:S(2)}) collective-permute-start(f32[2,2,256,128]{3,2,1,0:T(8,128)S(1)} %pad_maximum_fusion.refs_2_), channel_id=1, source_target_pairs={{0,112},{16,0},{32,16},{48,32},{64,48},{80,64},{96,80},{112,96},{1... | collective-permute-start | bytes 1572872 | tf_op jit(solution)/shard_map/ppermute | solution.py:243
  11.2 3.0 %collective-permute-start.1 = (f32[2,2,256,128]{3,2,1,0:T(8,128)S(1)}, f32[2,2,256,128]{3,2,1,0:T(8,128)S(1)}, u32[]{:S(2)}, u32[]{:S(2)}) collective-permute-start(f32[2,2,256,128]{3,2,1,0:T(8,128)S(1)} %pad_maximum_fusion.2.refs_5_), channel_id=1, source_target_pairs={{0,15},{1,0},{2,1},{3,2},{4,3},{5,4},{6,5},{7,6},{8,7},{9,8},{10,9... | collective-permute-start | bytes 1572872 | tf_op jit(solution)/shard_map/ppermute | solution.py:243
  14.2 1.9 fusion.2
  16.2 15.6 %collective-permute-done.2.refs_8_ = f32[2,2,256,128]{3,2,1,0:T(8,128)S(1)} collective-permute-done((f32[2,2,256,128]{3,2,1,0:T(8,128)S(1)}, f32[2,2,256,128]{3,2,1,0:T(8,128)S(1)}, u32[]{:S(2)}, u32[]{:S(2)}) %collective-permute-start.2) | collective-permute-done | bytes 524320 | tf_op jit(solution)/shard_map/ppermute | solution.py:243
  31.7 2.7 %collective-permute-start.4 = (f32[2,2,256,128]{3,2,1,0:T(8,128)S(1)}, f32[2,2,256,128]{3,2,1,0:T(8,128)S(1)}, u32[]{:S(2)}, u32[]{:S(2)}) collective-permute-start(f32[2,2,256,128]{3,2,1,0:T(8,128)S(1)} %collective-permute-done.2.refs_8_), channel_id=1, source_target_pairs={{0,15},{1,0},{2,1},{3,2},{4,3},{5,4},{6,5},{7,6},{8,7},{9,8},{10,9... | collective-permute-start | bytes 1572872 | tf_op jit(solution)/shard_map/ppermute | solution.py:243
  36.5 3.2 %fusion.refs_12_ = f32[8,256,256]{2,1,0:T(8,128)} fusion(f32[256,256,1]{1,0,2:T(8,128)S(1)} %copy-done.25, f32[256,8,256]{2,0,1:T(8,128)S(1)} %fusion.2), kind=kOutput, calls=%fused_computation | convolution fusion | flops 1610612736 | bytes 4456448 | tf_op jit(solution)/shard_map/sjk,lk->sjl/dot_general | solution.py:382
  39.6 9.0 %collective-permute-done.3.refs_9_ = f32[2,2,256,128]{3,2,1,0:T(8,128)S(1)} collective-permute-done((f32[2,2,256,128]{3,2,1,0:T(8,128)S(1)}, f32[2,2,256,128]{3,2,1,0:T(8,128)S(1)}, u32[]{:S(2)}, u32[]{:S(2)}) %collective-permute-start.3) | collective-permute-done | bytes 524320 | tf_op jit(solution)/shard_map/ppermute | solution.py:243
  48.6 2.0 collective-permute-done.4.refs_10_
  51.4 15.8 %windows.2 = (f32[2,2,256,128]{3,2,1,0:T(8,128)}, f32[2,2,256,128]{3,2,1,0:T(8,128)}, f32[2,2,256,128]{3,2,1,0:T(8,128)}, f32[2,2,256,128]{3,2,1,0:T(8,128)}, f3...) custom-call(s32[2,8]{1,0:T(2,128)S(1)} %bitcast.39, ...), custom_call_target="tpu_custom_call" | custom-call | tf_op jit(solution)/shard_map/windows/pallas_call | solution.py:228
  67.7 11.9 %all-to-all-start = ((f32[128,8,128]{2,1,0:T(8,128)}), f32[128,8,128]{2,1,0:T(8,128)}, u32[]{:S(2)}, u32[]{:S(2)}) async-start(f32[128,8,128]{2,1,0:T(8,128)} %bitcast.42), calls=%async_computation | async-start | bytes 1048576 | tf_op jit(solution)/shard_map/all_to_all | solution.py:350
  81.2 4.4 %collective-permute-start.12 = (f32[2,2,256,128]{3,2,1,0:T(8,128)}, f32[2,2,256,128]{3,2,1,0:T(8,128)}, u32[]{:S(2)}, u32[]{:S(2)}) collective-permute-start(f32[2,2,256,128]{3,2,1,0:T(8,128)} %get-tuple-element.44), channel_id=1, source_target_pairs={{0,112},{16,0},{32,16},{48,32},{64,48},{80,64},{96,80},{112,96},{1... | collective-permute-start | bytes 1572872 | tf_op jit(solution)/shard_map/ppermute | solution.py:243
  85.6 2.1 multiply_subtract_fusion.3.refs_6_.refs_3_
  87.7 2.1 add.29
  89.7 1.9 add.28
  91.7 5.1 %collective-permute-start.8 = (f32[2,2,256,128]{3,2,1,0:T(8,128)}, f32[2,2,256,128]{3,2,1,0:T(8,128)}, u32[]{:S(2)}, u32[]{:S(2)}) collective-permute-start(f32[2,2,256,128]{3,2,1,0:T(8,128)} %add.28), channel_id=1, source_target_pairs={{0,112},{16,0},{32,16},{48,32},{64,48},{80,64},{96,80},{112,96},{1... | collective-permute-start | bytes 1572872 | tf_op jit(solution)/shard_map/ppermute | solution.py:243
  96.7 2.4 %all-to-all-done = f32[128,8,128]{2,1,0:T(8,128)} async-done(((f32[128,8,128]{2,1,0:T(8,128)}), f32[128,8,128]{2,1,0:T(8,128)}, u32[]{:S(2)}, u32[]{:S(2)}) %all-to-all-start) | async-done | bytes 524320 | tf_op jit(solution)/shard_map/all_to_all | solution.py:350
  101.2 5.6 %all-to-all-start.1 = ((f32[128,8,128]{2,1,0:T(8,128)}), f32[128,8,128]{2,1,0:T(8,128)}, u32[]{:S(2)}, u32[]{:S(2)}) async-start(f32[128,8,128]{2,1,0:T(8,128)} %broadcast_in_dim.4), calls=%async_computation.1 | async-start | bytes 1048576 | tf_op jit(solution)/shard_map/all_to_all | solution.py:355
  110.6 1.9 multiply_subtract_fusion.4.refs_3_.refs_1_
  112.6 2.0 multiply_subtract_fusion.2.refs_9_
  114.5 14.8 %collective-permute-done.10.refs_7_ = f32[2,2,256,128]{3,2,1,0:T(8,128)S(1)} collective-permute-done((f32[2,2,256,128]{3,2,1,0:T(8,128)S(1)}, f32[2,2,256,128]{3,2,1,0:T(8,128)S(1)}, u32[]{:S(2)}, u32[]{:S(2)}) %collective-permute-start.10) | collective-permute-done | bytes 524320 | tf_op jit(solution)/shard_map/ppermute | solution.py:243
  130.9 2.3 %multiply_subtract_fusion.refs_8_ = f32[2,2,256,128]{3,2,1,0:T(8,128)} fusion(f32[2,2,256,128]{3,2,1,0:T(8,128)S(1)} %copy-done.22, f32[2,2,256,128]{3,2,1,0:T(8,128)} %add.29, f32[2,2,256,128]{3,2,1,0:T(8,128)} %collective-permute-done.8), kind=kLoop, calls=%fused_computation.9 | loop fusion | flops 393216 | bytes 2097152 | tf_op jit(solution)/shard_map/sub | solution.py:385
  134.3 1.9 fusion.4.refs_11_.probe
  136.1 5.7 %collective-permute-done.13.refs_4_ = f32[2,2,256,128]{3,2,1,0:T(8,128)} collective-permute-done((f32[2,2,256,128]{3,2,1,0:T(8,128)S(1)}, f32[2,2,256,128]{3,2,1,0:T(8,128)}, u32[]{:S(2)}, u32[]{:S(2)}) %collective-permute-start.13) | collective-permute-done | bytes 524320 | tf_op jit(solution)/shard_map/ppermute | solution.py:243
  141.9 5.6 %collective-permute-done.14.refs_10_ = f32[2,2,256,128]{3,2,1,0:T(8,128)} collective-permute-done((f32[2,2,256,128]{3,2,1,0:T(8,128)}, f32[2,2,256,128]{3,2,1,0:T(8,128)}, u32[]{:S(2)}, u32[]{:S(2)}) %collective-permute-start.14) | collective-permute-done | bytes 524320 | tf_op jit(solution)/shard_map/ppermute | solution.py:243
  147.5 15.9 %windows.3 = (f32[2,2,256,128]{3,2,1,0:T(8,128)}, f32[2,2,256,128]{3,2,1,0:T(8,128)}, f32[2,2,256,128]{3,2,1,0:T(8,128)}, f32[2,2,256,128]{3,2,1,0:T(8,128)}, f3...) custom-call(s32[2,8]{1,0:T(2,128)S(1)} %bitcast.40, ...), custom_call_target="tpu_custom_call" | custom-call | tf_op jit(solution)/shard_map/windows/pallas_call | solution.py:228
  163.5 8.9 %all-to-all-start.2 = ((f32[128,8,128]{2,1,0:T(8,128)}), f32[128,8,128]{2,1,0:T(8,128)S(1)}, u32[]{:S(2)}, u32[]{:S(2)}) async-start(f32[128,8,128]{2,1,0:T(8,128)} %bitcast.43), calls=%async_computation.2 | async-start | bytes 1048576 | tf_op jit(solution)/shard_map/all_to_all | solution.py:350
  174.2 2.1 add.35
  178.6 10.3 %collective-permute-start.18 = (f32[2,2,256,128]{3,2,1,0:T(8,128)}, f32[2,2,256,128]{3,2,1,0:T(8,128)}, u32[]{:S(2)}, u32[]{:S(2)}) collective-permute-start(f32[2,2,256,128]{3,2,1,0:T(8,128)} %collective-permute-done.17.near), channel_id=1, source_target_pairs={{0,64},{64,0},{1,65},{65,1},{2,66},{66,2},{3,67},{67,3},{4,68},{68... | collective-permute-start | bytes 1572872 | tf_op jit(solution)/shard_map/ppermute | solution.py:257
  190.0 5.7 %all-to-all-start.3 = ((f32[128,8,128]{2,1,0:T(8,128)}), f32[128,8,128]{2,1,0:T(8,128)S(1)}, u32[]{:S(2)}, u32[]{:S(2)}) async-start(f32[128,8,128]{2,1,0:T(8,128)} %broadcast_in_dim.5), calls=%async_computation.3 | async-start | bytes 1048576 | tf_op jit(solution)/shard_map/all_to_all | solution.py:355
  196.5 4.2 %most.1.whole_in = f32[2,512,512]{2,1,0:T(8,128)} custom-call(f32[2,2,256,128]{3,2,1,0:T(8,128)} %copy-done.8, f32[2,2,256,128]{3,2,1,0:T(8,128)} %multiply_subtract_fusion.4.refs_3_.refs_1_, f32[2,2,256,128]{3,2,1,0:T(8,128)} %copy-done.7, f32[2,2,256,128]{3,2,1,0:T(8,128)} %multiply_subtract_fusion.3.refs_6_.refs_3_, ...), custom_call_target="tpu_custom_call" | custom-call | tf_op jit(solution)/shard_map/most/pallas_call | solution.py:307
  200.7 11.4 %collective-permute-done.16.above0 = f32[2,2,256,128]{3,2,1,0:T(8,128)} collective-permute-done((f32[2,2,256,128]{3,2,1,0:T(8,128)}, f32[2,2,256,128]{3,2,1,0:T(8,128)}, u32[]{:S(2)}, u32[]{:S(2)}) %collective-permute-start.16) | collective-permute-done | bytes 524320 | tf_op jit(solution)/shard_map/ppermute | solution.py:243
  212.1 2.9 %rest.1 = f32[2,512,512]{2,1,0:T(8,128)} custom-call(s32[1]{0:T(128)} %bitcast.19.wrapped, f32[2,2,256,128]{3,2,1,0:T(8,128)} %collective-permute-done.16.above0, f32[2,2,256,128]{3,2,1,0:T(8,128)} %collective-permute-done.17.near, f32[2,2,256,128]{3,2,1,0:T(8,128)} %collective-permute-done.18.far, ...), custom_call_target="tpu_custom_call", output_to_operand_aliasing={{}: (4, {})} | custom-call | tf_op jit(solution)/shard_map/rest/pallas_call | solution.py:320
  (116 shorter events, 22.7 us)
Async XLA Ops:
  2.5 32.6 %copy-start.13 = (f32[1,2,256,128]{3,2,1,0:T(8,128)}, f32[1,2,256,128]{3,2,1,0:T(8,128)S(1)}, u32[]{:S(2)}) copy-start(f32[1,2,256,128]{3,2,1,0:T(8,128)S(1)} %get-tuple-element.70) | copy-start | bytes 786436
  2.5 32.6 %copy-start.14 = (f32[1,2,256,128]{3,2,1,0:T(8,128)}, f32[1,2,256,128]{3,2,1,0:T(8,128)S(1)}, u32[]{:S(2)}) copy-start(f32[1,2,256,128]{3,2,1,0:T(8,128)S(1)} %get-tuple-element.77) | copy-start | bytes 786436
  2.6 29.1 %collective-permute-start.2 = (f32[2,2,256,128]{3,2,1,0:T(8,128)S(1)}, f32[2,2,256,128]{3,2,1,0:T(8,128)S(1)}, u32[]{:S(2)}, u32[]{:S(2)}) collective-permute-start(f32[2,2,256,128]{3,2,1,0:T(8,128)S(1)} %pad_maximum_fusion.refs_2_), channel_id=1, source_target_pairs={{0,112},{16,0},{32,16},{48,32},{64,48},{80,64},{96,80},{112,96},{1... | collective-permute-start | bytes 1572872 | tf_op jit(solution)/shard_map/ppermute | solution.py:243
  9.9 38.7 %collective-permute-start = (f32[2,2,256,128]{3,2,1,0:T(8,128)S(1)}, f32[2,2,256,128]{3,2,1,0:T(8,128)S(1)}, u32[]{:S(2)}, u32[]{:S(2)}) collective-permute-start(f32[2,2,256,128]{3,2,1,0:T(8,128)S(1)} %pad_maximum_fusion.refs_2_), channel_id=1, source_target_pairs={{0,15},{1,0},{2,1},{3,2},{4,3},{5,4},{6,5},{7,6},{8,7},{9,8},{10,9... | collective-permute-start | bytes 1572872 | tf_op jit(solution)/shard_map/ppermute | solution.py:243
  10.9 37.7 %collective-permute-start.3 = (f32[2,2,256,128]{3,2,1,0:T(8,128)S(1)}, f32[2,2,256,128]{3,2,1,0:T(8,128)S(1)}, u32[]{:S(2)}, u32[]{:S(2)}) collective-permute-start(f32[2,2,256,128]{3,2,1,0:T(8,128)S(1)} %pad_maximum_fusion.1.refs_3_), channel_id=1, source_target_pairs={{0,112},{16,0},{32,16},{48,32},{64,48},{80,64},{96,80},{112,96},{1... | collective-permute-start | bytes 1572872 | tf_op jit(solution)/shard_map/ppermute | solution.py:243
  11.2 23.3 %copy-start.32 = (f32[2,256,256]{2,1,0:T(8,128)S(1)}, f32[2,256,256]{2,1,0:T(8,128)}, u32[]{:S(2)}) copy-start(f32[2,256,256]{2,1,0:T(8,128)} %param.12) | copy-start | bytes 1572868
  11.2 37.4 %collective-permute-start.1 = (f32[2,2,256,128]{3,2,1,0:T(8,128)S(1)}, f32[2,2,256,128]{3,2,1,0:T(8,128)S(1)}, u32[]{:S(2)}, u32[]{:S(2)}) collective-permute-start(f32[2,2,256,128]{3,2,1,0:T(8,128)S(1)} %pad_maximum_fusion.2.refs_5_), channel_id=1, source_target_pairs={{0,15},{1,0},{2,1},{3,2},{4,3},{5,4},{6,5},{7,6},{8,7},{9,8},{10,9... | collective-permute-start | bytes 1572872 | tf_op jit(solution)/shard_map/ppermute | solution.py:243
  31.7 18.8 %collective-permute-start.4 = (f32[2,2,256,128]{3,2,1,0:T(8,128)S(1)}, f32[2,2,256,128]{3,2,1,0:T(8,128)S(1)}, u32[]{:S(2)}, u32[]{:S(2)}) collective-permute-start(f32[2,2,256,128]{3,2,1,0:T(8,128)S(1)} %collective-permute-done.2.refs_8_), channel_id=1, source_target_pairs={{0,15},{1,0},{2,1},{3,2},{4,3},{5,4},{6,5},{7,6},{8,7},{9,8},{10,9... | collective-permute-start | bytes 1572872 | tf_op jit(solution)/shard_map/ppermute | solution.py:243
  36.5 15.0 %copy-start.5 = (bf16[256,256]{1,0:T(8,128)(2,1)S(1)}, bf16[256,256]{1,0:T(8,128)(2,1)}, u32[]{:S(2)}) copy-start(bf16[256,256]{1,0:T(8,128)(2,1)} %constant.39.clone.refs_16_) | copy-start | bytes 393220
  36.5 15.0 %copy-start.6 = (s32[1,1,2,8]{3,2,1,0:T(2,128)S(1)}, s32[1,1,2,8]{3,2,1,0:T(2,128)}, u32[]{:S(2)}) copy-start(s32[1,1,2,8]{3,2,1,0:T(2,128)} %param.13) | copy-start | bytes 196
  67.3 20.4 %collective-permute-start.6 = (f32[2,2,256,128]{3,2,1,0:T(8,128)}, f32[2,2,256,128]{3,2,1,0:T(8,128)}, u32[]{:S(2)}, u32[]{:S(2)}) collective-permute-start(f32[2,2,256,128]{3,2,1,0:T(8,128)} %get-tuple-element.39), channel_id=1, source_target_pairs={{0,1},{1,2},{2,3},{3,4},{4,5},{5,6},{6,7},{7,8},{8,9},{9,10},{10,1... | collective-permute-start | bytes 1572872 | tf_op jit(solution)/shard_map/ppermute | solution.py:243
  67.4 22.4 %collective-permute-start.5 = (f32[2,2,256,128]{3,2,1,0:T(8,128)}, f32[2,2,256,128]{3,2,1,0:T(8,128)}, u32[]{:S(2)}, u32[]{:S(2)}) collective-permute-start(f32[2,2,256,128]{3,2,1,0:T(8,128)} %get-tuple-element.37), channel_id=1, source_target_pairs={{0,1},{1,2},{2,3},{3,4},{4,5},{5,6},{6,7},{7,8},{8,9},{9,10},{10,1... | collective-permute-start | bytes 1572872 | tf_op jit(solution)/shard_map/ppermute | solution.py:243
  67.4 39.3 %collective-permute-start.9 = (f32[2,2,256,128]{3,2,1,0:T(8,128)}, f32[2,2,256,128]{3,2,1,0:T(8,128)}, u32[]{:S(2)}, u32[]{:S(2)}) collective-permute-start(f32[2,2,256,128]{3,2,1,0:T(8,128)} %get-tuple-element.43), channel_id=1, source_target_pairs={{0,1},{1,2},{2,3},{3,4},{4,5},{5,6},{6,7},{7,8},{8,9},{9,10},{10,1... | collective-permute-start | bytes 1572872 | tf_op jit(solution)/shard_map/ppermute | solution.py:243
  67.7 31.5 %all-to-all-start = ((f32[128,8,128]{2,1,0:T(8,128)}), f32[128,8,128]{2,1,0:T(8,128)}, u32[]{:S(2)}, u32[]{:S(2)}) async-start(f32[128,8,128]{2,1,0:T(8,128)} %bitcast.42), calls=%async_computation | async-start | bytes 1048576 | tf_op jit(solution)/shard_map/all_to_all | solution.py:350
  79.7 30.9 %collective-permute-start.11 = (f32[2,2,256,128]{3,2,1,0:T(8,128)}, f32[2,2,256,128]{3,2,1,0:T(8,128)}, u32[]{:S(2)}, u32[]{:S(2)}) collective-permute-start(f32[2,2,256,128]{3,2,1,0:T(8,128)} %get-tuple-element.45), channel_id=1, source_target_pairs={{0,16},{16,32},{32,48},{48,64},{64,80},{80,96},{96,112},{112,0},{1... | collective-permute-start | bytes 1572872 | tf_op jit(solution)/shard_map/ppermute | solution.py:243
  81.2 31.3 %collective-permute-start.12 = (f32[2,2,256,128]{3,2,1,0:T(8,128)}, f32[2,2,256,128]{3,2,1,0:T(8,128)}, u32[]{:S(2)}, u32[]{:S(2)}) collective-permute-start(f32[2,2,256,128]{3,2,1,0:T(8,128)} %get-tuple-element.44), channel_id=1, source_target_pairs={{0,112},{16,0},{32,16},{48,32},{64,48},{80,64},{96,80},{112,96},{1... | collective-permute-start | bytes 1572872 | tf_op jit(solution)/shard_map/ppermute | solution.py:243
  91.7 37.7 %collective-permute-start.7 = (f32[2,2,256,128]{3,2,1,0:T(8,128)}, f32[2,2,256,128]{3,2,1,0:T(8,128)}, u32[]{:S(2)}, u32[]{:S(2)}) collective-permute-start(f32[2,2,256,128]{3,2,1,0:T(8,128)} %add.29), channel_id=1, source_target_pairs={{0,16},{16,32},{32,48},{48,64},{64,80},{80,96},{96,112},{112,0},{1... | collective-permute-start | bytes 1572872 | tf_op jit(solution)/shard_map/ppermute | solution.py:243
  91.7 37.7 %collective-permute-start.8 = (f32[2,2,256,128]{3,2,1,0:T(8,128)}, f32[2,2,256,128]{3,2,1,0:T(8,128)}, u32[]{:S(2)}, u32[]{:S(2)}) collective-permute-start(f32[2,2,256,128]{3,2,1,0:T(8,128)} %add.28), channel_id=1, source_target_pairs={{0,112},{16,0},{32,16},{48,32},{64,48},{80,64},{96,80},{112,96},{1... | collective-permute-start | bytes 1572872 | tf_op jit(solution)/shard_map/ppermute | solution.py:243
  101.2 32.0 %all-to-all-start.1 = ((f32[128,8,128]{2,1,0:T(8,128)}), f32[128,8,128]{2,1,0:T(8,128)}, u32[]{:S(2)}, u32[]{:S(2)}) async-start(f32[128,8,128]{2,1,0:T(8,128)} %broadcast_in_dim.4), calls=%async_computation.1 | async-start | bytes 1048576 | tf_op jit(solution)/shard_map/all_to_all | solution.py:355
  108.3 21.0 %copy-start.10 = (f32[1,2,256,128]{3,2,1,0:T(8,128)S(1)}, f32[1,2,256,128]{3,2,1,0:T(8,128)}, u32[]{:S(2)}) copy-start(f32[1,2,256,128]{3,2,1,0:T(8,128)} %copy-done.9) | copy-start | bytes 786436
  108.3 21.0 %collective-permute-start.10 = (f32[2,2,256,128]{3,2,1,0:T(8,128)S(1)}, f32[2,2,256,128]{3,2,1,0:T(8,128)S(1)}, u32[]{:S(2)}, u32[]{:S(2)}) collective-permute-start(f32[2,2,256,128]{3,2,1,0:T(8,128)S(1)} %multiply_subtract_fusion.5.refs_5_.refs_2_), channel_id=1, source_target_pairs={{0,15},{1,0},{2,1},{3,2},{4,3},{5,4},{6,5},{7,6},{8,7},{9,8},{10,9... | collective-permute-start | bytes 1572872 | tf_op jit(solution)/shard_map/ppermute | solution.py:243
  112.5 18.3 %copy-start.22 = (f32[2,2,256,128]{3,2,1,0:T(8,128)S(1)}, f32[2,2,256,128]{3,2,1,0:T(8,128)}, u32[]{:S(2)}) copy-start(f32[2,2,256,128]{3,2,1,0:T(8,128)} %copy-done.21) | copy-start | bytes 1572868
  133.1 8.7 %collective-permute-start.13 = (f32[2,2,256,128]{3,2,1,0:T(8,128)S(1)}, f32[2,2,256,128]{3,2,1,0:T(8,128)}, u32[]{:S(2)}, u32[]{:S(2)}) collective-permute-start(f32[2,2,256,128]{3,2,1,0:T(8,128)S(1)} %multiply_subtract_fusion.1.refs_2_.refs_0_), channel_id=1, source_target_pairs={{0,15},{1,0},{2,1},{3,2},{4,3},{5,4},{6,5},{7,6},{8,7},{9,8},{10,9... | collective-permute-start | bytes 1572872 | tf_op jit(solution)/shard_map/ppermute | solution.py:243
  133.2 14.3 %collective-permute-start.14 = (f32[2,2,256,128]{3,2,1,0:T(8,128)}, f32[2,2,256,128]{3,2,1,0:T(8,128)}, u32[]{:S(2)}, u32[]{:S(2)}) collective-permute-start(f32[2,2,256,128]{3,2,1,0:T(8,128)} %multiply_subtract_fusion.refs_8_), channel_id=1, source_target_pairs={{0,15},{1,0},{2,1},{3,2},{4,3},{5,4},{6,5},{7,6},{8,7},{9,8},{10,9... | collective-permute-start | bytes 1572872 | tf_op jit(solution)/shard_map/ppermute | solution.py:243
  163.3 10.9 %collective-permute-start.15 = (f32[2,2,256,128]{3,2,1,0:T(8,128)}, f32[2,2,256,128]{3,2,1,0:T(8,128)}, u32[]{:S(2)}, u32[]{:S(2)}) collective-permute-start(f32[2,2,256,128]{3,2,1,0:T(8,128)} %get-tuple-element.59), channel_id=1, source_target_pairs={{0,1},{1,2},{2,3},{3,4},{4,5},{5,6},{6,7},{7,8},{8,9},{9,10},{10,1... | collective-permute-start | bytes 1572872 | tf_op jit(solution)/shard_map/ppermute | solution.py:243
  163.4 15.2 %collective-permute-start.17 = (f32[2,2,256,128]{3,2,1,0:T(8,128)}, f32[2,2,256,128]{3,2,1,0:T(8,128)}, u32[]{:S(2)}, u32[]{:S(2)}) collective-permute-start(f32[2,2,256,128]{3,2,1,0:T(8,128)} %get-tuple-element.61), channel_id=1, source_target_pairs={{0,16},{16,32},{32,48},{48,0},{64,80},{80,96},{96,112},{112,64},{1... | collective-permute-start | bytes 1572872 | tf_op jit(solution)/shard_map/ppermute | solution.py:251
  163.5 25.5 %all-to-all-start.2 = ((f32[128,8,128]{2,1,0:T(8,128)}), f32[128,8,128]{2,1,0:T(8,128)S(1)}, u32[]{:S(2)}, u32[]{:S(2)}) async-start(f32[128,8,128]{2,1,0:T(8,128)} %bitcast.43), calls=%async_computation.2 | async-start | bytes 1048576 | tf_op jit(solution)/shard_map/all_to_all | solution.py:350
  172.4 23.3 %collective-permute-start.19 = (f32[2,2,256,128]{3,2,1,0:T(8,128)}, f32[2,2,256,128]{3,2,1,0:T(8,128)S(1)}, u32[]{:S(2)}, u32[]{:S(2)}) collective-permute-start(f32[2,2,256,128]{3,2,1,0:T(8,128)} %get-tuple-element.66), channel_id=1, source_target_pairs={{0,1},{1,2},{2,3},{3,4},{4,5},{5,6},{6,7},{7,8},{8,9},{9,10},{10,1... | collective-permute-start | bytes 1572872 | tf_op jit(solution)/shard_map/ppermute | solution.py:243
  174.1 21.6 %collective-permute-start.20 = (f32[2,2,256,128]{3,2,1,0:T(8,128)}, f32[2,2,256,128]{3,2,1,0:T(8,128)}, u32[]{:S(2)}, u32[]{:S(2)}) collective-permute-start(f32[2,2,256,128]{3,2,1,0:T(8,128)} %get-tuple-element.67), channel_id=1, source_target_pairs={{0,1},{1,2},{2,3},{3,4},{4,5},{5,6},{6,7},{7,8},{8,9},{9,10},{10,1... | collective-permute-start | bytes 1572872 | tf_op jit(solution)/shard_map/ppermute | solution.py:243
  176.3 35.8 %collective-permute-start.16 = (f32[2,2,256,128]{3,2,1,0:T(8,128)}, f32[2,2,256,128]{3,2,1,0:T(8,128)}, u32[]{:S(2)}, u32[]{:S(2)}) collective-permute-start(f32[2,2,256,128]{3,2,1,0:T(8,128)} %add.35), channel_id=1, source_target_pairs={{0,16},{16,32},{32,48},{48,64},{64,80},{80,96},{96,112},{112,0},{1... | collective-permute-start | bytes 1572872 | tf_op jit(solution)/shard_map/ppermute | solution.py:243
  178.6 33.5 %collective-permute-start.18 = (f32[2,2,256,128]{3,2,1,0:T(8,128)}, f32[2,2,256,128]{3,2,1,0:T(8,128)}, u32[]{:S(2)}, u32[]{:S(2)}) collective-permute-start(f32[2,2,256,128]{3,2,1,0:T(8,128)} %collective-permute-done.17.near), channel_id=1, source_target_pairs={{0,64},{64,0},{1,65},{65,1},{2,66},{66,2},{3,67},{67,3},{4,68},{68... | collective-permute-start | bytes 1572872 | tf_op jit(solution)/shard_map/ppermute | solution.py:257
  190.0 25.0 %all-to-all-start.3 = ((f32[128,8,128]{2,1,0:T(8,128)}), f32[128,8,128]{2,1,0:T(8,128)S(1)}, u32[]{:S(2)}, u32[]{:S(2)}) async-start(f32[128,8,128]{2,1,0:T(8,128)} %broadcast_in_dim.5), calls=%async_computation.3 | async-start | bytes 1048576 | tf_op jit(solution)/shard_map/all_to_all | solution.py:355
  (28 other events, 188.9 us)

commit v3 on v2

--- a/solution.py
+++ b/solution.py
@@ -400,11 +400,12 @@
     g00, g20 = together(g00 + left0, g20 + left2)
     summed = collect(together(terms, g00, g20)[0], probe.shape)
     own10 = step(own10, g10, left1)
-    above0, under0, own12, own01, own11, own21 = together(
-        shift(g20, "row", 1), shift(g00, "row", -1), shift(own10, COL, -1),
+    own12 = shift(own10, COL, -1)
+    above0, under0, own10, own01, own11, own21 = together(
+        shift(g20, "row", 1), shift(g00, "row", -1), own10,
         step(own01, g01, above1), step(own11, g11), step(own21, g21, under1),
     )
-    own00, own20 = together(step(own00, g00, above0), step(own20, g20, under0))
+    own00, own20 = step(own00, g00, above0), step(own20, g20, under0)
     own02, own22 = shift(own00, COL, -1), shift(own20, COL, -1)
     probe = probe - pstep * summed
 

time: 217 us -> 220 us (1.014)
  starting transfers between devices: 72.5 us -> 88.6 us
  Pallas kernels: 39.7 us -> 30.1 us
    ppermute x19, starting transfers between devices: 30.1 us -> 42.5 us  [shift(): lax.ppermute(block, axis, [(i, (i + distance) % n) for i in range(n)])]
    pallas_call x2, Pallas kernels: 31.7 us -> 22.1 us  [windows(): pl.pallas_call(windows_kernel, out_shape=[pltpu.HBM(block.shape, F32)] *...]
    all_to_all x2, starting transfers between devices: 20.8 us -> 27.8 us  [deal(): lax.all_to_all(x.reshape(-1, 8, LANES), ('row', *COL), 0, 0, tiled=True)]
    ppermute x1, starting transfers between devices: 10.3 us -> 4.43 us  [cross_y(): lax.ppermute(block, 'row', [(i, (i + RING) % n) for i in range(edge, n, R...]
    ppermute x19, waiting for transfers between devices: 65.1 us -> 59.7 us  [shift(): lax.ppermute(block, axis, [(i, (i + distance) % n) for i in range(n)])]
    all_to_all x2, waiting for transfers between devices: 2.43 us -> 6.85 us  [deal(): lax.all_to_all(x.reshape(-1, 8, LANES), ('row', *COL), 0, 0, tiled=True)]
    all_to_all x2, starting transfers between devices: 11.3 us -> 13.9 us  [collect(): lax.all_to_all(spread, ('row', *COL), 0, 0, tiled=True).reshape(shape)]
where the time goes in v3:
time: 220 us
  starting transfers between devices  88.6 us (40%)
  waiting for transfers between devices  66.6 us (30%)
  Pallas kernels  30.1 us (14%)
  other arithmetic  23.4 us (11%)
  matrix products  5.08 us (2%)
  local copies, waits for them, and re-layouts  4.57 us (2%)
    ppermute x19, waiting for transfers between devices, shift(): lax.ppermute(block, axis, [(i, (i + distance) % n) for i in range(n)])  59.7 us
    ppermute x19, starting transfers between devices, shift(): lax.ppermute(block, axis, [(i, (i + distance) % n) for i in range(n)])  42.5 us
    all_to_all x2, starting transfers between devices, deal(): lax.all_to_all(x.reshape(-1, 8, LANES), ('row', *COL), 0, 0, tiled=True)  27.8 us
    pallas_call x2, Pallas kernels, windows(): pl.pallas_call(windows_kernel, out_shape=[pltpu.HBM(block.shape, F32)] *...  22.1 us
    all_to_all x2, starting transfers between devices, collect(): lax.all_to_all(spread, ('row', *COL), 0, 0, tiled=True).reshape(shape)  13.9 us
    sub x6, other arithmetic, step(): return x - OBJECT_RATE * sum(grads[1:], grads[0])  11.8 us
    all_to_all x2, waiting for transfers between devices, deal(): lax.all_to_all(x.reshape(-1, 8, LANES), ('row', *COL), 0, 0, tiled=True)  6.85 us
    ppermute x1, starting transfers between devices, cross_y(): lax.ppermute(block, 'row', [(i, (i + RING) % n) for i in range(edge, n, R...  4.43 us
  transfers between devices with their start and end apart: 25, of which 10 were waited for; matrix products, arithmetic and copies ran while one was open for 14% of the time, Pallas kernels for 3%

profile of v3, /device:TPU:1, one launch (start us, length us, event | category | flops | bytes accessed | tf_op | source)
XLA Modules:
  0.0 220.1 jit_solution(10355358408319219649)
XLA Ops:
  2.6 7.3 %collective-permute-start.2 = (f32[2,2,256,128]{3,2,1,0:T(8,128)S(1)}, f32[2,2,256,128]{3,2,1,0:T(8,128)S(1)}, u32[]{:S(2)}, u32[]{:S(2)}) collective-permute-start(f32[2,2,256,128]{3,2,1,0:T(8,128)S(1)} %pad_maximum_fusion.refs_2_), channel_id=1, source_target_pairs={{0,112},{16,0},{32,16},{48,32},{64,48},{80,64},{96,80},{112,96},{1... | collective-permute-start | bytes 1572872 | tf_op jit(solution)/shard_map/ppermute | solution.py:243
  11.2 3.0 %collective-permute-start.1 = (f32[2,2,256,128]{3,2,1,0:T(8,128)S(1)}, f32[2,2,256,128]{3,2,1,0:T(8,128)S(1)}, u32[]{:S(2)}, u32[]{:S(2)}) collective-permute-start(f32[2,2,256,128]{3,2,1,0:T(8,128)S(1)} %pad_maximum_fusion.2.refs_5_), channel_id=1, source_target_pairs={{0,15},{1,0},{2,1},{3,2},{4,3},{5,4},{6,5},{7,6},{8,7},{9,8},{10,9... | collective-permute-start | bytes 1572872 | tf_op jit(solution)/shard_map/ppermute | solution.py:243
  16.2 15.6 %collective-permute-done.2.refs_8_ = f32[2,2,256,128]{3,2,1,0:T(8,128)S(1)} collective-permute-done((f32[2,2,256,128]{3,2,1,0:T(8,128)S(1)}, f32[2,2,256,128]{3,2,1,0:T(8,128)S(1)}, u32[]{:S(2)}, u32[]{:S(2)}) %collective-permute-start.2) | collective-permute-done | bytes 524320 | tf_op jit(solution)/shard_map/ppermute | solution.py:243
  31.7 2.7 %collective-permute-start.4 = (f32[2,2,256,128]{3,2,1,0:T(8,128)S(1)}, f32[2,2,256,128]{3,2,1,0:T(8,128)S(1)}, u32[]{:S(2)}, u32[]{:S(2)}) collective-permute-start(f32[2,2,256,128]{3,2,1,0:T(8,128)S(1)} %collective-permute-done.2.refs_8_), channel_id=1, source_target_pairs={{0,15},{1,0},{2,1},{3,2},{4,3},{5,4},{6,5},{7,6},{8,7},{9,8},{10,9... | collective-permute-start | bytes 1572872 | tf_op jit(solution)/shard_map/ppermute | solution.py:243
  36.4 3.2 %fusion.refs_12_ = f32[8,256,256]{2,1,0:T(8,128)} fusion(f32[256,256,1]{1,0,2:T(8,128)S(1)} %copy-done.23, f32[256,8,256]{2,0,1:T(8,128)S(1)} %fusion.2), kind=kOutput, calls=%fused_computation | convolution fusion | flops 1610612736 | bytes 4456448 | tf_op jit(solution)/shard_map/sjk,lk->sjl/dot_general | solution.py:382
  39.6 9.0 %collective-permute-done.3.refs_9_ = f32[2,2,256,128]{3,2,1,0:T(8,128)S(1)} collective-permute-done((f32[2,2,256,128]{3,2,1,0:T(8,128)S(1)}, f32[2,2,256,128]{3,2,1,0:T(8,128)S(1)}, u32[]{:S(2)}, u32[]{:S(2)}) %collective-permute-start.3) | collective-permute-done | bytes 524320 | tf_op jit(solution)/shard_map/ppermute | solution.py:243
  51.4 11.1 %windows.2 = (f32[2,2,256,128]{3,2,1,0:T(8,128)}, f32[2,2,256,128]{3,2,1,0:T(8,128)}, f32[2,2,256,128]{3,2,1,0:T(8,128)}, f32[2,2,256,128]{3,2,1,0:T(8,128)}, f3...) custom-call(s32[2,8]{1,0:T(2,128)S(1)} %bitcast.39, ...), custom_call_target="tpu_custom_call" | custom-call | tf_op jit(solution)/shard_map/windows/pallas_call | solution.py:228
  62.5 4.6 %collective-permute-start.6 = (f32[2,2,256,128]{3,2,1,0:T(8,128)}, f32[2,2,256,128]{3,2,1,0:T(8,128)}, u32[]{:S(2)}, u32[]{:S(2)}) collective-permute-start(f32[2,2,256,128]{3,2,1,0:T(8,128)} %get-tuple-element.37), channel_id=1, source_target_pairs={{0,1},{1,2},{2,3},{3,4},{4,5},{5,6},{6,7},{7,8},{8,9},{9,10},{10,1... | collective-permute-start | bytes 1572872 | tf_op jit(solution)/shard_map/ppermute | solution.py:243
  67.2 2.9 %collective-permute-start.9 = (f32[2,2,256,128]{3,2,1,0:T(8,128)}, f32[2,2,256,128]{3,2,1,0:T(8,128)}, u32[]{:S(2)}, u32[]{:S(2)}) collective-permute-start(f32[2,2,256,128]{3,2,1,0:T(8,128)} %get-tuple-element.41), channel_id=1, source_target_pairs={{0,1},{1,2},{2,3},{3,4},{4,5},{5,6},{6,7},{7,8},{8,9},{9,10},{10,1... | collective-permute-start | bytes 1572872 | tf_op jit(solution)/shard_map/ppermute | solution.py:243
  70.1 7.5 %all-to-all-start = ((f32[128,8,128]{2,1,0:T(8,128)}), f32[128,8,128]{2,1,0:T(8,128)}, u32[]{:S(2)}, u32[]{:S(2)}) async-start(f32[128,8,128]{2,1,0:T(8,128)} %bitcast.42), calls=%async_computation | async-start | bytes 1048576 | tf_op jit(solution)/shard_map/all_to_all | solution.py:350
  79.2 4.4 %collective-permute-start.11 = (f32[2,2,256,128]{3,2,1,0:T(8,128)}, f32[2,2,256,128]{3,2,1,0:T(8,128)}, u32[]{:S(2)}, u32[]{:S(2)}) collective-permute-start(f32[2,2,256,128]{3,2,1,0:T(8,128)} %get-tuple-element.42), channel_id=1, source_target_pairs={{0,112},{16,0},{32,16},{48,32},{64,48},{80,64},{96,80},{112,96},{1... | collective-permute-start | bytes 1572872 | tf_op jit(solution)/shard_map/ppermute | solution.py:243
  85.5 2.1 add.29
  89.4 5.1 %collective-permute-start.8 = (f32[2,2,256,128]{3,2,1,0:T(8,128)}, f32[2,2,256,128]{3,2,1,0:T(8,128)}, u32[]{:S(2)}, u32[]{:S(2)}) collective-permute-start(f32[2,2,256,128]{3,2,1,0:T(8,128)} %add.28), channel_id=1, source_target_pairs={{0,112},{16,0},{32,16},{48,32},{64,48},{80,64},{96,80},{112,96},{1... | collective-permute-start | bytes 1572872 | tf_op jit(solution)/shard_map/ppermute | solution.py:243
  94.5 2.7 %all-to-all-done = f32[128,8,128]{2,1,0:T(8,128)} async-done(((f32[128,8,128]{2,1,0:T(8,128)}), f32[128,8,128]{2,1,0:T(8,128)}, u32[]{:S(2)}, u32[]{:S(2)}) %all-to-all-start) | async-done | bytes 524320 | tf_op jit(solution)/shard_map/all_to_all | solution.py:350
  99.2 9.4 %all-to-all-start.1 = ((f32[128,8,128]{2,1,0:T(8,128)}), f32[128,8,128]{2,1,0:T(8,128)}, u32[]{:S(2)}, u32[]{:S(2)}) async-start(f32[128,8,128]{2,1,0:T(8,128)} %broadcast_in_dim.4), calls=%async_computation.1 | async-start | bytes 1048576 | tf_op jit(solution)/shard_map/all_to_all | solution.py:355
  111.4 2.2 %multiply_subtract_fusion.4.refs_3_.refs_1_ = f32[2,2,256,128]{3,2,1,0:T(8,128)} fusion(f32[2,2,256,128]{3,2,1,0:T(8,128)} %get-tuple-element.42, f32[2,2,256,128]{3,2,1,0:T(8,128)} %collective-permute-done.10, f32[1,2,256,128]{3,2,1,0:T(8,128)} %copy-done.10, f32[1,2,256,128]{3,2,1,0:T(8,128)} %copy-done.11), kind=kLoop, calls=%fused_computation.13 | loop fusion | flops 524288 | bytes 2097152 | tf_op jit(solution)/shard_map/sub | solution.py:385
  115.6 7.8 %collective-permute-done.8 = f32[2,2,256,128]{3,2,1,0:T(8,128)} collective-permute-done((f32[2,2,256,128]{3,2,1,0:T(8,128)}, f32[2,2,256,128]{3,2,1,0:T(8,128)}, u32[]{:S(2)}, u32[]{:S(2)}) %collective-permute-start.8) | collective-permute-done | bytes 524320 | tf_op jit(solution)/shard_map/ppermute | solution.py:243
  123.4 2.1 multiply_subtract_fusion.refs_8_
  125.5 2.1 multiply_subtract_fusion.1.refs_2_.refs_0_
  131.3 3.7 %collective-permute-done.14.refs_10_ = f32[2,2,256,128]{3,2,1,0:T(8,128)} collective-permute-done((f32[2,2,256,128]{3,2,1,0:T(8,128)}, f32[2,2,256,128]{3,2,1,0:T(8,128)}, u32[]{:S(2)}, u32[]{:S(2)}) %collective-permute-start.14) | collective-permute-done | bytes 524320 | tf_op jit(solution)/shard_map/ppermute | solution.py:243
  135.0 5.6 %collective-permute-done.12.refs_4_ = f32[2,2,256,128]{3,2,1,0:T(8,128)} collective-permute-done((f32[2,2,256,128]{3,2,1,0:T(8,128)}, f32[2,2,256,128]{3,2,1,0:T(8,128)}, u32[]{:S(2)}, u32[]{:S(2)}) %collective-permute-start.12) | collective-permute-done | bytes 524320 | tf_op jit(solution)/shard_map/ppermute | solution.py:243
  140.7 11.0 %windows.3 = (f32[2,2,256,128]{3,2,1,0:T(8,128)}, f32[2,2,256,128]{3,2,1,0:T(8,128)}, f32[2,2,256,128]{3,2,1,0:T(8,128)}, f32[2,2,256,128]{3,2,1,0:T(8,128)}, f3...) custom-call(s32[2,8]{1,0:T(2,128)S(1)} %bitcast.40, ...), custom_call_target="tpu_custom_call" | custom-call | tf_op jit(solution)/shard_map/windows/pallas_call | solution.py:228
  151.7 4.6 %collective-permute-start.15 = (f32[2,2,256,128]{3,2,1,0:T(8,128)}, f32[2,2,256,128]{3,2,1,0:T(8,128)}, u32[]{:S(2)}, u32[]{:S(2)}) collective-permute-start(f32[2,2,256,128]{3,2,1,0:T(8,128)} %get-tuple-element.55), channel_id=1, source_target_pairs={{0,1},{1,2},{2,3},{3,4},{4,5},{5,6},{6,7},{7,8},{8,9},{9,10},{10,1... | collective-permute-start | bytes 1572872 | tf_op jit(solution)/shard_map/ppermute | solution.py:243
  156.3 20.3 %all-to-all-start.2 = ((f32[128,8,128]{2,1,0:T(8,128)}), f32[128,8,128]{2,1,0:T(8,128)S(1)}, u32[]{:S(2)}, u32[]{:S(2)}) async-start(f32[128,8,128]{2,1,0:T(8,128)} %bitcast.43), calls=%async_computation.2 | async-start | bytes 1048576 | tf_op jit(solution)/shard_map/all_to_all | solution.py:350
  178.5 2.1 add.35
  181.9 4.4 %collective-permute-start.18 = (f32[2,2,256,128]{3,2,1,0:T(8,128)}, f32[2,2,256,128]{3,2,1,0:T(8,128)}, u32[]{:S(2)}, u32[]{:S(2)}) collective-permute-start(f32[2,2,256,128]{3,2,1,0:T(8,128)} %collective-permute-done.17.near), channel_id=1, source_target_pairs={{0,64},{64,0},{1,65},{65,1},{2,66},{66,2},{3,67},{67,3},{4,68},{68... | collective-permute-start | bytes 1572872 | tf_op jit(solution)/shard_map/ppermute | solution.py:257
  186.3 4.2 %all-to-all-done.2 = f32[128,8,128]{2,1,0:T(8,128)S(1)} async-done(((f32[128,8,128]{2,1,0:T(8,128)}), f32[128,8,128]{2,1,0:T(8,128)S(1)}, u32[]{:S(2)}, u32[]{:S(2)}) %all-to-all-start.2) | async-done | bytes 524320 | tf_op jit(solution)/shard_map/all_to_all | solution.py:350
  191.5 4.5 %all-to-all-start.3 = ((f32[128,8,128]{2,1,0:T(8,128)}), f32[128,8,128]{2,1,0:T(8,128)S(1)}, u32[]{:S(2)}, u32[]{:S(2)}) async-start(f32[128,8,128]{2,1,0:T(8,128)} %broadcast_in_dim.5), calls=%async_computation.3 | async-start | bytes 1048576 | tf_op jit(solution)/shard_map/all_to_all | solution.py:355
  196.1 7.7 %collective-permute-done.20.refs_9_ = f32[2,2,256,128]{3,2,1,0:T(8,128)} collective-permute-done((f32[2,2,256,128]{3,2,1,0:T(8,128)}, f32[2,2,256,128]{3,2,1,0:T(8,128)}, u32[]{:S(2)}, u32[]{:S(2)}) %collective-permute-start.20) | collective-permute-done | bytes 524320 | tf_op jit(solution)/shard_map/ppermute | solution.py:243
  203.8 4.2 %most.1.whole_in = f32[2,512,512]{2,1,0:T(8,128)} custom-call(f32[2,2,256,128]{3,2,1,0:T(8,128)} %multiply_subtract_fusion.1.refs_2_.refs_0_, f32[2,2,256,128]{3,2,1,0:T(8,128)} %multiply_subtract_fusion.4.refs_3_.refs_1_, f32[2,2,256,128]{3,2,1,0:T(8,128)} %copy-done.7, f32[2,2,256,128]{3,2,1,0:T(8,128)} %multiply_subtract_fusion.3.refs_6_.refs_3_, ...), custom_call_target="tpu_custom_call" | custom-call | tf_op jit(solution)/shard_map/most/pallas_call | solution.py:307
  208.0 8.3 %collective-permute-done.16.above0 = f32[2,2,256,128]{3,2,1,0:T(8,128)} collective-permute-done((f32[2,2,256,128]{3,2,1,0:T(8,128)}, f32[2,2,256,128]{3,2,1,0:T(8,128)}, u32[]{:S(2)}, u32[]{:S(2)}) %collective-permute-start.16) | collective-permute-done | bytes 524320 | tf_op jit(solution)/shard_map/ppermute | solution.py:243
  216.3 2.9 %rest.1 = f32[2,512,512]{2,1,0:T(8,128)} custom-call(s32[1]{0:T(128)} %bitcast.19.wrapped, f32[2,2,256,128]{3,2,1,0:T(8,128)} %collective-permute-done.16.above0, f32[2,2,256,128]{3,2,1,0:T(8,128)} %collective-permute-done.17.near, f32[2,2,256,128]{3,2,1,0:T(8,128)} %collective-permute-done.18.far, ...), custom_call_target="tpu_custom_call", output_to_operand_aliasing={{}: (4, {})} | custom-call | tf_op jit(solution)/shard_map/rest/pallas_call | solution.py:320
  (108 shorter events, 30.2 us)
Async XLA Ops:
  2.5 13.6 %copy-start.8 = (f32[1,2,256,128]{3,2,1,0:T(8,128)}, f32[1,2,256,128]{3,2,1,0:T(8,128)S(1)}, u32[]{:S(2)}) copy-start(f32[1,2,256,128]{3,2,1,0:T(8,128)S(1)} %get-tuple-element.72) | copy-start | bytes 786436
  2.6 29.1 %collective-permute-start.2 = (f32[2,2,256,128]{3,2,1,0:T(8,128)S(1)}, f32[2,2,256,128]{3,2,1,0:T(8,128)S(1)}, u32[]{:S(2)}, u32[]{:S(2)}) collective-permute-start(f32[2,2,256,128]{3,2,1,0:T(8,128)S(1)} %pad_maximum_fusion.refs_2_), channel_id=1, source_target_pairs={{0,112},{16,0},{32,16},{48,32},{64,48},{80,64},{96,80},{112,96},{1... | collective-permute-start | bytes 1572872 | tf_op jit(solution)/shard_map/ppermute | solution.py:243
  9.9 38.7 %collective-permute-start = (f32[2,2,256,128]{3,2,1,0:T(8,128)S(1)}, f32[2,2,256,128]{3,2,1,0:T(8,128)S(1)}, u32[]{:S(2)}, u32[]{:S(2)}) collective-permute-start(f32[2,2,256,128]{3,2,1,0:T(8,128)S(1)} %pad_maximum_fusion.refs_2_), channel_id=1, source_target_pairs={{0,15},{1,0},{2,1},{3,2},{4,3},{5,4},{6,5},{7,6},{8,7},{9,8},{10,9... | collective-permute-start | bytes 1572872 | tf_op jit(solution)/shard_map/ppermute | solution.py:243
  10.9 37.7 %collective-permute-start.3 = (f32[2,2,256,128]{3,2,1,0:T(8,128)S(1)}, f32[2,2,256,128]{3,2,1,0:T(8,128)S(1)}, u32[]{:S(2)}, u32[]{:S(2)}) collective-permute-start(f32[2,2,256,128]{3,2,1,0:T(8,128)S(1)} %pad_maximum_fusion.1.refs_3_), channel_id=1, source_target_pairs={{0,112},{16,0},{32,16},{48,32},{64,48},{80,64},{96,80},{112,96},{1... | collective-permute-start | bytes 1572872 | tf_op jit(solution)/shard_map/ppermute | solution.py:243
  11.2 23.2 %copy-start.29 = (f32[2,256,256]{2,1,0:T(8,128)S(1)}, f32[2,256,256]{2,1,0:T(8,128)}, u32[]{:S(2)}) copy-start(f32[2,256,256]{2,1,0:T(8,128)} %param.12) | copy-start | bytes 1572868
  11.2 37.4 %collective-permute-start.1 = (f32[2,2,256,128]{3,2,1,0:T(8,128)S(1)}, f32[2,2,256,128]{3,2,1,0:T(8,128)S(1)}, u32[]{:S(2)}, u32[]{:S(2)}) collective-permute-start(f32[2,2,256,128]{3,2,1,0:T(8,128)S(1)} %pad_maximum_fusion.2.refs_5_), channel_id=1, source_target_pairs={{0,15},{1,0},{2,1},{3,2},{4,3},{5,4},{6,5},{7,6},{8,7},{9,8},{10,9... | collective-permute-start | bytes 1572872 | tf_op jit(solution)/shard_map/ppermute | solution.py:243
  31.7 18.8 %collective-permute-start.4 = (f32[2,2,256,128]{3,2,1,0:T(8,128)S(1)}, f32[2,2,256,128]{3,2,1,0:T(8,128)S(1)}, u32[]{:S(2)}, u32[]{:S(2)}) collective-permute-start(f32[2,2,256,128]{3,2,1,0:T(8,128)S(1)} %collective-permute-done.2.refs_8_), channel_id=1, source_target_pairs={{0,15},{1,0},{2,1},{3,2},{4,3},{5,4},{6,5},{7,6},{8,7},{9,8},{10,9... | collective-permute-start | bytes 1572872 | tf_op jit(solution)/shard_map/ppermute | solution.py:243
  36.4 15.0 %copy-start.2 = (bf16[256,256]{1,0:T(8,128)(2,1)S(1)}, bf16[256,256]{1,0:T(8,128)(2,1)}, u32[]{:S(2)}) copy-start(bf16[256,256]{1,0:T(8,128)(2,1)} %constant.36.clone.refs_13_) | copy-start | bytes 393220
  36.4 15.0 %copy-start.3 = (bf16[256,256]{1,0:T(8,128)(2,1)S(1)}, bf16[256,256]{1,0:T(8,128)(2,1)}, u32[]{:S(2)}) copy-start(bf16[256,256]{1,0:T(8,128)(2,1)} %constant.37.clone.refs_14_) | copy-start | bytes 393220
  36.4 15.0 %copy-start.4 = (bf16[256,256]{1,0:T(8,128)(2,1)S(1)}, bf16[256,256]{1,0:T(8,128)(2,1)}, u32[]{:S(2)}) copy-start(bf16[256,256]{1,0:T(8,128)(2,1)} %constant.38.clone.refs_15_) | copy-start | bytes 393220
  36.4 15.0 %copy-start.5 = (bf16[256,256]{1,0:T(8,128)(2,1)S(1)}, bf16[256,256]{1,0:T(8,128)(2,1)}, u32[]{:S(2)}) copy-start(bf16[256,256]{1,0:T(8,128)(2,1)} %constant.39.clone.refs_16_) | copy-start | bytes 393220
  36.4 15.0 %copy-start.6 = (s32[1,1,2,8]{3,2,1,0:T(2,128)S(1)}, s32[1,1,2,8]{3,2,1,0:T(2,128)}, u32[]{:S(2)}) copy-start(s32[1,1,2,8]{3,2,1,0:T(2,128)} %param.13) | copy-start | bytes 196
  62.5 23.0 %collective-permute-start.6 = (f32[2,2,256,128]{3,2,1,0:T(8,128)}, f32[2,2,256,128]{3,2,1,0:T(8,128)}, u32[]{:S(2)}, u32[]{:S(2)}) collective-permute-start(f32[2,2,256,128]{3,2,1,0:T(8,128)} %get-tuple-element.37), channel_id=1, source_target_pairs={{0,1},{1,2},{2,3},{3,4},{4,5},{5,6},{6,7},{7,8},{8,9},{9,10},{10,1... | collective-permute-start | bytes 1572872 | tf_op jit(solution)/shard_map/ppermute | solution.py:243
  67.1 20.4 %collective-permute-start.5 = (f32[2,2,256,128]{3,2,1,0:T(8,128)}, f32[2,2,256,128]{3,2,1,0:T(8,128)}, u32[]{:S(2)}, u32[]{:S(2)}) collective-permute-start(f32[2,2,256,128]{3,2,1,0:T(8,128)} %get-tuple-element.35), channel_id=1, source_target_pairs={{0,1},{1,2},{2,3},{3,4},{4,5},{5,6},{6,7},{7,8},{8,9},{9,10},{10,1... | collective-permute-start | bytes 1572872 | tf_op jit(solution)/shard_map/ppermute | solution.py:243
  67.2 41.4 %collective-permute-start.9 = (f32[2,2,256,128]{3,2,1,0:T(8,128)}, f32[2,2,256,128]{3,2,1,0:T(8,128)}, u32[]{:S(2)}, u32[]{:S(2)}) collective-permute-start(f32[2,2,256,128]{3,2,1,0:T(8,128)} %get-tuple-element.41), channel_id=1, source_target_pairs={{0,1},{1,2},{2,3},{3,4},{4,5},{5,6},{6,7},{7,8},{8,9},{9,10},{10,1... | collective-permute-start | bytes 1572872 | tf_op jit(solution)/shard_map/ppermute | solution.py:243
  70.1 27.1 %all-to-all-start = ((f32[128,8,128]{2,1,0:T(8,128)}), f32[128,8,128]{2,1,0:T(8,128)}, u32[]{:S(2)}, u32[]{:S(2)}) async-start(f32[128,8,128]{2,1,0:T(8,128)} %bitcast.42), calls=%async_computation | async-start | bytes 1048576 | tf_op jit(solution)/shard_map/all_to_all | solution.py:350
  77.6 33.8 %collective-permute-start.10 = (f32[2,2,256,128]{3,2,1,0:T(8,128)}, f32[2,2,256,128]{3,2,1,0:T(8,128)}, u32[]{:S(2)}, u32[]{:S(2)}) collective-permute-start(f32[2,2,256,128]{3,2,1,0:T(8,128)} %get-tuple-element.43), channel_id=1, source_target_pairs={{0,16},{16,32},{32,48},{48,64},{64,80},{80,96},{96,112},{112,0},{1... | collective-permute-start | bytes 1572872 | tf_op jit(solution)/shard_map/ppermute | solution.py:243
  79.2 34.4 %collective-permute-start.11 = (f32[2,2,256,128]{3,2,1,0:T(8,128)}, f32[2,2,256,128]{3,2,1,0:T(8,128)}, u32[]{:S(2)}, u32[]{:S(2)}) collective-permute-start(f32[2,2,256,128]{3,2,1,0:T(8,128)} %get-tuple-element.42), channel_id=1, source_target_pairs={{0,112},{16,0},{32,16},{48,32},{64,48},{80,64},{96,80},{112,96},{1... | collective-permute-start | bytes 1572872 | tf_op jit(solution)/shard_map/ppermute | solution.py:243
  89.4 26.2 %collective-permute-start.7 = (f32[2,2,256,128]{3,2,1,0:T(8,128)}, f32[2,2,256,128]{3,2,1,0:T(8,128)}, u32[]{:S(2)}, u32[]{:S(2)}) collective-permute-start(f32[2,2,256,128]{3,2,1,0:T(8,128)} %add.29), channel_id=1, source_target_pairs={{0,16},{16,32},{32,48},{48,64},{64,80},{80,96},{96,112},{112,0},{1... | collective-permute-start | bytes 1572872 | tf_op jit(solution)/shard_map/ppermute | solution.py:243
  89.4 34.0 %collective-permute-start.8 = (f32[2,2,256,128]{3,2,1,0:T(8,128)}, f32[2,2,256,128]{3,2,1,0:T(8,128)}, u32[]{:S(2)}, u32[]{:S(2)}) collective-permute-start(f32[2,2,256,128]{3,2,1,0:T(8,128)} %add.28), channel_id=1, source_target_pairs={{0,112},{16,0},{32,16},{48,32},{64,48},{80,64},{96,80},{112,96},{1... | collective-permute-start | bytes 1572872 | tf_op jit(solution)/shard_map/ppermute | solution.py:243
  99.2 29.1 %all-to-all-start.1 = ((f32[128,8,128]{2,1,0:T(8,128)}), f32[128,8,128]{2,1,0:T(8,128)}, u32[]{:S(2)}, u32[]{:S(2)}) async-start(f32[128,8,128]{2,1,0:T(8,128)} %broadcast_in_dim.4), calls=%async_computation.1 | async-start | bytes 1048576 | tf_op jit(solution)/shard_map/all_to_all | solution.py:355
  110.2 21.2 %collective-permute-start.13 = (f32[2,2,256,128]{3,2,1,0:T(8,128)S(1)}, f32[2,2,256,128]{3,2,1,0:T(8,128)}, u32[]{:S(2)}, u32[]{:S(2)}) collective-permute-start(f32[2,2,256,128]{3,2,1,0:T(8,128)S(1)} %multiply_subtract_fusion.5.refs_5_.refs_2_), channel_id=1, source_target_pairs={{0,15},{1,0},{2,1},{3,2},{4,3},{5,4},{6,5},{7,6},{8,7},{9,8},{10,9... | collective-permute-start | bytes 1572872 | tf_op jit(solution)/shard_map/ppermute | solution.py:243
  125.5 9.5 %collective-permute-start.14 = (f32[2,2,256,128]{3,2,1,0:T(8,128)}, f32[2,2,256,128]{3,2,1,0:T(8,128)}, u32[]{:S(2)}, u32[]{:S(2)}) collective-permute-start(f32[2,2,256,128]{3,2,1,0:T(8,128)} %multiply_subtract_fusion.refs_8_), channel_id=1, source_target_pairs={{0,15},{1,0},{2,1},{3,2},{4,3},{5,4},{6,5},{7,6},{8,7},{9,8},{10,9... | collective-permute-start | bytes 1572872 | tf_op jit(solution)/shard_map/ppermute | solution.py:243
  127.6 13.1 %collective-permute-start.12 = (f32[2,2,256,128]{3,2,1,0:T(8,128)}, f32[2,2,256,128]{3,2,1,0:T(8,128)}, u32[]{:S(2)}, u32[]{:S(2)}) collective-permute-start(f32[2,2,256,128]{3,2,1,0:T(8,128)} %multiply_subtract_fusion.1.refs_2_.refs_0_), channel_id=1, source_target_pairs={{0,15},{1,0},{2,1},{3,2},{4,3},{5,4},{6,5},{7,6},{8,7},{9,8},{10,9... | collective-permute-start | bytes 1572872 | tf_op jit(solution)/shard_map/ppermute | solution.py:243
  151.7 26.8 %collective-permute-start.15 = (f32[2,2,256,128]{3,2,1,0:T(8,128)}, f32[2,2,256,128]{3,2,1,0:T(8,128)}, u32[]{:S(2)}, u32[]{:S(2)}) collective-permute-start(f32[2,2,256,128]{3,2,1,0:T(8,128)} %get-tuple-element.55), channel_id=1, source_target_pairs={{0,1},{1,2},{2,3},{3,4},{4,5},{5,6},{6,7},{7,8},{8,9},{9,10},{10,1... | collective-permute-start | bytes 1572872 | tf_op jit(solution)/shard_map/ppermute | solution.py:243
  156.3 25.6 %collective-permute-start.17 = (f32[2,2,256,128]{3,2,1,0:T(8,128)}, f32[2,2,256,128]{3,2,1,0:T(8,128)}, u32[]{:S(2)}, u32[]{:S(2)}) collective-permute-start(f32[2,2,256,128]{3,2,1,0:T(8,128)} %get-tuple-element.57), channel_id=1, source_target_pairs={{0,16},{16,32},{32,48},{48,0},{64,80},{80,96},{96,112},{112,64},{1... | collective-permute-start | bytes 1572872 | tf_op jit(solution)/shard_map/ppermute | solution.py:251
  156.3 34.2 %all-to-all-start.2 = ((f32[128,8,128]{2,1,0:T(8,128)}), f32[128,8,128]{2,1,0:T(8,128)S(1)}, u32[]{:S(2)}, u32[]{:S(2)}) async-start(f32[128,8,128]{2,1,0:T(8,128)} %bitcast.43), calls=%async_computation.2 | async-start | bytes 1048576 | tf_op jit(solution)/shard_map/all_to_all | solution.py:350
  176.6 19.4 %collective-permute-start.19 = (f32[2,2,256,128]{3,2,1,0:T(8,128)}, f32[2,2,256,128]{3,2,1,0:T(8,128)S(1)}, u32[]{:S(2)}, u32[]{:S(2)}) collective-permute-start(f32[2,2,256,128]{3,2,1,0:T(8,128)} %get-tuple-element.62), channel_id=1, source_target_pairs={{0,1},{1,2},{2,3},{3,4},{4,5},{5,6},{6,7},{7,8},{8,9},{9,10},{10,1... | collective-permute-start | bytes 1572872 | tf_op jit(solution)/shard_map/ppermute | solution.py:243
  178.3 25.4 %collective-permute-start.20 = (f32[2,2,256,128]{3,2,1,0:T(8,128)}, f32[2,2,256,128]{3,2,1,0:T(8,128)}, u32[]{:S(2)}, u32[]{:S(2)}) collective-permute-start(f32[2,2,256,128]{3,2,1,0:T(8,128)} %get-tuple-element.63), channel_id=1, source_target_pairs={{0,1},{1,2},{2,3},{3,4},{4,5},{5,6},{6,7},{7,8},{8,9},{9,10},{10,1... | collective-permute-start | bytes 1572872 | tf_op jit(solution)/shard_map/ppermute | solution.py:243
  180.5 35.8 %collective-permute-start.16 = (f32[2,2,256,128]{3,2,1,0:T(8,128)}, f32[2,2,256,128]{3,2,1,0:T(8,128)}, u32[]{:S(2)}, u32[]{:S(2)}) collective-permute-start(f32[2,2,256,128]{3,2,1,0:T(8,128)} %add.35), channel_id=1, source_target_pairs={{0,16},{16,32},{32,48},{48,64},{64,80},{80,96},{96,112},{112,0},{1... | collective-permute-start | bytes 1572872 | tf_op jit(solution)/shard_map/ppermute | solution.py:243
  181.9 34.4 %collective-permute-start.18 = (f32[2,2,256,128]{3,2,1,0:T(8,128)}, f32[2,2,256,128]{3,2,1,0:T(8,128)}, u32[]{:S(2)}, u32[]{:S(2)}) collective-permute-start(f32[2,2,256,128]{3,2,1,0:T(8,128)} %collective-permute-done.17.near), channel_id=1, source_target_pairs={{0,64},{64,0},{1,65},{65,1},{2,66},{66,2},{3,67},{67,3},{4,68},{68... | collective-permute-start | bytes 1572872 | tf_op jit(solution)/shard_map/ppermute | solution.py:257
  191.5 27.7 %all-to-all-start.3 = ((f32[128,8,128]{2,1,0:T(8,128)}), f32[128,8,128]{2,1,0:T(8,128)S(1)}, u32[]{:S(2)}, u32[]{:S(2)}) async-start(f32[128,8,128]{2,1,0:T(8,128)} %broadcast_in_dim.5), calls=%async_computation.3 | async-start | bytes 1048576 | tf_op jit(solution)/shard_map/all_to_all | solution.py:355
  (24 other events, 161.0 us)

commit v4 on v2

--- a/solution.py
+++ b/solution.py
@@ -404,7 +404,7 @@
         shift(g20, "row", 1), shift(g00, "row", -1), shift(own10, COL, -1),
         step(own01, g01, above1), step(own11, g11), step(own21, g21, under1),
     )
-    own00, own20 = together(step(own00, g00, above0), step(own20, g20, under0))
+    own00, own20 = step(own00, g00, above0), step(own20, g20, under0)
     own02, own22 = shift(own00, COL, -1), shift(own20, COL, -1)
     probe = probe - pstep * summed
 

time: 217 us -> 214 us (0.986)
  starting transfers between devices: 72.5 us -> 64.8 us
  waiting for transfers between devices: 68.5 us -> 75.9 us
    all_to_all x2, waiting for transfers between devices: 2.43 us -> 9.2 us  [deal(): lax.all_to_all(x.reshape(-1, 8, LANES), ('row', *COL), 0, 0, tiled=True)]
    ppermute x1, starting transfers between devices: 10.3 us -> 3.61 us  [cross_y(): lax.ppermute(block, 'row', [(i, (i + RING) % n) for i in range(edge, n, R...]
    all_to_all x2, starting transfers between devices: 20.8 us -> 17.3 us  [deal(): lax.all_to_all(x.reshape(-1, 8, LANES), ('row', *COL), 0, 0, tiled=True)]
    ppermute x19, starting transfers between devices: 30.1 us -> 32.6 us  [shift(): lax.ppermute(block, axis, [(i, (i + distance) % n) for i in range(n)])]
  transfers between devices with their start and end apart: 25 -> 25, of which waited for: 10 -> 12; matrix products, arithmetic and copies ran while one was open for 14% -> 14% of each run, Pallas kernels for 3% -> 3%
where the time goes in v4:
time: 214 us; the launch traced here: 215 us
  waiting for transfers between devices  75.9 us (35%)
  starting transfers between devices  64.8 us (30%)
  Pallas kernels  39.6 us (19%)
  other arithmetic  22.7 us (11%)
  matrix products  5.08 us (2%)
  local copies, waits for them, and re-layouts  4.66 us (2%)
    ppermute x19, waiting for transfers between devices, shift(): lax.ppermute(block, axis, [(i, (i + distance) % n) for i in range(n)])  65.8 us
    ppermute x19, starting transfers between devices, shift(): lax.ppermute(block, axis, [(i, (i + distance) % n) for i in range(n)])  32.6 us
    pallas_call x2, Pallas kernels, windows(): pl.pallas_call(windows_kernel, out_shape=[pltpu.HBM(block.shape, F32)] *...  31.7 us
    all_to_all x2, starting transfers between devices, deal(): lax.all_to_all(x.reshape(-1, 8, LANES), ('row', *COL), 0, 0, tiled=True)  17.3 us
    all_to_all x2, starting transfers between devices, collect(): lax.all_to_all(spread, ('row', *COL), 0, 0, tiled=True).reshape(shape)  11.2 us
    sub x6, other arithmetic, step(): return x - OBJECT_RATE * sum(grads[1:], grads[0])  11 us
    all_to_all x2, waiting for transfers between devices, deal(): lax.all_to_all(x.reshape(-1, 8, LANES), ('row', *COL), 0, 0, tiled=True)  9.2 us
  transfers between devices with their start and end apart: 25, of which 12 were waited for; matrix products, arithmetic and copies ran while one was open for 14% of the time, Pallas kernels for 3%

profile of v4, /device:TPU:1, one launch (start us, length us, event | category | flops | bytes accessed | tf_op | source)
XLA Modules:
  0.0 214.7 jit_solution(854687680842509089)
XLA Ops:
  2.6 7.3 %collective-permute-start.2 = (f32[2,2,256,128]{3,2,1,0:T(8,128)S(1)}, f32[2,2,256,128]{3,2,1,0:T(8,128)S(1)}, u32[]{:S(2)}, u32[]{:S(2)}) collective-permute-start(f32[2,2,256,128]{3,2,1,0:T(8,128)S(1)} %pad_maximum_fusion.refs_2_), channel_id=1, source_target_pairs={{0,112},{16,0},{32,16},{48,32},{64,48},{80,64},{96,80},{112,96},{1... | collective-permute-start | bytes 1572872 | tf_op jit(solution)/shard_map/ppermute | solution.py:243
  11.2 3.0 %collective-permute-start.1 = (f32[2,2,256,128]{3,2,1,0:T(8,128)S(1)}, f32[2,2,256,128]{3,2,1,0:T(8,128)S(1)}, u32[]{:S(2)}, u32[]{:S(2)}) collective-permute-start(f32[2,2,256,128]{3,2,1,0:T(8,128)S(1)} %pad_maximum_fusion.2.refs_5_), channel_id=1, source_target_pairs={{0,15},{1,0},{2,1},{3,2},{4,3},{5,4},{6,5},{7,6},{8,7},{9,8},{10,9... | collective-permute-start | bytes 1572872 | tf_op jit(solution)/shard_map/ppermute | solution.py:243
  14.2 1.9 fusion.2
  16.2 15.6 %collective-permute-done.2.refs_8_ = f32[2,2,256,128]{3,2,1,0:T(8,128)S(1)} collective-permute-done((f32[2,2,256,128]{3,2,1,0:T(8,128)S(1)}, f32[2,2,256,128]{3,2,1,0:T(8,128)S(1)}, u32[]{:S(2)}, u32[]{:S(2)}) %collective-permute-start.2) | collective-permute-done | bytes 524320 | tf_op jit(solution)/shard_map/ppermute | solution.py:243
  31.7 2.7 %collective-permute-start.4 = (f32[2,2,256,128]{3,2,1,0:T(8,128)S(1)}, f32[2,2,256,128]{3,2,1,0:T(8,128)S(1)}, u32[]{:S(2)}, u32[]{:S(2)}) collective-permute-start(f32[2,2,256,128]{3,2,1,0:T(8,128)S(1)} %collective-permute-done.2.refs_8_), channel_id=1, source_target_pairs={{0,15},{1,0},{2,1},{3,2},{4,3},{5,4},{6,5},{7,6},{8,7},{9,8},{10,9... | collective-permute-start | bytes 1572872 | tf_op jit(solution)/shard_map/ppermute | solution.py:243
  36.5 3.2 %fusion.refs_12_ = f32[8,256,256]{2,1,0:T(8,128)} fusion(f32[256,256,1]{1,0,2:T(8,128)S(1)} %copy-done.24, f32[256,8,256]{2,0,1:T(8,128)S(1)} %fusion.2), kind=kOutput, calls=%fused_computation | convolution fusion | flops 1610612736 | bytes 4456448 | tf_op jit(solution)/shard_map/sjk,lk->sjl/dot_general | solution.py:382
  39.6 9.0 %collective-permute-done.3.refs_9_ = f32[2,2,256,128]{3,2,1,0:T(8,128)S(1)} collective-permute-done((f32[2,2,256,128]{3,2,1,0:T(8,128)S(1)}, f32[2,2,256,128]{3,2,1,0:T(8,128)S(1)}, u32[]{:S(2)}, u32[]{:S(2)}) %collective-permute-start.3) | collective-permute-done | bytes 524320 | tf_op jit(solution)/shard_map/ppermute | solution.py:243
  48.6 2.0 collective-permute-done.4.refs_10_
  51.4 15.7 %windows.2 = (f32[2,2,256,128]{3,2,1,0:T(8,128)}, f32[2,2,256,128]{3,2,1,0:T(8,128)}, f32[2,2,256,128]{3,2,1,0:T(8,128)}, f32[2,2,256,128]{3,2,1,0:T(8,128)}, f3...) custom-call(s32[2,8]{1,0:T(2,128)S(1)} %bitcast.39, ...), custom_call_target="tpu_custom_call" | custom-call | tf_op jit(solution)/shard_map/windows/pallas_call | solution.py:228
  67.3 2.8 %collective-permute-start.9 = (f32[2,2,256,128]{3,2,1,0:T(8,128)}, f32[2,2,256,128]{3,2,1,0:T(8,128)}, u32[]{:S(2)}, u32[]{:S(2)}) collective-permute-start(f32[2,2,256,128]{3,2,1,0:T(8,128)} %get-tuple-element.41), channel_id=1, source_target_pairs={{0,1},{1,2},{2,3},{3,4},{4,5},{5,6},{6,7},{7,8},{8,9},{9,10},{10,1... | collective-permute-start | bytes 1572872 | tf_op jit(solution)/shard_map/ppermute | solution.py:243
  70.1 8.3 %all-to-all-start = ((f32[128,8,128]{2,1,0:T(8,128)}), f32[128,8,128]{2,1,0:T(8,128)}, u32[]{:S(2)}, u32[]{:S(2)}) async-start(f32[128,8,128]{2,1,0:T(8,128)} %bitcast.42), calls=%async_computation | async-start | bytes 1048576 | tf_op jit(solution)/shard_map/all_to_all | solution.py:350
  80.0 4.4 %collective-permute-start.12 = (f32[2,2,256,128]{3,2,1,0:T(8,128)}, f32[2,2,256,128]{3,2,1,0:T(8,128)}, u32[]{:S(2)}, u32[]{:S(2)}) collective-permute-start(f32[2,2,256,128]{3,2,1,0:T(8,128)} %get-tuple-element.42), channel_id=1, source_target_pairs={{0,112},{16,0},{32,16},{48,32},{64,48},{80,64},{96,80},{112,96},{1... | collective-permute-start | bytes 1572872 | tf_op jit(solution)/shard_map/ppermute | solution.py:243
  84.4 2.1 multiply_subtract_fusion.3.refs_6_.refs_3_
  86.5 2.0 add.29
  90.4 5.1 %collective-permute-start.8 = (f32[2,2,256,128]{3,2,1,0:T(8,128)}, f32[2,2,256,128]{3,2,1,0:T(8,128)}, u32[]{:S(2)}, u32[]{:S(2)}) collective-permute-start(f32[2,2,256,128]{3,2,1,0:T(8,128)} %add.28), channel_id=1, source_target_pairs={{0,112},{16,0},{32,16},{48,32},{64,48},{80,64},{96,80},{112,96},{1... | collective-permute-start | bytes 1572872 | tf_op jit(solution)/shard_map/ppermute | solution.py:243
  95.5 5.0 %all-to-all-done = f32[128,8,128]{2,1,0:T(8,128)} async-done(((f32[128,8,128]{2,1,0:T(8,128)}), f32[128,8,128]{2,1,0:T(8,128)}, u32[]{:S(2)}, u32[]{:S(2)}) %all-to-all-start) | async-done | bytes 524320 | tf_op jit(solution)/shard_map/all_to_all | solution.py:350
  102.6 5.1 %all-to-all-start.1 = ((f32[128,8,128]{2,1,0:T(8,128)}), f32[128,8,128]{2,1,0:T(8,128)}, u32[]{:S(2)}, u32[]{:S(2)}) async-start(f32[128,8,128]{2,1,0:T(8,128)} %broadcast_in_dim.4), calls=%async_computation.1 | async-start | bytes 1048576 | tf_op jit(solution)/shard_map/all_to_all | solution.py:355
  113.7 2.0 multiply_subtract_fusion.2.refs_9_
  115.7 13.6 %collective-permute-done.10.refs_7_ = f32[2,2,256,128]{3,2,1,0:T(8,128)S(1)} collective-permute-done((f32[2,2,256,128]{3,2,1,0:T(8,128)S(1)}, f32[2,2,256,128]{3,2,1,0:T(8,128)S(1)}, u32[]{:S(2)}, u32[]{:S(2)}) %collective-permute-start.10) | collective-permute-done | bytes 524320 | tf_op jit(solution)/shard_map/ppermute | solution.py:243
  129.3 2.3 %multiply_subtract_fusion.refs_8_ = f32[2,2,256,128]{3,2,1,0:T(8,128)} fusion(f32[2,2,256,128]{3,2,1,0:T(8,128)S(1)} %copy-done.21, f32[2,2,256,128]{3,2,1,0:T(8,128)} %add.29, f32[2,2,256,128]{3,2,1,0:T(8,128)} %collective-permute-done.8), kind=kLoop, calls=%fused_computation.9 | loop fusion | flops 393216 | bytes 2097152 | tf_op jit(solution)/shard_map/sub | solution.py:385
  134.1 1.9 fusion.4.refs_11_.probe
  136.1 4.4 %collective-permute-done.14.refs_10_ = f32[2,2,256,128]{3,2,1,0:T(8,128)} collective-permute-done((f32[2,2,256,128]{3,2,1,0:T(8,128)}, f32[2,2,256,128]{3,2,1,0:T(8,128)}, u32[]{:S(2)}, u32[]{:S(2)}) %collective-permute-start.14) | collective-permute-done | bytes 524320 | tf_op jit(solution)/shard_map/ppermute | solution.py:243
  140.5 5.6 %collective-permute-done.13.refs_4_ = f32[2,2,256,128]{3,2,1,0:T(8,128)} collective-permute-done((f32[2,2,256,128]{3,2,1,0:T(8,128)S(1)}, f32[2,2,256,128]{3,2,1,0:T(8,128)}, u32[]{:S(2)}, u32[]{:S(2)}) %collective-permute-start.13) | collective-permute-done | bytes 524320 | tf_op jit(solution)/shard_map/ppermute | solution.py:243
  146.1 15.9 %windows.3 = (f32[2,2,256,128]{3,2,1,0:T(8,128)}, f32[2,2,256,128]{3,2,1,0:T(8,128)}, f32[2,2,256,128]{3,2,1,0:T(8,128)}, f32[2,2,256,128]{3,2,1,0:T(8,128)}, f3...) custom-call(s32[2,8]{1,0:T(2,128)S(1)} %bitcast.40, ...), custom_call_target="tpu_custom_call" | custom-call | tf_op jit(solution)/shard_map/windows/pallas_call | solution.py:228
  162.2 9.0 %all-to-all-start.2 = ((f32[128,8,128]{2,1,0:T(8,128)}), f32[128,8,128]{2,1,0:T(8,128)S(1)}, u32[]{:S(2)}, u32[]{:S(2)}) async-start(f32[128,8,128]{2,1,0:T(8,128)} %bitcast.43), calls=%async_computation.2 | async-start | bytes 1048576 | tf_op jit(solution)/shard_map/all_to_all | solution.py:350
  173.0 2.1 add.35
  177.3 3.6 %collective-permute-start.18 = (f32[2,2,256,128]{3,2,1,0:T(8,128)}, f32[2,2,256,128]{3,2,1,0:T(8,128)}, u32[]{:S(2)}, u32[]{:S(2)}) collective-permute-start(f32[2,2,256,128]{3,2,1,0:T(8,128)} %collective-permute-done.17.near), channel_id=1, source_target_pairs={{0,64},{64,0},{1,65},{65,1},{2,66},{66,2},{3,67},{67,3},{4,68},{68... | collective-permute-start | bytes 1572872 | tf_op jit(solution)/shard_map/ppermute | solution.py:257
  180.9 4.2 %all-to-all-done.2 = f32[128,8,128]{2,1,0:T(8,128)S(1)} async-done(((f32[128,8,128]{2,1,0:T(8,128)}), f32[128,8,128]{2,1,0:T(8,128)S(1)}, u32[]{:S(2)}, u32[]{:S(2)}) %all-to-all-start.2) | async-done | bytes 524320 | tf_op jit(solution)/shard_map/all_to_all | solution.py:350
  186.1 6.1 %all-to-all-start.3 = ((f32[128,8,128]{2,1,0:T(8,128)}), f32[128,8,128]{2,1,0:T(8,128)S(1)}, u32[]{:S(2)}, u32[]{:S(2)}) async-start(f32[128,8,128]{2,1,0:T(8,128)} %broadcast_in_dim.5), calls=%async_computation.3 | async-start | bytes 1048576 | tf_op jit(solution)/shard_map/all_to_all | solution.py:355
  194.0 4.2 %most.1.whole_in = f32[2,512,512]{2,1,0:T(8,128)} custom-call(f32[2,2,256,128]{3,2,1,0:T(8,128)} %copy-done.8, f32[2,2,256,128]{3,2,1,0:T(8,128)} %multiply_subtract_fusion.4.refs_3_.refs_1_, f32[2,2,256,128]{3,2,1,0:T(8,128)} %copy-done.7, f32[2,2,256,128]{3,2,1,0:T(8,128)} %multiply_subtract_fusion.3.refs_6_.refs_3_, ...), custom_call_target="tpu_custom_call" | custom-call | tf_op jit(solution)/shard_map/most/pallas_call | solution.py:307
  198.2 12.6 %collective-permute-done.16.above0 = f32[2,2,256,128]{3,2,1,0:T(8,128)} collective-permute-done((f32[2,2,256,128]{3,2,1,0:T(8,128)}, f32[2,2,256,128]{3,2,1,0:T(8,128)}, u32[]{:S(2)}, u32[]{:S(2)}) %collective-permute-start.16) | collective-permute-done | bytes 524320 | tf_op jit(solution)/shard_map/ppermute | solution.py:243
  210.9 2.9 %rest.1 = f32[2,512,512]{2,1,0:T(8,128)} custom-call(s32[1]{0:T(128)} %bitcast.19.wrapped, f32[2,2,256,128]{3,2,1,0:T(8,128)} %collective-permute-done.16.above0, f32[2,2,256,128]{3,2,1,0:T(8,128)} %collective-permute-done.17.near, f32[2,2,256,128]{3,2,1,0:T(8,128)} %collective-permute-done.18.far, ...), custom_call_target="tpu_custom_call", output_to_operand_aliasing={{}: (4, {})} | custom-call | tf_op jit(solution)/shard_map/rest/pallas_call | solution.py:320
  (114 shorter events, 27.4 us)
Async XLA Ops:
  2.5 32.6 %copy-start.13 = (f32[1,2,256,128]{3,2,1,0:T(8,128)}, f32[1,2,256,128]{3,2,1,0:T(8,128)S(1)}, u32[]{:S(2)}) copy-start(f32[1,2,256,128]{3,2,1,0:T(8,128)S(1)} %get-tuple-element.66) | copy-start | bytes 786436
  2.5 32.6 %copy-start.14 = (f32[1,2,256,128]{3,2,1,0:T(8,128)}, f32[1,2,256,128]{3,2,1,0:T(8,128)S(1)}, u32[]{:S(2)}) copy-start(f32[1,2,256,128]{3,2,1,0:T(8,128)S(1)} %get-tuple-element.73) | copy-start | bytes 786436
  2.6 29.1 %collective-permute-start.2 = (f32[2,2,256,128]{3,2,1,0:T(8,128)S(1)}, f32[2,2,256,128]{3,2,1,0:T(8,128)S(1)}, u32[]{:S(2)}, u32[]{:S(2)}) collective-permute-start(f32[2,2,256,128]{3,2,1,0:T(8,128)S(1)} %pad_maximum_fusion.refs_2_), channel_id=1, source_target_pairs={{0,112},{16,0},{32,16},{48,32},{64,48},{80,64},{96,80},{112,96},{1... | collective-permute-start | bytes 1572872 | tf_op jit(solution)/shard_map/ppermute | solution.py:243
  9.9 38.7 %collective-permute-start = (f32[2,2,256,128]{3,2,1,0:T(8,128)S(1)}, f32[2,2,256,128]{3,2,1,0:T(8,128)S(1)}, u32[]{:S(2)}, u32[]{:S(2)}) collective-permute-start(f32[2,2,256,128]{3,2,1,0:T(8,128)S(1)} %pad_maximum_fusion.refs_2_), channel_id=1, source_target_pairs={{0,15},{1,0},{2,1},{3,2},{4,3},{5,4},{6,5},{7,6},{8,7},{9,8},{10,9... | collective-permute-start | bytes 1572872 | tf_op jit(solution)/shard_map/ppermute | solution.py:243
  10.9 37.7 %collective-permute-start.3 = (f32[2,2,256,128]{3,2,1,0:T(8,128)S(1)}, f32[2,2,256,128]{3,2,1,0:T(8,128)S(1)}, u32[]{:S(2)}, u32[]{:S(2)}) collective-permute-start(f32[2,2,256,128]{3,2,1,0:T(8,128)S(1)} %pad_maximum_fusion.1.refs_3_), channel_id=1, source_target_pairs={{0,112},{16,0},{32,16},{48,32},{64,48},{80,64},{96,80},{112,96},{1... | collective-permute-start | bytes 1572872 | tf_op jit(solution)/shard_map/ppermute | solution.py:243
  11.2 23.3 %copy-start.31 = (f32[2,256,256]{2,1,0:T(8,128)S(1)}, f32[2,256,256]{2,1,0:T(8,128)}, u32[]{:S(2)}) copy-start(f32[2,256,256]{2,1,0:T(8,128)} %param.12) | copy-start | bytes 1572868
  11.2 37.4 %collective-permute-start.1 = (f32[2,2,256,128]{3,2,1,0:T(8,128)S(1)}, f32[2,2,256,128]{3,2,1,0:T(8,128)S(1)}, u32[]{:S(2)}, u32[]{:S(2)}) collective-permute-start(f32[2,2,256,128]{3,2,1,0:T(8,128)S(1)} %pad_maximum_fusion.2.refs_5_), channel_id=1, source_target_pairs={{0,15},{1,0},{2,1},{3,2},{4,3},{5,4},{6,5},{7,6},{8,7},{9,8},{10,9... | collective-permute-start | bytes 1572872 | tf_op jit(solution)/shard_map/ppermute | solution.py:243
  31.7 18.8 %collective-permute-start.4 = (f32[2,2,256,128]{3,2,1,0:T(8,128)S(1)}, f32[2,2,256,128]{3,2,1,0:T(8,128)S(1)}, u32[]{:S(2)}, u32[]{:S(2)}) collective-permute-start(f32[2,2,256,128]{3,2,1,0:T(8,128)S(1)} %collective-permute-done.2.refs_8_), channel_id=1, source_target_pairs={{0,15},{1,0},{2,1},{3,2},{4,3},{5,4},{6,5},{7,6},{8,7},{9,8},{10,9... | collective-permute-start | bytes 1572872 | tf_op jit(solution)/shard_map/ppermute | solution.py:243
  36.5 15.0 %copy-start.5 = (bf16[256,256]{1,0:T(8,128)(2,1)S(1)}, bf16[256,256]{1,0:T(8,128)(2,1)}, u32[]{:S(2)}) copy-start(bf16[256,256]{1,0:T(8,128)(2,1)} %constant.39.clone.refs_16_) | copy-start | bytes 393220
  36.5 15.0 %copy-start.6 = (s32[1,1,2,8]{3,2,1,0:T(2,128)S(1)}, s32[1,1,2,8]{3,2,1,0:T(2,128)}, u32[]{:S(2)}) copy-start(s32[1,1,2,8]{3,2,1,0:T(2,128)} %param.13) | copy-start | bytes 196
  67.2 19.3 %collective-permute-start.6 = (f32[2,2,256,128]{3,2,1,0:T(8,128)}, f32[2,2,256,128]{3,2,1,0:T(8,128)}, u32[]{:S(2)}, u32[]{:S(2)}) collective-permute-start(f32[2,2,256,128]{3,2,1,0:T(8,128)} %get-tuple-element.37), channel_id=1, source_target_pairs={{0,1},{1,2},{2,3},{3,4},{4,5},{5,6},{6,7},{7,8},{8,9},{9,10},{10,1... | collective-permute-start | bytes 1572872 | tf_op jit(solution)/shard_map/ppermute | solution.py:243
  67.2 21.3 %collective-permute-start.5 = (f32[2,2,256,128]{3,2,1,0:T(8,128)}, f32[2,2,256,128]{3,2,1,0:T(8,128)}, u32[]{:S(2)}, u32[]{:S(2)}) collective-permute-start(f32[2,2,256,128]{3,2,1,0:T(8,128)} %get-tuple-element.35), channel_id=1, source_target_pairs={{0,1},{1,2},{2,3},{3,4},{4,5},{5,6},{6,7},{7,8},{8,9},{9,10},{10,1... | collective-permute-start | bytes 1572872 | tf_op jit(solution)/shard_map/ppermute | solution.py:243
  67.3 40.4 %collective-permute-start.9 = (f32[2,2,256,128]{3,2,1,0:T(8,128)}, f32[2,2,256,128]{3,2,1,0:T(8,128)}, u32[]{:S(2)}, u32[]{:S(2)}) collective-permute-start(f32[2,2,256,128]{3,2,1,0:T(8,128)} %get-tuple-element.41), channel_id=1, source_target_pairs={{0,1},{1,2},{2,3},{3,4},{4,5},{5,6},{6,7},{7,8},{8,9},{9,10},{10,1... | collective-permute-start | bytes 1572872 | tf_op jit(solution)/shard_map/ppermute | solution.py:243
  70.1 30.4 %all-to-all-start = ((f32[128,8,128]{2,1,0:T(8,128)}), f32[128,8,128]{2,1,0:T(8,128)}, u32[]{:S(2)}, u32[]{:S(2)}) async-start(f32[128,8,128]{2,1,0:T(8,128)} %bitcast.42), calls=%async_computation | async-start | bytes 1048576 | tf_op jit(solution)/shard_map/all_to_all | solution.py:350
  78.5 33.3 %collective-permute-start.11 = (f32[2,2,256,128]{3,2,1,0:T(8,128)}, f32[2,2,256,128]{3,2,1,0:T(8,128)}, u32[]{:S(2)}, u32[]{:S(2)}) collective-permute-start(f32[2,2,256,128]{3,2,1,0:T(8,128)} %get-tuple-element.43), channel_id=1, source_target_pairs={{0,16},{16,32},{32,48},{48,64},{64,80},{80,96},{96,112},{112,0},{1... | collective-permute-start | bytes 1572872 | tf_op jit(solution)/shard_map/ppermute | solution.py:243
  80.0 33.7 %collective-permute-start.12 = (f32[2,2,256,128]{3,2,1,0:T(8,128)}, f32[2,2,256,128]{3,2,1,0:T(8,128)}, u32[]{:S(2)}, u32[]{:S(2)}) collective-permute-start(f32[2,2,256,128]{3,2,1,0:T(8,128)} %get-tuple-element.42), channel_id=1, source_target_pairs={{0,112},{16,0},{32,16},{48,32},{64,48},{80,64},{96,80},{112,96},{1... | collective-permute-start | bytes 1572872 | tf_op jit(solution)/shard_map/ppermute | solution.py:243
  90.4 38.9 %collective-permute-start.7 = (f32[2,2,256,128]{3,2,1,0:T(8,128)}, f32[2,2,256,128]{3,2,1,0:T(8,128)}, u32[]{:S(2)}, u32[]{:S(2)}) collective-permute-start(f32[2,2,256,128]{3,2,1,0:T(8,128)} %add.29), channel_id=1, source_target_pairs={{0,16},{16,32},{32,48},{48,64},{64,80},{80,96},{96,112},{112,0},{1... | collective-permute-start | bytes 1572872 | tf_op jit(solution)/shard_map/ppermute | solution.py:243
  90.4 38.9 %collective-permute-start.8 = (f32[2,2,256,128]{3,2,1,0:T(8,128)}, f32[2,2,256,128]{3,2,1,0:T(8,128)}, u32[]{:S(2)}, u32[]{:S(2)}) collective-permute-start(f32[2,2,256,128]{3,2,1,0:T(8,128)} %add.28), channel_id=1, source_target_pairs={{0,112},{16,0},{32,16},{48,32},{64,48},{80,64},{96,80},{112,96},{1... | collective-permute-start | bytes 1572872 | tf_op jit(solution)/shard_map/ppermute | solution.py:243
  102.6 30.4 %all-to-all-start.1 = ((f32[128,8,128]{2,1,0:T(8,128)}), f32[128,8,128]{2,1,0:T(8,128)}, u32[]{:S(2)}, u32[]{:S(2)}) async-start(f32[128,8,128]{2,1,0:T(8,128)} %broadcast_in_dim.4), calls=%async_computation.1 | async-start | bytes 1048576 | tf_op jit(solution)/shard_map/all_to_all | solution.py:355
  109.3 20.0 %copy-start.21 = (f32[2,2,256,128]{3,2,1,0:T(8,128)S(1)}, f32[2,2,256,128]{3,2,1,0:T(8,128)}, u32[]{:S(2)}) copy-start(f32[2,2,256,128]{3,2,1,0:T(8,128)} %copy-done.20) | copy-start | bytes 1572868
  109.3 20.0 %collective-permute-start.10 = (f32[2,2,256,128]{3,2,1,0:T(8,128)S(1)}, f32[2,2,256,128]{3,2,1,0:T(8,128)S(1)}, u32[]{:S(2)}, u32[]{:S(2)}) collective-permute-start(f32[2,2,256,128]{3,2,1,0:T(8,128)S(1)} %multiply_subtract_fusion.5.refs_5_.refs_2_), channel_id=1, source_target_pairs={{0,15},{1,0},{2,1},{3,2},{4,3},{5,4},{6,5},{7,6},{8,7},{9,8},{10,9... | collective-permute-start | bytes 1572872 | tf_op jit(solution)/shard_map/ppermute | solution.py:243
  113.7 17.9 %copy-start.10 = (f32[1,2,256,128]{3,2,1,0:T(8,128)S(1)}, f32[1,2,256,128]{3,2,1,0:T(8,128)}, u32[]{:S(2)}) copy-start(f32[1,2,256,128]{3,2,1,0:T(8,128)} %copy-done.9) | copy-start | bytes 786436
  131.6 8.9 %collective-permute-start.14 = (f32[2,2,256,128]{3,2,1,0:T(8,128)}, f32[2,2,256,128]{3,2,1,0:T(8,128)}, u32[]{:S(2)}, u32[]{:S(2)}) collective-permute-start(f32[2,2,256,128]{3,2,1,0:T(8,128)} %multiply_subtract_fusion.refs_8_), channel_id=1, source_target_pairs={{0,15},{1,0},{2,1},{3,2},{4,3},{5,4},{6,5},{7,6},{8,7},{9,8},{10,9... | collective-permute-start | bytes 1572872 | tf_op jit(solution)/shard_map/ppermute | solution.py:243
  132.9 13.2 %collective-permute-start.13 = (f32[2,2,256,128]{3,2,1,0:T(8,128)S(1)}, f32[2,2,256,128]{3,2,1,0:T(8,128)}, u32[]{:S(2)}, u32[]{:S(2)}) collective-permute-start(f32[2,2,256,128]{3,2,1,0:T(8,128)S(1)} %multiply_subtract_fusion.1.refs_2_.refs_0_), channel_id=1, source_target_pairs={{0,15},{1,0},{2,1},{3,2},{4,3},{5,4},{6,5},{7,6},{8,7},{9,8},{10,9... | collective-permute-start | bytes 1572872 | tf_op jit(solution)/shard_map/ppermute | solution.py:243
  162.1 11.0 %collective-permute-start.15 = (f32[2,2,256,128]{3,2,1,0:T(8,128)}, f32[2,2,256,128]{3,2,1,0:T(8,128)}, u32[]{:S(2)}, u32[]{:S(2)}) collective-permute-start(f32[2,2,256,128]{3,2,1,0:T(8,128)} %get-tuple-element.55), channel_id=1, source_target_pairs={{0,1},{1,2},{2,3},{3,4},{4,5},{5,6},{6,7},{7,8},{8,9},{9,10},{10,1... | collective-permute-start | bytes 1572872 | tf_op jit(solution)/shard_map/ppermute | solution.py:243
  162.1 15.2 %collective-permute-start.17 = (f32[2,2,256,128]{3,2,1,0:T(8,128)}, f32[2,2,256,128]{3,2,1,0:T(8,128)}, u32[]{:S(2)}, u32[]{:S(2)}) collective-permute-start(f32[2,2,256,128]{3,2,1,0:T(8,128)} %get-tuple-element.57), channel_id=1, source_target_pairs={{0,16},{16,32},{32,48},{48,0},{64,80},{80,96},{96,112},{112,64},{1... | collective-permute-start | bytes 1572872 | tf_op jit(solution)/shard_map/ppermute | solution.py:251
  162.2 22.9 %all-to-all-start.2 = ((f32[128,8,128]{2,1,0:T(8,128)}), f32[128,8,128]{2,1,0:T(8,128)S(1)}, u32[]{:S(2)}, u32[]{:S(2)}) async-start(f32[128,8,128]{2,1,0:T(8,128)} %bitcast.43), calls=%async_computation.2 | async-start | bytes 1048576 | tf_op jit(solution)/shard_map/all_to_all | solution.py:350
  171.2 21.0 %collective-permute-start.19 = (f32[2,2,256,128]{3,2,1,0:T(8,128)}, f32[2,2,256,128]{3,2,1,0:T(8,128)S(1)}, u32[]{:S(2)}, u32[]{:S(2)}) collective-permute-start(f32[2,2,256,128]{3,2,1,0:T(8,128)} %get-tuple-element.62), channel_id=1, source_target_pairs={{0,1},{1,2},{2,3},{3,4},{4,5},{5,6},{6,7},{7,8},{8,9},{9,10},{10,1... | collective-permute-start | bytes 1572872 | tf_op jit(solution)/shard_map/ppermute | solution.py:243
  172.9 21.1 %collective-permute-start.20 = (f32[2,2,256,128]{3,2,1,0:T(8,128)}, f32[2,2,256,128]{3,2,1,0:T(8,128)}, u32[]{:S(2)}, u32[]{:S(2)}) collective-permute-start(f32[2,2,256,128]{3,2,1,0:T(8,128)} %get-tuple-element.63), channel_id=1, source_target_pairs={{0,1},{1,2},{2,3},{3,4},{4,5},{5,6},{6,7},{7,8},{8,9},{9,10},{10,1... | collective-permute-start | bytes 1572872 | tf_op jit(solution)/shard_map/ppermute | solution.py:243
  175.1 35.8 %collective-permute-start.16 = (f32[2,2,256,128]{3,2,1,0:T(8,128)}, f32[2,2,256,128]{3,2,1,0:T(8,128)}, u32[]{:S(2)}, u32[]{:S(2)}) collective-permute-start(f32[2,2,256,128]{3,2,1,0:T(8,128)} %add.35), channel_id=1, source_target_pairs={{0,16},{16,32},{32,48},{48,64},{64,80},{80,96},{96,112},{112,0},{1... | collective-permute-start | bytes 1572872 | tf_op jit(solution)/shard_map/ppermute | solution.py:243
  177.3 33.6 %collective-permute-start.18 = (f32[2,2,256,128]{3,2,1,0:T(8,128)}, f32[2,2,256,128]{3,2,1,0:T(8,128)}, u32[]{:S(2)}, u32[]{:S(2)}) collective-permute-start(f32[2,2,256,128]{3,2,1,0:T(8,128)} %collective-permute-done.17.near), channel_id=1, source_target_pairs={{0,64},{64,0},{1,65},{65,1},{2,66},{66,2},{3,67},{67,3},{4,68},{68... | collective-permute-start | bytes 1572872 | tf_op jit(solution)/shard_map/ppermute | solution.py:257
  186.1 27.7 %all-to-all-start.3 = ((f32[128,8,128]{2,1,0:T(8,128)}), f32[128,8,128]{2,1,0:T(8,128)S(1)}, u32[]{:S(2)}, u32[]{:S(2)}) async-start(f32[128,8,128]{2,1,0:T(8,128)} %broadcast_in_dim.5), calls=%async_computation.3 | async-start | bytes 1048576 | tf_op jit(solution)/shard_map/all_to_all | solution.py:355
  (27 other events, 194.9 us)
